TPU v7x, 32 devices: a whole 2x2x4 slice. The times are simulated.
32 devices in a mesh: dp: 16 (over z, y, x), expert: 2 (over core).
Axes of the slice: x: 2, y: 2, z: 4, core: 2. Of those that a mesh axis runs over, the one named last changes fastest.
Arguments:
- tokens: bfloat16 [2048, 2048], P('dp'), may hold values from -6 to 6
- arms: int32 [2048], P('dp'), may hold values from 0 to 3
- arm_bias: bfloat16 [4, 2048], replicated, may hold values from -3 to 3
- routes: int32 [2048, 6], P('dp'), may hold values from 0 to 63, all different within a row; in each aligned block of 128 rows (0 to 127, 128 to 255, ...) at most 16 rows name the same one
- gates: int32 [2048, 6], P('dp'), may hold values from 1 to 64
- up_weight: bfloat16 [64, 1408, 2048], P('dp', 'expert'), may hold values from -0.125 to 0.125
- down_weight: bfloat16 [64, 1408, 2048], P('dp', 'expert'), may hold values from -0.15625 to 0.15625
- cotangent: bfloat16 [2048, 2048], P('dp'), may hold values from -1.5 to 1.5
Outputs:
- grad_tokens: float32 [2048, 2048], P('dp', 'expert')
- grad_up: bfloat16 [64, 1408, 2048], P('dp', 'expert')
- grad_down: bfloat16 [64, 1408, 2048], P('dp', 'expert')
Inputs may be any that keep to these rules, and one draw needn't show every extreme that they name: The 6 ids of a token differ. Among the routes of the 128 tokens of one index of dp, at most 16 name one expert, and in some such block some expert is named exactly 16 times.
All inputs are finite; a program needn't handle non-finite values.
Results may differ from a plain program's by a relative error of at most 0.014.
Values may be sent and summed in bfloat16 or wider, within the bound.
No kernel may reach another device: no remote copies, remote signals or barrier semaphores. Data moves between devices by JAX's collectives and lax.ppermute only.
A program may use at most 128 MiB of HBM per device.

v0:
```python
import jax
import jax.numpy as jnp
from jax import lax
from jax.sharding import PartitionSpec as P

EXPERTS = 64
TOPK = 6
CAP = 16


def local_slots(flat_routes):
    expert_ids = jnp.arange(EXPERTS, dtype=jnp.int32)
    one_hot = (flat_routes[:, None] == expert_ids[None, :]).astype(jnp.int32)
    rank_table = jnp.cumsum(one_hot, axis=0) - one_hot
    return jnp.sum(rank_table * one_hot, axis=1)


def local(tokens, arms, arm_bias, routes, gates, up_weight, down_weight, cotangent):
    token_count = tokens.shape[0]
    feature_width = tokens.shape[1]
    expert_local = up_weight.shape[0]
    dp_count = lax.axis_size("dp")
    arm_ids = jnp.arange(arm_bias.shape[0], dtype=jnp.int32)
    arm_pick = (arms[:, None] == arm_ids[None, :]).astype(jnp.bfloat16)
    lifted = (
        tokens.astype(jnp.float32) + jnp.dot(arm_pick, arm_bias, preferred_element_type=jnp.float32)
    ).astype(jnp.bfloat16)
    flat_routes = routes.reshape(-1)
    slot_ids = local_slots(flat_routes)
    target_pos = flat_routes * CAP + slot_ids
    route_weight = gates.reshape(-1).astype(jnp.float32) / 64.0
    route_rows = jnp.repeat(lifted, TOPK, axis=0)
    scaled = (
        jnp.repeat(cotangent, TOPK, axis=0).astype(jnp.float32) * route_weight[:, None]
    ).astype(jnp.bfloat16)

    def place_slots(values):
        blank_buffer = jnp.zeros((EXPERTS * CAP, values.shape[1]), jnp.bfloat16)
        filled = blank_buffer.at[target_pos].set(values)
        return filled.reshape(dp_count, expert_local, CAP, values.shape[1])

    part_width = feature_width // lax.axis_size("expert")
    column_index = lax.axis_index("expert")

    def column_cut(values):
        return lax.dynamic_slice_in_dim(values, column_index * part_width, part_width, 1)

    full_rows = lax.all_gather(
        lax.all_to_all(
            place_slots(column_cut(route_rows)), "dp", split_axis=0, concat_axis=0, tiled=True
        ),
        "expert",
        axis=3,
        tiled=True,
    )
    preact = jnp.einsum("sekd,ehd->sekh", full_rows, up_weight, preferred_element_type=jnp.float32)
    backward_full_rows = lax.all_gather(
        lax.all_to_all(
            place_slots(column_cut(scaled)), "dp", split_axis=0, concat_axis=0, tiled=True
        ),
        "expert",
        axis=3,
        tiled=True,
    )
    backprop = jnp.einsum(
        "sekd,ehd->sekh", backward_full_rows, down_weight, preferred_element_type=jnp.float32
    )
    hidden = jax.nn.silu(preact).astype(jnp.bfloat16)
    sigmoid_pre = jax.nn.sigmoid(preact)
    grad_pre = (backprop * sigmoid_pre * (1.0 + preact * (1.0 - sigmoid_pre))).astype(jnp.bfloat16)
    partial_value = jnp.einsum(
        "sekh,ehd->sekd", grad_pre, up_weight, preferred_element_type=jnp.float32
    ).astype(jnp.bfloat16)
    grad_down = jnp.einsum(
        "sekh,sekd->ehd", hidden, backward_full_rows, preferred_element_type=jnp.float32
    ).astype(jnp.bfloat16)
    grad_up = jnp.einsum(
        "sekh,sekd->ehd", grad_pre, full_rows, preferred_element_type=jnp.float32
    ).astype(jnp.bfloat16)
    returned = lax.all_to_all(partial_value, "dp", split_axis=0, concat_axis=0, tiled=True)
    flat_back = returned.reshape(EXPERTS * CAP, feature_width)
    picked = flat_back[target_pos].astype(jnp.float32).reshape(token_count, TOPK, feature_width)
    summed = jnp.sum(picked, axis=1)
    grad_tokens = lax.psum_scatter(
        summed.astype(jnp.bfloat16), "expert", scatter_dimension=1, tiled=True
    ).astype(jnp.float32)
    return (grad_tokens, grad_up, grad_down)


def solution(mesh):
    in_specs = (
        P("dp", None),
        P("dp"),
        P(),
        P("dp", None),
        P("dp", None),
        P("dp", "expert", None),
        P("dp", "expert", None),
        P("dp", None),
    )
    out_specs = (P("dp", "expert"), P("dp", "expert", None), P("dp", "expert", None))
    return jax.shard_map(local, mesh=mesh, in_specs=in_specs, out_specs=out_specs, check_vma=False)
```

profile of v0, /device:TPU:0, one launch (start us, length us, event | category | flops | bytes accessed | tf_op | source)
XLA Modules:
  0.0 333.7 jit_solution(10117765915381565007)
XLA Ops:
  7.2 0.0 copy-start
  7.2 0.0 all-gather.5.cloned.1.call-start
  7.2 0.7 broadcast_multiply_fusion
  7.9 0.8 copy.28
  8.7 0.1 eq.42
  8.9 0.1 eq.38
  9.0 0.1 copy.27
  9.1 0.1 mul.46
  9.3 1.8 reduce-window.6
  11.1 0.3 slice_reduce_fusion
  11.4 0.0 copy-done
  11.4 1.4 fusion.16
  12.8 2.7 broadcast_in_dim.5
  15.5 6.3 %reshape.81 = bf16[768,2048]{1,0:T(8,128)(2,1)} reshape(bf16[128,6,2048]{2,1,0:T(8,128)(2,1)} %broadcast_in_dim.5) | data formatting | bytes 6291456 | tf_op jit(solution)/shard_map/reshape | solution.py:32
  21.8 0.1 fusion.30
  22.0 7.1 %scatter_custom_fusion.1 = bf16[1024,1024]{1,0:T(8,128)(2,1)S(1)} fusion(s32[768]{0:T(1024)S(1)} %fusion.33, bf16[768,2048]{1,0:T(8,128)(2,1)} %reshape.81, s32[]{:T(128)} %constant.10.clone.1, s32[]{:T(128)S(6)} %select_n.17, bf16[]{:T(256)} %constant.8.clone.1), kind=kCustom, calls=%fused_computation.29 | custom fusion | bytes 3671044 | tf_op jit(solution)/shard_map/scatter | solution.py:39
  29.1 57.0 %all_to_all.15 = bf16[16,4,16,1024]{3,2,1,0:T(8,128)(2,1)S(1)} all-to-all(bf16[16,4,16,1024]{3,2,1,0:T(8,128)(2,1)S(1)} %bitcast.83), channel_id=1, replica_groups=mesh['dp'=16,'expert'=2] {'dp'}, dimensions={0} | all-to-all | bytes 4194304 | tf_op jit(solution)/shard_map/all_to_all | solution.py:49
  86.1 1.6 copy.33
  87.6 0.0 all-gather.5.cloned.1.call-update
  87.6 0.0 all-gather.3.cloned.1.call-start
  87.7 0.0 copy-done.3
  87.7 0.1 copy.31
  87.8 0.1 div.15
  88.0 4.5 %broadcast_in_dim.4 = f32[128,6,2048]{2,1,0:T(8,128)} broadcast(bf16[128,2048]{1,0:T(8,128)(2,1)S(1)} %copy-done.2), dimensions={0,2} | broadcast | bytes 6815744 | tf_op jit(solution)/shard_map/broadcast_in_dim | solution.py:34
  92.4 8.6 %convert_element_type.59 = f32[768,2048]{1,0:T(8,128)} reshape(f32[128,6,2048]{2,1,0:T(8,128)} %broadcast_in_dim.4) | data formatting | bytes 12582912 | tf_op jit(solution)/shard_map/convert_element_type | solution.py:34
  101.1 10.5 %scatter_custom_fusion = bf16[1024,1024]{1,0:T(8,128)(2,1)S(1)} fusion(s32[768]{0:T(1024)S(1)} %fusion.33, f32[768,2048]{1,0:T(8,128)} %convert_element_type.59, s32[]{:T(128)} %constant.10.clone.1, s32[]{:T(128)S(6)} %select_n.17, f32[768]{0:T(1024)S(1)} %div.15, bf16[]{:T(256)} %constant.8.clone.1), kind=kCustom, calls=%fused_computation.27 | custom fusion | flops 1572864 | bytes 5248004 | tf_op jit(solution)/shard_map/scatter | solution.py:39
  111.6 51.8 %all_to_all.16 = bf16[16,4,16,1024]{3,2,1,0:T(8,128)(2,1)S(1)} all-to-all(bf16[16,4,16,1024]{3,2,1,0:T(8,128)(2,1)S(1)} %bitcast.84), channel_id=1, replica_groups=mesh['dp'=16,'expert'=2] {'dp'}, dimensions={0} | all-to-all | bytes 4194304 | tf_op jit(solution)/shard_map/all_to_all | solution.py:58
  163.4 1.5 copy.32
  164.9 0.0 all-gather.3.cloned.1.call-update
  164.9 0.0 all-gather.5.cloned.1.call-done
  164.9 12.7 %fusion.2 = f32[4,16,16,704]{3,2,1,0:T(8,128)S(1)} fusion(bf16[16,4,16,2048]{3,2,0,1:T(8,128)(2,1)} %all-gather.5.cloned.1.call-done, bf16[4,704,2048]{2,1,0:T(8,128)(2,1)} %param.13), kind=kOutput, calls=%fused_computation.7 | convolution fusion | flops 2952790016 | bytes 18612224 | tf_op jit(solution)/shard_map/sekd,ehd->sekh/dot_general | solution.py:56
  177.6 0.0 all-gather.3.cloned.1.call-done
  177.6 9.4 %fusion.14 = bf16[16,4,16,704]{3,2,0,1:T(8,128)(2,1)S(1)} fusion(f32[4,16,16,704]{3,2,1,0:T(8,128)S(1)} %fusion.2, bf16[16,4,16,2048]{3,2,0,1:T(8,128)(2,1)} %all-gather.3.cloned.1.call-done, bf16[4,704,2048]{2,1,0:T(8,128)(2,1)} %param.14), kind=kOutput, calls=%fused_computation.22 | convolution fusion | flops 2959278080 | bytes 20054016 | tf_op jit(solution)/shard_map/sekd,ehd->sekh/dot_general | solution.py:65
  187.0 8.6 %convert_bitcast_fusion = bf16[16,4,16,2048]{3,2,0,1:T(8,128)(2,1)S(1)} fusion(bf16[16,4,16,704]{3,2,0,1:T(8,128)(2,1)S(1)} %fusion.14, bf16[4,704,2048]{2,1,0:T(8,128)(2,1)} %param.13), kind=kOutput, calls=%fused_computation.11 | convolution fusion | flops 2954887168 | bytes 17170432 | tf_op jit(solution)/shard_map/sekh,ehd->sekd/dot_general | solution.py:71
  195.6 2.3 copy.34
  198.0 6.2 %all-to-all-start.2 = ((bf16[16,4,16,2048]{3,2,1,0:T(8,128)(2,1)}), bf16[16,4,16,2048]{3,2,1,0:T(8,128)(2,1)}, u32[]{:S(2)}, u32[]{:S(2)}) async-start(bf16[16,4,16,2048]{3,2,1,0:T(8,128)(2,1)} %copy.34), calls=%async_computation.2 | async-start | bytes 8388608 | tf_op jit(solution)/shard_map/all_to_all | solution.py:80
  204.1 0.3 reduce-scatter.2.cloned.1.call-start
  204.4 9.9 %bitcast_convert_fusion = bf16[4,704,2048]{2,1,0:T(8,128)(2,1)} fusion(bf16[16,4,16,2048]{3,2,0,1:T(8,128)(2,1)} %all-gather.3.cloned.1.call-done, f32[4,16,16,704]{3,2,1,0:T(8,128)S(1)} %fusion.2), kind=kOutput, calls=%fused_computation.3 | convolution fusion | flops 2962161664 | bytes 18612224 | tf_op jit(solution)/shard_map/sekh,sekd->ehd/dot_general | solution.py:74
  214.3 70.3 %all-to-all-done.2 = bf16[16,4,16,2048]{3,2,1,0:T(8,128)(2,1)} async-done(((bf16[16,4,16,2048]{3,2,1,0:T(8,128)(2,1)}), bf16[16,4,16,2048]{3,2,1,0:T(8,128)(2,1)}, u32[]{:S(2)}, u32[]{:S(2)}) %all-to-all-start.2) | async-done | bytes 4194336 | tf_op jit(solution)/shard_map/all_to_all | solution.py:80
  284.6 9.1 %gather_fusion = bf16[768,2048]{1,0:T(8,128)(2,1)S(1)} fusion(bf16[1024,2048]{1,0:T(8,128)(2,1)} %bitcast.10, s32[1024]{0:T(1024)S(1)} %pad_clamp_fusion), kind=kCustom, calls=%fused_computation | custom fusion | bytes 6294528 | tf_op jit(solution)/shard_map/gather | solution.py:82
  293.7 2.8 gather.6
  296.5 5.8 %reduce_sum.25 = bf16[128,2048]{1,0:T(8,128)(2,1)} reduce(bf16[128,6,2048]{2,1,0:T(8,128)(2,1)} %gather.6, bf16[]{:T(256)} %constant.8.clone.1), dimensions={1}, to_apply=%region_5.6 | reduce | flops 1310720 | bytes 3670018 | tf_op jit(solution)/shard_map/reduce_sum | solution.py:83
  302.3 0.0 reduce-scatter.2.cloned.1.call-update
  302.4 0.0 copy-start.1
  302.4 9.8 %bitcast_convert_fusion.1 = bf16[4,704,2048]{2,1,0:T(8,128)(2,1)} fusion(bf16[16,4,16,704]{3,2,0,1:T(8,128)(2,1)S(1)} %copy-done.5, bf16[16,4,16,2048]{3,2,0,1:T(8,128)(2,1)} %all-gather.5.cloned.1.call-done), kind=kOutput, calls=%fused_computation.4 | convolution fusion | flops 2958557184 | bytes 17170432 | tf_op jit(solution)/shard_map/sekh,sekd->ehd/dot_general | solution.py:77
  312.2 13.2 %reduce-scatter.2.cloned.1.call-done = bf16[128,1024]{1,0:T(8,128)(2,1)} async-done(((bf16[128,2048]{1,0:T(8,128)(2,1)}), bf16[128,1024]{1,0:T(8,128)(2,1)}) %reduce-scatter.2.cloned.1.call-update) | async-done | bytes 262160 | tf_op jit(solution)/shard_map/reduce_scatter | solution.py:84
  325.4 1.8 convert_element_type.67
  327.2 0.0 copy-done.1
  (12 shorter events, 0.1 us)
Async XLA Ops:
  7.2 4.2 %copy-start = (bf16[4,2048]{1,0:T(4,128)(2,1)S(1)}, bf16[4,2048]{1,0:T(4,128)(2,1)}, u32[]{:S(2)}) copy-start(bf16[4,2048]{1,0:T(4,128)(2,1)} %param.10) | copy-start | bytes 49156
  7.2 157.8 %all-gather.5.cloned.1.call-start = ((), (), s32[]{:S(2)}) async-start(), calls=%async_computation.5 | async-start | bytes 6291456 | tf_op jit(solution)/shard_map/all_gather | solution.py:48
  86.1 1.6 copy-start.3
  86.1 1.9 copy-start.2
  87.6 90.0 %all-gather.3.cloned.1.call-start = ((), (), s32[]{:S(2)}) async-start(), calls=%async_computation.4 | async-start | bytes 6291456 | tf_op jit(solution)/shard_map/all_gather | solution.py:57
  187.0 8.6 %copy-start.4 = (bf16[16,4,16,704]{3,2,0,1:T(8,128)(2,1)}, bf16[16,4,16,704]{3,2,0,1:T(8,128)(2,1)S(1)}, u32[]{:S(2)}) copy-start(bf16[16,4,16,704]{3,2,0,1:T(8,128)(2,1)S(1)} %fusion.14) | copy-start | bytes 4325380
  198.0 86.7 %all-to-all-start.2 = ((bf16[16,4,16,2048]{3,2,1,0:T(8,128)(2,1)}), bf16[16,4,16,2048]{3,2,1,0:T(8,128)(2,1)}, u32[]{:S(2)}, u32[]{:S(2)}) async-start(bf16[16,4,16,2048]{3,2,1,0:T(8,128)(2,1)} %copy.34), calls=%async_computation.2 | async-start | bytes 8388608 | tf_op jit(solution)/shard_map/all_to_all | solution.py:80
  204.1 121.3 %reduce-scatter.2.cloned.1.call-start = ((), (), s32[]{:S(2)}) async-start(), calls=%async_computation.6 | async-start | bytes 786432 | tf_op jit(solution)/shard_map/reduce_scatter | solution.py:84
  296.5 5.8 %copy-start.5 = (bf16[16,4,16,704]{3,2,0,1:T(8,128)(2,1)S(1)}, bf16[16,4,16,704]{3,2,0,1:T(8,128)(2,1)}, u32[]{:S(2)}) copy-start(bf16[16,4,16,704]{3,2,0,1:T(8,128)(2,1)} %copy-done.4) | copy-start | bytes 4325380
  302.4 24.8 %copy-start.1 = (bf16[4,2048]{1,0:T(4,128)(2,1)S(1)}, bf16[4,2048]{1,0:T(4,128)(2,1)}, u32[]{:S(2)}) copy-start(bf16[4,2048]{1,0:T(4,128)(2,1)} %param.10) | copy-start | bytes 49156
Sparse Core Ops, SparseCore 0:
  87.8 11.9 all-gather.4
  165.0 11.8 all-gather.2
  302.5 22.8 reduce-scatter.1
where the time goes:
time: 336 us; the launch traced here: 334 us
  blocking collectives  109 us (32%)
  waiting for transfers between devices  83.6 us (25%)
  matrix products  51.7 us (15%)
  local copies, waits for them, and re-layouts  48.3 us (14%)
  other arithmetic  20.8 us (6%)
  between operations  14 us (4%)
  starting transfers between devices  6.51 us (2%)
    all_to_all x1, waiting for transfers between devices, local(): lax.all_to_all(partial_value, 'dp', split_axis=0, concat_axis=0, tiled=True)  70.3 us
    all_to_all x1, blocking collectives, local(): lax.all_to_all(place_slots(column_cut(route_rows)), 'dp', split_axis=0, c...  57 us
    all_to_all x1, blocking collectives, local(): lax.all_to_all(place_slots(column_cut(scaled)), 'dp', split_axis=0, conca...  51.8 us
    reduce_scatter x1, waiting for transfers between devices, local(): lax.psum_scatter(summed.astype(jnp.bfloat16), 'expert', scatter_dimension...  13.2 us
    dot_general x1, matrix products, local(): jnp.einsum('sekd,ehd->sekh', full_rows, up_weight, preferred_element_type...  12.7 us
    gather x2, local copies, waits for them, and re-layouts, local(): flat_back[target_pos].astype(jnp.float32)  11.9 us
    scatter x1, other arithmetic, place_slots(): filled = blank_buffer.at[target_pos].set(values)  10.5 us
    dot_general x1, matrix products, local(): jnp.einsum('sekh,sekd->ehd', hidden, backward_full_rows, preferred_elemen...  9.88 us
  transfers between devices with their start and end apart: 4, of which 2 were waited for; matrix products, arithmetic and copies ran while one was open for 17% of the time, Pallas kernels for 0%

commit v1 on v0

v1 whole, which is shorter than its diff:
```python
import functools

import jax
import jax.numpy as jnp
from jax import lax
from jax.experimental import pallas as pl
from jax.experimental.pallas import tpu as pltpu
from jax.sharding import PartitionSpec as P

EXPERTS = 64
TOPK = 6
CAP = 16
META = 16
F32 = jnp.float32
BF16 = jnp.bfloat16
VMEM_LIMIT = 48 << 20


def outer_extent(mesh):
    line = list(mesh.devices.reshape(mesh.devices.shape[0], -1)[:, 0])
    total = len(line)
    block = 1
    coords = [getattr(device, "coords", None) for device in line]
    if all(c is not None for c in coords):
        for axis in range(len(coords[0])):
            run = 1
            while run < total and coords[run][axis] == coords[0][axis]:
                run += 1
            if run < total:
                block = max(block, run)
    if block == 1:
        while block * block < total:
            block *= 2
    return total // block


def dot(a, b, dims):
    return lax.dot_general(a, b, (dims, ((), ())), preferred_element_type=F32)


def payload_body(where, tokens, cotangent, meta, bias, out):
    rows = tokens.shape[0]
    arms = meta[2 * TOPK : 2 * TOPK + 1, :].astype(F32)
    ids = lax.broadcasted_iota(jnp.int32, (bias.shape[0], rows), 0).astype(F32)
    pick = (ids == arms).astype(BF16)
    lift = dot(pick, bias[...], ((0,), (0,)))
    out[0:rows, :] = (tokens[...].astype(F32) + lift).astype(BF16)
    out[rows : 2 * rows, :] = cotangent[...]
    out[2 * rows :, :] = jnp.zeros((META, out.shape[1]), BF16)
    out[2 * rows :, 0:rows] = meta[...]


def choose_body(inner, experts_here, where, *refs):
    outs = refs[-(inner + 1) :]
    payloads = refs[: -(inner + 1)]
    table_out = outs[-1]
    rows = (payloads[0].shape[0] - META) // 2
    width = payloads[0].shape[1]
    if len(payloads) == 1:
        load = lambda a, b, c, d: payloads[0][a:b, c:d]
    else:
        flag = where[3] == 1
        load = lambda a, b, c, d: jnp.where(flag, payloads[0][a:b, c:d], payloads[1][a:b, c:d])
    meta = load(2 * rows, 2 * rows + META, 0, rows).astype(F32)
    count = inner * experts_here
    line = lax.broadcasted_iota(jnp.int32, (count, rows), 0)
    owner = jnp.bitwise_xor(lax.div(line, experts_here), where[2])
    ids = ((where[1] * inner + owner) * experts_here + lax.rem(line, experts_here)).astype(F32)
    named = jnp.zeros((count, rows), F32)
    weight = jnp.zeros((count, rows), F32)
    for k in range(TOPK):
        hit = (ids == meta[k : k + 1, :]).astype(F32)
        named = named + hit
        weight = weight + hit * meta[TOPK + k : TOPK + k + 1, :]
    earlier = (
        lax.broadcasted_iota(jnp.int32, (rows, rows), 0) < lax.broadcasted_iota(jnp.int32, (rows, rows), 1)
    ).astype(F32)
    rank = dot(named.astype(BF16), earlier.astype(BF16), ((1,), (0,)))
    rank = jnp.where(named > 0, rank, -1.0)
    slot = lax.broadcasted_iota(jnp.int32, (count, CAP, rows), 1).astype(F32)
    here = slot == rank[:, None, :]
    table = jnp.where(here, 1.0, 0.0).reshape(count * CAP, rows).astype(BF16)
    scale = jnp.where(here, (weight * (1.0 / 64.0))[:, None, :], 0.0).reshape(count * CAP, rows).astype(BF16)
    table_out[...] = table
    lifted = dot(table, load(0, rows, 0, width), ((1,), (0,))).astype(BF16)
    scaled = dot(scale, load(rows, 2 * rows, 0, width), ((1,), (0,))).astype(BF16)
    part = experts_here * CAP
    for m in range(inner):
        outs[m][:, 0:width] = lifted[m * part : (m + 1) * part]
        outs[m][:, width : 2 * width] = scaled[m * part : (m + 1) * part]


def gathered(refs):
    return jnp.concatenate([ref[...].reshape(-1, ref.shape[-1]) for ref in refs], axis=0)


def forward_body(rounds, pieces, where, *refs):
    xs = refs[: rounds * pieces]
    up, hidden_out, slope_out = refs[rounds * pieces :]
    total = None
    for q in range(pieces):
        x = gathered(xs[q * rounds : (q + 1) * rounds])
        width = x.shape[1]
        at = pl.multiple_of(jnp.bitwise_xor(where[0], q) * width, width)
        term = dot(up[0, :, pl.ds(at, width)], x, ((1,), (1,)))
        total = term if total is None else total + term
    s = 1.0 / (1.0 + jnp.exp(-total))
    hidden_out[0] = (total * s).astype(BF16)
    slope_out[0] = s * (1.0 + total * (1.0 - s))


def backward_body(rounds, pieces, where, *refs):
    xs = refs[: rounds * pieces]
    down, up, slope, pre_out = refs[rounds * pieces : rounds * pieces + 4]
    outs = refs[rounds * pieces + 4 :]
    total = None
    for q in range(pieces):
        x = gathered(xs[q * rounds : (q + 1) * rounds])
        width = x.shape[1]
        at = pl.multiple_of(jnp.bitwise_xor(where[0], q) * width, width)
        term = dot(down[0, :, pl.ds(at, width)], x, ((1,), (1,)))
        total = term if total is None else total + term
    pre = (total * slope[0]).astype(BF16)
    pre_out[0] = pre
    for q in range(pieces):
        width = outs[0].shape[-1]
        at = pl.multiple_of(jnp.bitwise_xor(where[0], q) * width, width)
        part = dot(pre, up[0, :, pl.ds(at, width)], ((0,), (0,))).astype(BF16)
        each = part.shape[0] // rounds
        for r in range(rounds):
            ref = outs[q * rounds + r]
            ref[...] = part[r * each : (r + 1) * each].reshape(ref.shape)


def grads_body(rounds, pieces, where, *refs):
    n = rounds * pieces
    lifted, scaled = refs[:n], refs[n : 2 * n]
    hidden, pre, grad_up, grad_down = refs[2 * n :]
    for q in range(pieces):
        width = lifted[0].shape[-1]
        at = pl.multiple_of(jnp.bitwise_xor(where[0], q) * width, width)
        x = gathered(lifted[q * rounds : (q + 1) * rounds])
        grad_up[0, :, pl.ds(at, width)] = dot(pre[0], x, ((1,), (0,))).astype(BF16)
        x = gathered(scaled[q * rounds : (q + 1) * rounds])
        grad_down[0, :, pl.ds(at, width)] = dot(hidden[0], x, ((1,), (0,))).astype(BF16)


def combine_body(blocks, out_dtype, extra, *refs):
    table, out = refs[0], refs[-1]
    rows = jnp.concatenate([ref[...] for ref in refs[1 : 1 + blocks]], axis=0)
    total = dot(table[...], rows, ((0,), (0,)))
    for ref in refs[1 + blocks : 1 + blocks + extra]:
        total = total + ref[...].astype(F32)
    out[...] = total.astype(out_dtype)


def local(outer, tokens, arms, arm_bias, routes, gates, up_weight, down_weight, cotangent):
    count, features = tokens.shape
    here, hidden_width, _ = up_weight.shape
    inner = lax.axis_size("dp") // outer
    pieces = lax.axis_size("expert")
    width = features // pieces
    part = here * CAP
    plane = inner * part
    line = outer * inner * CAP
    dp_index = lax.axis_index("dp")
    core = lax.axis_index("expert")
    z_index = dp_index // inner
    edge = jnp.logical_or(z_index == 0, z_index == outer - 1)
    where = jnp.stack([core, z_index, dp_index % inner, edge.astype(jnp.int32)]).astype(jnp.int32)
    smem = pl.BlockSpec(memory_space=pltpu.SMEM)
    vmem = pl.BlockSpec(memory_space=pltpu.VMEM)
    params = pltpu.CompilerParams(vmem_limit_bytes=VMEM_LIMIT)
    shape = jax.ShapeDtypeStruct

    def cost(flops, moved):
        return pl.CostEstimate(flops=int(flops), bytes_accessed=int(moved), transcendentals=0)

    meta = jnp.concatenate(
        [
            routes.T.astype(BF16),
            gates.T.astype(BF16),
            arms[None, :].astype(BF16),
            jnp.zeros((META - 2 * TOPK - 1, count), BF16),
        ],
        axis=0,
    )
    payload = pl.pallas_call(
        payload_body,
        grid_spec=pltpu.PrefetchScalarGridSpec(
            num_scalar_prefetch=1,
            grid=(1,),
            in_specs=[
                pl.BlockSpec((count, width), lambda i, w: (0, w[0])),
                pl.BlockSpec((count, width), lambda i, w: (0, w[0])),
                pl.BlockSpec((META, count), lambda i, w: (0, 0)),
                pl.BlockSpec((arm_bias.shape[0], width), lambda i, w: (0, w[0])),
            ],
            out_specs=pl.BlockSpec((2 * count + META, width), lambda i, w: (0, 0)),
        ),
        out_shape=shape((2 * count + META, width), BF16),
        compiler_params=params,
        name="payload",
    )(where, tokens, cotangent, meta, arm_bias)

    def across(value, m):
        return lax.ppermute(value, "dp", [(i, i ^ (m * inner)) for i in range(outer * inner)])

    def within(value, m):
        return lax.ppermute(value, "dp", [(i, i ^ m) for i in range(outer * inner)])

    def core_swap(value, q):
        return lax.ppermute(value, "expert", [(i, i ^ q) for i in range(pieces)])

    if outer == 4:
        middle = [(i, i ^ (3 * inner)) for i in range(inner, 3 * inner)]
        outward = [(i, i ^ inner) for i in range(inner, 3 * inner)]
        near = across(payload, 1)
        mid = lax.ppermute(payload, "dp", middle)
        far = lax.ppermute(near, "dp", middle)
        out_mid = lax.ppermute(mid, "dp", outward)
        out_far = lax.ppermute(far, "dp", outward)
        sources = [(payload,), (near,), (out_mid, far), (out_far, mid)]
    else:
        sources = [(payload,)] + [(across(payload, m),) for m in range(1, outer)]

    def choose(candidates):
        outs = pl.pallas_call(
            functools.partial(choose_body, inner, here),
            in_specs=[smem] + [vmem] * len(candidates),
            out_specs=[vmem] * (inner + 1),
            out_shape=[shape((part, 2 * width), BF16)] * inner + [shape((plane, count), BF16)],
            compiler_params=params,
            cost_estimate=cost(4 * plane * count * width, 6 * plane * width),
            name="choose",
        )(where, *candidates)
        return outs[:-1], outs[-1]

    tables, owned = [], []
    for candidates in sources:
        blocks, table = choose(candidates)
        tables.append(table)
        arrived = [blocks[0]] + [within(blocks[m], m) for m in range(1, inner)]
        mine = jnp.concatenate(arrived, axis=0).reshape(inner, here, CAP, 2 * width)
        owned.append([mine] + [core_swap(mine, q) for q in range(1, pieces)])

    rows_in = [owned[r][q] for q in range(pieces) for r in range(outer)]
    n_in = len(rows_in)
    lifted_spec = [pl.BlockSpec((inner, 1, CAP, width), lambda e: (0, e, 0, 0))] * n_in
    scaled_spec = [pl.BlockSpec((inner, 1, CAP, width), lambda e: (0, e, 0, 1))] * n_in
    weight_spec = pl.BlockSpec((1, hidden_width, features), lambda e: (e, 0, 0))
    unit_spec = pl.BlockSpec((1, hidden_width, line), lambda e: (e, 0, 0))
    weight_bytes = 2 * here * hidden_width * features
    row_bytes = 2 * here * line * features
    flops = 2 * here * line * hidden_width * features
    unit_shape = (here, hidden_width, line)
    hidden, slope = pl.pallas_call(
        functools.partial(forward_body, outer, pieces),
        grid=(here,),
        in_specs=[smem] + lifted_spec + [weight_spec],
        out_specs=[unit_spec, unit_spec],
        out_shape=[shape(unit_shape, BF16), shape(unit_shape, F32)],
        compiler_params=params,
        cost_estimate=cost(flops, weight_bytes + row_bytes),
        name="forward",
    )(where, *rows_in, up_weight)
    back = pl.pallas_call(
        functools.partial(backward_body, outer, pieces),
        grid=(here,),
        in_specs=[smem] + scaled_spec + [weight_spec, weight_spec, unit_spec],
        out_specs=[unit_spec] + lifted_spec,
        out_shape=[shape(unit_shape, BF16)] + [shape((inner, here, CAP, width), BF16)] * n_in,
        compiler_params=params,
        cost_estimate=cost(2 * flops, 2 * weight_bytes + 2 * row_bytes),
        name="backward",
    )(where, *rows_in, down_weight, up_weight, slope)
    pre, partial = back[0], back[1:]
    grad_up, grad_down = pl.pallas_call(
        functools.partial(grads_body, outer, pieces),
        grid=(here,),
        in_specs=[smem] + lifted_spec + scaled_spec + [unit_spec, unit_spec],
        out_specs=[weight_spec, weight_spec],
        out_shape=[shape(up_weight.shape, BF16)] * 2,
        compiler_params=params,
        cost_estimate=cost(2 * flops, 2 * weight_bytes + 2 * row_bytes),
        name="grads",
    )(where, *rows_in, *rows_in, hidden, pre)

    def combine(r, blocks, extra, dtype):
        return pl.pallas_call(
            functools.partial(combine_body, len(blocks), dtype, len(extra)),
            in_specs=[vmem] * (1 + len(blocks) + len(extra)),
            out_specs=vmem,
            out_shape=shape((count, width), dtype),
            compiler_params=params,
            cost_estimate=cost(2 * plane * count * width, 2 * plane * width),
            name="combine",
        )(tables[r], *blocks, *extra)

    sums = []
    for r in reversed(range(outer)):
        total = partial[r].astype(F32)
        for q in range(1, pieces):
            total = total + core_swap(partial[q * outer + r], q).astype(F32)
        ready = total.astype(BF16).reshape(inner, part, width)
        blocks = [ready[0]] + [within(ready[m], m) for m in range(1, inner)]
        if r:
            sums.append(across(combine(r, blocks, [], BF16), r))
        else:
            grad_tokens = combine(0, blocks, sums, F32)
    return (grad_tokens, grad_up, grad_down)


def solution(mesh):
    in_specs = (
        P("dp", None),
        P("dp"),
        P(),
        P("dp", None),
        P("dp", None),
        P("dp", "expert", None),
        P("dp", "expert", None),
        P("dp", None),
    )
    out_specs = (P("dp", "expert"), P("dp", "expert", None), P("dp", "expert", None))
    return jax.shard_map(
        functools.partial(local, outer_extent(mesh)), mesh=mesh, in_specs=in_specs, out_specs=out_specs, check_vma=False
    )
```

time: 336 us -> 160 us (0.48)
  blocking collectives: 109 us -> 0 us
  matrix products: 51.7 us -> 0 us
  starting transfers between devices: 6.51 us -> 55.6 us
  Pallas kernels: 0 us -> 45.5 us
  local copies, waits for them, and re-layouts: 48.3 us -> 4.06 us
  waiting for transfers between devices: 83.6 us -> 50.4 us
  other arithmetic: 20.8 us -> 2.68 us
  between operations: 14 us -> 1.1 us
    all_to_all x2 -> x0, blocking collectives: 109 us -> none  [the longest x1 57 us: local(): lax.all_to_all(place_slots(column_cut(route_rows)), 'dp', split_axis=0, c...]
    all_to_all x1 -> x0, waiting for transfers between devices: 70.3 us -> none  [local(): lax.all_to_all(partial_value, 'dp', split_axis=0, concat_axis=0, tiled=True)]
    ppermute x0 -> x40, starting transfers between devices: none -> 55.6 us  [the longest x24 31.4 us: within(): return lax.ppermute(value, 'dp', [(i, i ^ m) for i in range(outer * inner)])]
    dot_general x6 -> x0, matrix products: 51.7 us -> none  [the longest x1 12.7 us: local(): jnp.einsum('sekd,ehd->sekh', full_rows, up_weight, preferred_element_type...]
    ppermute x0 -> x40, waiting for transfers between devices: none -> 50.4 us  [the longest x24 23.9 us: within(): return lax.ppermute(value, 'dp', [(i, i ^ m) for i in range(outer * inner)])]
    pallas_call x0 -> x12, Pallas kernels: none -> 45.5 us  [the longest x1 17.1 us: local(): pl.pallas_call(functools.partial(backward_body, outer, pieces), grid=(her...]
    reduce_scatter x1 -> x0, waiting for transfers between devices: 13.2 us -> none  [local(): lax.psum_scatter(summed.astype(jnp.bfloat16), 'expert', scatter_dimension...]
    gather x2 -> x0, local copies, waits for them, and re-layouts: 11.9 us -> none  [local(): flat_back[target_pos].astype(jnp.float32)]
  transfers between devices with their start and end apart: 4 -> 40, of which waited for: 2 -> 15; matrix products, arithmetic and copies ran while one was open for 17% -> 1% of each run, Pallas kernels for 0% -> 11%
where the time goes in v1:
time: 160 us; the launch traced here: 159 us
  starting transfers between devices  55.6 us (35%)
  waiting for transfers between devices  50.4 us (32%)
  Pallas kernels  45.5 us (28%)
  local copies, waits for them, and re-layouts  4.06 us (3%)
  other arithmetic  2.68 us (2%)
    ppermute x24, starting transfers between devices, within(): return lax.ppermute(value, 'dp', [(i, i ^ m) for i in range(outer * inner)])  31.4 us
    ppermute x24, waiting for transfers between devices, within(): return lax.ppermute(value, 'dp', [(i, i ^ m) for i in range(outer * inner)])  23.9 us
    ppermute x4, starting transfers between devices, across(): lax.ppermute(value, 'dp', [(i, i ^ m * inner) for i in range(outer * inne...  18.6 us
    pallas_call x1, Pallas kernels, local(): pl.pallas_call(functools.partial(backward_body, outer, pieces), grid=(her...  17.1 us
    ppermute x4, waiting for transfers between devices, across(): lax.ppermute(value, 'dp', [(i, i ^ m * inner) for i in range(outer * inne...  12.8 us
    pallas_call x1, Pallas kernels, local(): pl.pallas_call(functools.partial(grads_body, outer, pieces), grid=(here,)...  12.3 us
    ppermute x1, waiting for transfers between devices, local(): out_mid = lax.ppermute(mid, 'dp', outward)  9.56 us
    pallas_call x1, Pallas kernels, local(): pl.pallas_call(functools.partial(forward_body, outer, pieces), grid=(here...  9.13 us
  transfers between devices with their start and end apart: 40, of which 15 were waited for; matrix products, arithmetic and copies ran while one was open for 1% of the time, Pallas kernels for 11%

profile of v1, /device:TPU:0, one launch (start us, length us, event | category | flops | bytes accessed | tf_op | source)
XLA Modules:
  0.0 159.3 jit_solution(9470747691122250452)
XLA Ops:
  2.3 1.0 copy-done.8
  3.3 1.0 copy-done.9
  5.1 0.8 payload.1.refs_0_
  5.9 3.1 %collective-permute-start.3 = (bf16[272,1024]{1,0:T(8,128)(2,1)S(1)}, bf16[272,1024]{1,0:T(8,128)(2,1)S(1)}, u32[]{:S(2)}, u32[]{:S(2)}) collective-permute-start(bf16[272,1024]{1,0:T(8,128)(2,1)S(1)} %payload.1.refs_0_), channel_id=1, source_target_pairs={{0,8},{2,10},{4,12},{6,14},{8,0},{10,2},{12,4},{14,6},{16,24},{18,... | collective-permute-start | bytes 1671176 | tf_op jit(solution)/shard_map/ppermute | solution.py:207
  9.6 11.9 %collective-permute-done.3.refs_0_ = bf16[272,1024]{1,0:T(8,128)(2,1)S(1)} collective-permute-done((bf16[272,1024]{1,0:T(8,128)(2,1)S(1)}, bf16[272,1024]{1,0:T(8,128)(2,1)S(1)}, u32[]{:S(2)}, u32[]{:S(2)}) %collective-permute-start.3) | collective-permute-done | bytes 557088 | tf_op jit(solution)/shard_map/ppermute | solution.py:207
  22.3 1.3 collective-permute-start.8
  23.6 1.3 collective-permute-start.13
  24.9 1.1 choose.4
  26.0 1.7 %collective-permute-start = (bf16[64,2048]{1,0:T(8,128)(2,1)S(1)}, bf16[64,2048]{1,0:T(8,128)(2,1)S(1)}, u32[]{:S(2)}, u32[]{:S(2)}) collective-permute-start(bf16[64,2048]{1,0:T(8,128)(2,1)S(1)} %get-tuple-element.38), channel_id=1, source_target_pairs={{0,2},{2,0},{4,6},{6,4},{8,10},{10,8},{12,14},{14,12},{16,18},{18,... | collective-permute-start | bytes 786440 | tf_op jit(solution)/shard_map/ppermute | solution.py:210
  27.7 1.5 collective-permute-start.1
  29.5 1.1 choose.5
  30.6 9.6 %collective-permute-done.8.refs_0_ = bf16[272,1024]{1,0:T(8,128)(2,1)S(1)} collective-permute-done((bf16[272,1024]{1,0:T(8,128)(2,1)S(1)}, bf16[272,1024]{1,0:T(8,128)(2,1)S(1)}, u32[]{:S(2)}, u32[]{:S(2)}) %collective-permute-start.8) | collective-permute-done | bytes 557088 | tf_op jit(solution)/shard_map/ppermute | solution.py:221
  40.2 1.5 collective-permute-start.4
  41.7 1.1 choose.6
  42.8 1.5 collective-permute-start.5
  44.8 1.5 collective-permute-start.10
  46.5 2.9 %collective-permute-done.4 = bf16[64,2048]{1,0:T(8,128)(2,1)S(1)} collective-permute-done((bf16[64,2048]{1,0:T(8,128)(2,1)S(1)}, bf16[64,2048]{1,0:T(8,128)(2,1)S(1)}, u32[]{:S(2)}, u32[]{:S(2)}) %collective-permute-start.4) | collective-permute-done | bytes 262176 | tf_op jit(solution)/shard_map/ppermute | solution.py:210
  49.4 1.5 collective-permute-start.11
  51.5 2.4 %collective-permute-start.12 = (bf16[64,2048]{1,0:T(8,128)(2,1)S(1)}, bf16[64,2048]{1,0:T(8,128)(2,1)S(1)}, u32[]{:S(2)}, u32[]{:S(2)}) collective-permute-start(bf16[64,2048]{1,0:T(8,128)(2,1)S(1)} %get-tuple-element.48), channel_id=1, source_target_pairs={{0,6},{2,4},{4,2},{6,0},{8,14},{10,12},{12,10},{14,8},{16,22},{18,... | collective-permute-start | bytes 786440 | tf_op jit(solution)/shard_map/ppermute | solution.py:210
  53.9 1.1 choose.7
  55.0 2.8 %collective-permute-done.5 = bf16[64,2048]{1,0:T(8,128)(2,1)S(1)} collective-permute-done((bf16[64,2048]{1,0:T(8,128)(2,1)S(1)}, bf16[64,2048]{1,0:T(8,128)(2,1)S(1)}, u32[]{:S(2)}, u32[]{:S(2)}) %collective-permute-start.5) | collective-permute-done | bytes 262176 | tf_op jit(solution)/shard_map/ppermute | solution.py:210
  58.3 1.5 collective-permute-start.15
  59.8 0.8 collective-permute-done.10
  60.6 2.5 %collective-permute-start.16 = (bf16[64,2048]{1,0:T(8,128)(2,1)S(1)}, bf16[64,2048]{1,0:T(8,128)(2,1)S(1)}, u32[]{:S(2)}, u32[]{:S(2)}) collective-permute-start(bf16[64,2048]{1,0:T(8,128)(2,1)S(1)} %get-tuple-element.52), channel_id=1, source_target_pairs={{0,6},{2,4},{4,2},{6,0},{8,14},{10,12},{12,10},{14,8},{16,22},{18,... | collective-permute-start | bytes 786440 | tf_op jit(solution)/shard_map/ppermute | solution.py:210
  63.3 5.3 %collective-permute-done.11 = bf16[64,2048]{1,0:T(8,128)(2,1)S(1)} collective-permute-done((bf16[64,2048]{1,0:T(8,128)(2,1)S(1)}, bf16[64,2048]{1,0:T(8,128)(2,1)S(1)}, u32[]{:S(2)}, u32[]{:S(2)}) %collective-permute-start.11) | collective-permute-done | bytes 262176 | tf_op jit(solution)/shard_map/ppermute | solution.py:210
  69.2 2.7 %collective-permute-done.14 = bf16[64,2048]{1,0:T(8,128)(2,1)S(1)} collective-permute-done((bf16[64,2048]{1,0:T(8,128)(2,1)S(1)}, bf16[64,2048]{1,0:T(8,128)(2,1)S(1)}, u32[]{:S(2)}, u32[]{:S(2)}) %collective-permute-start.14) | collective-permute-done | bytes 262176 | tf_op jit(solution)/shard_map/ppermute | solution.py:210
  71.8 4.4 %collective-permute-done.15 = bf16[64,2048]{1,0:T(8,128)(2,1)S(1)} collective-permute-done((bf16[64,2048]{1,0:T(8,128)(2,1)S(1)}, bf16[64,2048]{1,0:T(8,128)(2,1)S(1)}, u32[]{:S(2)}, u32[]{:S(2)}) %collective-permute-start.15) | collective-permute-done | bytes 262176 | tf_op jit(solution)/shard_map/ppermute | solution.py:210
  76.5 2.6 %collective-permute-done.20.refs_7_.refs_15_ = bf16[4,4,16,2048]{3,2,1,0:T(8,128)(2,1)S(1)} collective-permute-done((bf16[4,4,16,2048]{3,2,1,0:T(8,128)(2,1)S(1)}, bf16[4,4,16,2048]{3,2,1,0:T(8,128)(2,1)S(1)}, u32[]{:S(2)}, u32[]{:S(2)}) %collective-permute-start.20) | collective-permute-done | bytes 1048608 | tf_op jit(solution)/shard_map/ppermute | solution.py:213
  79.1 1.0 copy-done.13
  80.1 9.1 %forward.1 = (bf16[4,704,256]{2,1,0:T(8,128)(2,1)}, f32[4,704,256]{2,1,0:T(8,128)}) custom-call(s32[4]{0:T(128)S(1)} %pad_add_fusion.where, bf16[4,4,16,2048]{3,2,1,0:T(8,128)(2,1)S(1)} %bitcast.31, bf16[4,4,16,2048]{3,2,1,0:T(8,128)(2,1)S(1)} %bitcast.36, bf16[4,4,16,2048]{3,2,1,0:T(8,128)(2,1)S(1)} %bitcast.41, bf16[4,4,16,2048]{3,2,1,0:T(8,128)(2,1)S(1)} %bitcast.46, ...), custom_call_target="tpu_custom_call" | custom-call | flops 2952790016 | bytes 15728640 | tf_op jit(solution)/shard_map/forward/pallas_call | solution.py:257
  89.2 17.1 %backward.1 = (bf16[4,704,256]{2,1,0:T(8,128)(2,1)}, bf16[4,4,16,1024]{3,2,1,0:T(8,128)(2,1)S(1)}, bf16[4,4,16,1024]{3,2,1,0:T(8,128)(2,1)S(1)}, bf16[4,4,16,102...) custom-call(s32[4]{0:T(128)S(1)} %pad_add_fusion.where, ...), custom_call_target="tpu_custom_call" | custom-call | flops 5905580032 | bytes 31457280 | tf_op jit(solution)/shard_map/backward/pallas_call | solution.py:267
  107.4 0.9 collective-permute-done.25
  108.5 1.6 collective-permute-start.27
  110.6 1.5 collective-permute-start.26
  112.3 1.6 collective-permute-start.32
  115.0 2.5 %collective-permute-done.27.refs_3_ = bf16[64,1024]{1,0:T(8,128)(2,1)S(1)} collective-permute-done((bf16[64,1024]{1,0:T(8,128)(2,1)S(1)}, bf16[64,1024]{1,0:T(8,128)(2,1)S(1)}, u32[]{:S(2)}, u32[]{:S(2)}) %collective-permute-start.27) | collective-permute-done | bytes 131104 | tf_op jit(solution)/shard_map/ppermute | solution.py:210
  118.0 2.5 %collective-permute-start.37 = (bf16[64,1024]{1,0:T(8,128)(2,1)S(1)}, bf16[64,1024]{1,0:T(8,128)(2,1)S(1)}, u32[]{:S(2)}, u32[]{:S(2)}) collective-permute-start(bf16[64,1024]{1,0:T(8,128)(2,1)S(1)} %bitcast.59), channel_id=1, source_target_pairs={{0,4},{2,6},{4,0},{6,2},{8,12},{10,14},{12,8},{14,10},{16,20},{18,... | collective-permute-start | bytes 393224 | tf_op jit(solution)/shard_map/ppermute | solution.py:210
  120.5 1.0 collective-permute-start.38
  121.5 1.6 collective-permute-done.32.refs_3_
  123.7 2.6 %collective-permute-start.23 = (bf16[64,1024]{1,0:T(8,128)(2,1)S(1)}, bf16[64,1024]{1,0:T(8,128)(2,1)S(1)}, u32[]{:S(2)}, u32[]{:S(2)}) collective-permute-start(bf16[64,1024]{1,0:T(8,128)(2,1)S(1)} %bitcast.62), channel_id=1, source_target_pairs={{0,4},{2,6},{4,0},{6,2},{8,12},{10,14},{12,8},{14,10},{16,20},{18,... | collective-permute-start | bytes 393224 | tf_op jit(solution)/shard_map/ppermute | solution.py:210
  126.5 1.0 collective-permute-start.24
  127.8 0.9 collective-permute-done.37.refs_3_
  129.1 2.6 %collective-permute-start.29 = (bf16[128,1024]{1,0:T(8,128)(2,1)S(1)}, bf16[128,1024]{1,0:T(8,128)(2,1)S(1)}, u32[]{:S(2)}, u32[]{:S(2)}) collective-permute-start(bf16[128,1024]{1,0:T(8,128)(2,1)S(1)} %combine.4), channel_id=1, source_target_pairs={{0,24},{2,26},{4,28},{6,30},{8,16},{10,18},{12,20},{14,22},{16,8},... | collective-permute-start | bytes 786440 | tf_op jit(solution)/shard_map/ppermute | solution.py:207
  131.7 12.2 %collective-permute-start.34 = (bf16[128,1024]{1,0:T(8,128)(2,1)S(1)}, bf16[128,1024]{1,0:T(8,128)(2,1)S(1)}, u32[]{:S(2)}, u32[]{:S(2)}) collective-permute-start(bf16[128,1024]{1,0:T(8,128)(2,1)S(1)} %combine.5), channel_id=1, source_target_pairs={{0,16},{2,18},{4,20},{6,22},{8,24},{10,26},{12,28},{14,30},{16,0},... | collective-permute-start | bytes 786440 | tf_op jit(solution)/shard_map/ppermute | solution.py:207
  144.2 0.8 collective-permute-start.39
  145.0 12.3 %grads.1 = (bf16[4,704,2048]{2,1,0:T(8,128)(2,1)}, bf16[4,704,2048]{2,1,0:T(8,128)(2,1)}) custom-call(s32[4]{0:T(128)S(1)} %pad_add_fusion.where, bf16[4,4,16,2048]{3,2,1,0:T(8,128)(2,1)S(1)} %bitcast.33, bf16[4,4,16,2048]{3,2,1,0:T(8,128)(2,1)S(1)} %bitcast.38, bf16[4,4,16,2048]{3,2,1,0:T(8,128)(2,1)S(1)} %bitcast.43, ...), custom_call_target="tpu_custom_call" | custom-call | flops 5905580032 | bytes 31457280 | tf_op jit(solution)/shard_map/grads/pallas_call | solution.py:278
  157.3 0.9 collective-permute-done.34.refs_6_
  158.3 1.1 combine.7
  (90 shorter events, 12.0 us)
Async XLA Ops:
  5.9 15.7 %collective-permute-start.3 = (bf16[272,1024]{1,0:T(8,128)(2,1)S(1)}, bf16[272,1024]{1,0:T(8,128)(2,1)S(1)}, u32[]{:S(2)}, u32[]{:S(2)}) collective-permute-start(bf16[272,1024]{1,0:T(8,128)(2,1)S(1)} %payload.1.refs_0_), channel_id=1, source_target_pairs={{0,8},{2,10},{4,12},{6,14},{8,0},{10,2},{12,4},{14,6},{16,24},{18,... | collective-permute-start | bytes 1671176 | tf_op jit(solution)/shard_map/ppermute | solution.py:207
  8.9 13.3 %collective-permute-start.7 = (bf16[272,1024]{1,0:T(8,128)(2,1)S(1)}, bf16[272,1024]{1,0:T(8,128)(2,1)S(1)}, u32[]{:S(2)}, u32[]{:S(2)}) collective-permute-start(bf16[272,1024]{1,0:T(8,128)(2,1)S(1)} %payload.1.refs_0_), channel_id=1, source_target_pairs={{8,16},{10,18},{12,20},{14,22},{16,8},{18,10},{20,12},{22,14},{9,1... | collective-permute-start | bytes 1671176 | tf_op jit(solution)/shard_map/ppermute | solution.py:219
  21.6 2.0 %collective-permute-start.9 = (bf16[272,1024]{1,0:T(8,128)(2,1)S(1)}, bf16[272,1024]{1,0:T(8,128)(2,1)S(1)}, u32[]{:S(2)}, u32[]{:S(2)}) collective-permute-start(bf16[272,1024]{1,0:T(8,128)(2,1)S(1)} %collective-permute-done.3.refs_0_), channel_id=1, source_target_pairs={{8,16},{10,18},{12,20},{14,22},{16,8},{18,10},{20,12},{22,14},{9,1... | collective-permute-start | bytes 1671176 | tf_op jit(solution)/shard_map/ppermute | solution.py:220
  22.3 17.9 %collective-permute-start.8 = (bf16[272,1024]{1,0:T(8,128)(2,1)S(1)}, bf16[272,1024]{1,0:T(8,128)(2,1)S(1)}, u32[]{:S(2)}, u32[]{:S(2)}) collective-permute-start(bf16[272,1024]{1,0:T(8,128)(2,1)S(1)} %collective-permute-done.7.refs_1_), channel_id=1, source_target_pairs={{8,0},{10,2},{12,4},{14,6},{16,24},{18,26},{20,28},{22,30},{9,1},{... | collective-permute-start | bytes 1671176 | tf_op jit(solution)/shard_map/ppermute | solution.py:221
  23.6 27.9 %collective-permute-start.13 = (bf16[272,1024]{1,0:T(8,128)(2,1)S(1)}, bf16[272,1024]{1,0:T(8,128)(2,1)S(1)}, u32[]{:S(2)}, u32[]{:S(2)}) collective-permute-start(bf16[272,1024]{1,0:T(8,128)(2,1)S(1)} %collective-permute-done.9.refs_1_), channel_id=1, source_target_pairs={{8,0},{10,2},{12,4},{14,6},{16,24},{18,26},{20,28},{22,30},{9,1},{... | collective-permute-start | bytes 1671176 | tf_op jit(solution)/shard_map/ppermute | solution.py:222
  26.0 16.8 %collective-permute-start = (bf16[64,2048]{1,0:T(8,128)(2,1)S(1)}, bf16[64,2048]{1,0:T(8,128)(2,1)S(1)}, u32[]{:S(2)}, u32[]{:S(2)}) collective-permute-start(bf16[64,2048]{1,0:T(8,128)(2,1)S(1)} %get-tuple-element.38), channel_id=1, source_target_pairs={{0,2},{2,0},{4,6},{6,4},{8,10},{10,8},{12,14},{14,12},{16,18},{18,... | collective-permute-start | bytes 786440 | tf_op jit(solution)/shard_map/ppermute | solution.py:210
  27.7 16.6 %collective-permute-start.1 = (bf16[64,2048]{1,0:T(8,128)(2,1)S(1)}, bf16[64,2048]{1,0:T(8,128)(2,1)S(1)}, u32[]{:S(2)}, u32[]{:S(2)}) collective-permute-start(bf16[64,2048]{1,0:T(8,128)(2,1)S(1)} %get-tuple-element.39), channel_id=1, source_target_pairs={{0,4},{2,6},{4,0},{6,2},{8,12},{10,14},{12,8},{14,10},{16,20},{18,... | collective-permute-start | bytes 786440 | tf_op jit(solution)/shard_map/ppermute | solution.py:210
  29.2 15.6 %collective-permute-start.2 = (bf16[64,2048]{1,0:T(8,128)(2,1)S(1)}, bf16[64,2048]{1,0:T(8,128)(2,1)S(1)}, u32[]{:S(2)}, u32[]{:S(2)}) collective-permute-start(bf16[64,2048]{1,0:T(8,128)(2,1)S(1)} %get-tuple-element.40), channel_id=1, source_target_pairs={{0,6},{2,4},{4,2},{6,0},{8,14},{10,12},{12,10},{14,8},{16,22},{18,... | collective-permute-start | bytes 786440 | tf_op jit(solution)/shard_map/ppermute | solution.py:210
  40.2 9.2 %collective-permute-start.4 = (bf16[64,2048]{1,0:T(8,128)(2,1)S(1)}, bf16[64,2048]{1,0:T(8,128)(2,1)S(1)}, u32[]{:S(2)}, u32[]{:S(2)}) collective-permute-start(bf16[64,2048]{1,0:T(8,128)(2,1)S(1)} %get-tuple-element.42), channel_id=1, source_target_pairs={{0,2},{2,0},{4,6},{6,4},{8,10},{10,8},{12,14},{14,12},{16,18},{18,... | collective-permute-start | bytes 786440 | tf_op jit(solution)/shard_map/ppermute | solution.py:210
  42.8 15.0 %collective-permute-start.5 = (bf16[64,2048]{1,0:T(8,128)(2,1)S(1)}, bf16[64,2048]{1,0:T(8,128)(2,1)S(1)}, u32[]{:S(2)}, u32[]{:S(2)}) collective-permute-start(bf16[64,2048]{1,0:T(8,128)(2,1)S(1)} %get-tuple-element.43), channel_id=1, source_target_pairs={{0,4},{2,6},{4,0},{6,2},{8,12},{10,14},{12,8},{14,10},{16,20},{18,... | collective-permute-start | bytes 786440 | tf_op jit(solution)/shard_map/ppermute | solution.py:210
  44.3 13.9 %collective-permute-start.6 = (bf16[64,2048]{1,0:T(8,128)(2,1)S(1)}, bf16[64,2048]{1,0:T(8,128)(2,1)S(1)}, u32[]{:S(2)}, u32[]{:S(2)}) collective-permute-start(bf16[64,2048]{1,0:T(8,128)(2,1)S(1)} %get-tuple-element.44), channel_id=1, source_target_pairs={{0,6},{2,4},{4,2},{6,0},{8,14},{10,12},{12,10},{14,8},{16,22},{18,... | collective-permute-start | bytes 786440 | tf_op jit(solution)/shard_map/ppermute | solution.py:210
  44.8 15.8 %collective-permute-start.10 = (bf16[64,2048]{1,0:T(8,128)(2,1)S(1)}, bf16[64,2048]{1,0:T(8,128)(2,1)S(1)}, u32[]{:S(2)}, u32[]{:S(2)}) collective-permute-start(bf16[64,2048]{1,0:T(8,128)(2,1)S(1)} %get-tuple-element.46), channel_id=1, source_target_pairs={{0,2},{2,0},{4,6},{6,4},{8,10},{10,8},{12,14},{14,12},{16,18},{18,... | collective-permute-start | bytes 786440 | tf_op jit(solution)/shard_map/ppermute | solution.py:210
  49.4 19.2 %collective-permute-start.11 = (bf16[64,2048]{1,0:T(8,128)(2,1)S(1)}, bf16[64,2048]{1,0:T(8,128)(2,1)S(1)}, u32[]{:S(2)}, u32[]{:S(2)}) collective-permute-start(bf16[64,2048]{1,0:T(8,128)(2,1)S(1)} %get-tuple-element.47), channel_id=1, source_target_pairs={{0,4},{2,6},{4,0},{6,2},{8,12},{10,14},{12,8},{14,10},{16,20},{18,... | collective-permute-start | bytes 786440 | tf_op jit(solution)/shard_map/ppermute | solution.py:210
  51.5 17.1 %collective-permute-start.12 = (bf16[64,2048]{1,0:T(8,128)(2,1)S(1)}, bf16[64,2048]{1,0:T(8,128)(2,1)S(1)}, u32[]{:S(2)}, u32[]{:S(2)}) collective-permute-start(bf16[64,2048]{1,0:T(8,128)(2,1)S(1)} %get-tuple-element.48), channel_id=1, source_target_pairs={{0,6},{2,4},{4,2},{6,0},{8,14},{10,12},{12,10},{14,8},{16,22},{18,... | collective-permute-start | bytes 786440 | tf_op jit(solution)/shard_map/ppermute | solution.py:210
  57.8 14.0 %collective-permute-start.14 = (bf16[64,2048]{1,0:T(8,128)(2,1)S(1)}, bf16[64,2048]{1,0:T(8,128)(2,1)S(1)}, u32[]{:S(2)}, u32[]{:S(2)}) collective-permute-start(bf16[64,2048]{1,0:T(8,128)(2,1)S(1)} %get-tuple-element.50), channel_id=1, source_target_pairs={{0,2},{2,0},{4,6},{6,4},{8,10},{10,8},{12,14},{14,12},{16,18},{18,... | collective-permute-start | bytes 786440 | tf_op jit(solution)/shard_map/ppermute | solution.py:210
  58.3 18.0 %collective-permute-start.15 = (bf16[64,2048]{1,0:T(8,128)(2,1)S(1)}, bf16[64,2048]{1,0:T(8,128)(2,1)S(1)}, u32[]{:S(2)}, u32[]{:S(2)}) collective-permute-start(bf16[64,2048]{1,0:T(8,128)(2,1)S(1)} %get-tuple-element.51), channel_id=1, source_target_pairs={{0,4},{2,6},{4,0},{6,2},{8,12},{10,14},{12,8},{14,10},{16,20},{18,... | collective-permute-start | bytes 786440 | tf_op jit(solution)/shard_map/ppermute | solution.py:210
  60.6 15.7 %collective-permute-start.16 = (bf16[64,2048]{1,0:T(8,128)(2,1)S(1)}, bf16[64,2048]{1,0:T(8,128)(2,1)S(1)}, u32[]{:S(2)}, u32[]{:S(2)}) collective-permute-start(bf16[64,2048]{1,0:T(8,128)(2,1)S(1)} %get-tuple-element.52), channel_id=1, source_target_pairs={{0,6},{2,4},{4,2},{6,0},{8,14},{10,12},{12,10},{14,8},{16,22},{18,... | collective-permute-start | bytes 786440 | tf_op jit(solution)/shard_map/ppermute | solution.py:210
  63.2 15.9 %copy-start = (bf16[256,2048]{1,0:T(8,128)(2,1)}, bf16[256,2048]{1,0:T(8,128)(2,1)S(1)}, u32[]{:S(2)}) copy-start(bf16[256,2048]{1,0:T(8,128)(2,1)S(1)} %pad_maximum_fusion.1) | copy-start | bytes 3145732
  68.5 7.9 %collective-permute-start.17 = (bf16[4,4,16,2048]{3,2,1,0:T(8,128)(2,1)S(1)}, bf16[4,4,16,2048]{3,2,1,0:T(8,128)(2,1)S(1)}, u32[]{:S(2)}, u32[]{:S(2)}) collective-permute-start(bf16[4,4,16,2048]{3,2,1,0:T(8,128)(2,1)S(1)} %bitcast.30), channel_id=1, source_target_pairs={{0,1},{1,0},{2,3},{3,2},{4,5},{5,4},{6,7},{7,6},{8,9},{9,8},{10,11... | collective-permute-start | bytes 3145736 | tf_op jit(solution)/shard_map/ppermute | solution.py:213
  68.5 7.9 %collective-permute-start.18 = (bf16[4,4,16,2048]{3,2,1,0:T(8,128)(2,1)S(1)}, bf16[4,4,16,2048]{3,2,1,0:T(8,128)(2,1)S(1)}, u32[]{:S(2)}, u32[]{:S(2)}) collective-permute-start(bf16[4,4,16,2048]{3,2,1,0:T(8,128)(2,1)S(1)} %bitcast.35), channel_id=1, source_target_pairs={{0,1},{1,0},{2,3},{3,2},{4,5},{5,4},{6,7},{7,6},{8,9},{9,8},{10,11... | collective-permute-start | bytes 3145736 | tf_op jit(solution)/shard_map/ppermute | solution.py:213
  69.2 20.1 %copy-start.2 = (bf16[256,2048]{1,0:T(8,128)(2,1)}, bf16[256,2048]{1,0:T(8,128)(2,1)S(1)}, u32[]{:S(2)}) copy-start(bf16[256,2048]{1,0:T(8,128)(2,1)S(1)} %pad_maximum_fusion.2) | copy-start | bytes 3145732
  71.8 4.7 %collective-permute-start.19 = (bf16[4,4,16,2048]{3,2,1,0:T(8,128)(2,1)S(1)}, bf16[4,4,16,2048]{3,2,1,0:T(8,128)(2,1)S(1)}, u32[]{:S(2)}, u32[]{:S(2)}) collective-permute-start(bf16[4,4,16,2048]{3,2,1,0:T(8,128)(2,1)S(1)} %bitcast.40), channel_id=1, source_target_pairs={{0,1},{1,0},{2,3},{3,2},{4,5},{5,4},{6,7},{7,6},{8,9},{9,8},{10,11... | collective-permute-start | bytes 3145736 | tf_op jit(solution)/shard_map/ppermute | solution.py:213
  76.4 12.9 %copy-start.4 = (bf16[256,2048]{1,0:T(8,128)(2,1)}, bf16[256,2048]{1,0:T(8,128)(2,1)S(1)}, u32[]{:S(2)}) copy-start(bf16[256,2048]{1,0:T(8,128)(2,1)S(1)} %pad_maximum_fusion.3) | copy-start | bytes 3145732
  76.4 2.7 %collective-permute-start.20 = (bf16[4,4,16,2048]{3,2,1,0:T(8,128)(2,1)S(1)}, bf16[4,4,16,2048]{3,2,1,0:T(8,128)(2,1)S(1)}, u32[]{:S(2)}, u32[]{:S(2)}) collective-permute-start(bf16[4,4,16,2048]{3,2,1,0:T(8,128)(2,1)S(1)} %bitcast.45), channel_id=1, source_target_pairs={{0,1},{1,0},{2,3},{3,2},{4,5},{5,4},{6,7},{7,6},{8,9},{9,8},{10,11... | collective-permute-start | bytes 3145736 | tf_op jit(solution)/shard_map/ppermute | solution.py:213
  76.5 12.8 %copy-start.6 = (bf16[4,4,16,2048]{3,2,1,0:T(8,128)(2,1)}, bf16[4,4,16,2048]{3,2,1,0:T(8,128)(2,1)S(1)}, u32[]{:S(2)}) copy-start(bf16[4,4,16,2048]{3,2,1,0:T(8,128)(2,1)S(1)} %collective-permute-done.17.refs_4_.refs_12_) | copy-start | bytes 3145732
  106.3 2.0 %collective-permute-start.25 = (bf16[4,4,16,1024]{3,2,1,0:T(8,128)(2,1)S(1)}, bf16[4,4,16,1024]{3,2,1,0:T(8,128)(2,1)S(1)}, u32[]{:S(2)}, u32[]{:S(2)}) collective-permute-start(bf16[4,4,16,1024]{3,2,1,0:T(8,128)(2,1)S(1)} %get-tuple-element.58), channel_id=1, source_target_pairs={{0,1},{1,0},{2,3},{3,2},{4,5},{5,4},{6,7},{7,6},{8,9},{9,8},{10,11... | collective-permute-start | bytes 1572872 | tf_op jit(solution)/shard_map/ppermute | solution.py:213
  106.5 4.1 %collective-permute-start.30 = (bf16[4,4,16,1024]{3,2,1,0:T(8,128)(2,1)S(1)}, bf16[4,4,16,1024]{3,2,1,0:T(8,128)(2,1)S(1)}, u32[]{:S(2)}, u32[]{:S(2)}) collective-permute-start(bf16[4,4,16,1024]{3,2,1,0:T(8,128)(2,1)S(1)} %get-tuple-element.61), channel_id=1, source_target_pairs={{0,1},{1,0},{2,3},{3,2},{4,5},{5,4},{6,7},{7,6},{8,9},{9,8},{10,11... | collective-permute-start | bytes 1572872 | tf_op jit(solution)/shard_map/ppermute | solution.py:213
  106.9 5.5 %collective-permute-start.21 = (bf16[4,4,16,1024]{3,2,1,0:T(8,128)(2,1)S(1)}, bf16[4,4,16,1024]{3,2,1,0:T(8,128)(2,1)S(1)}, u32[]{:S(2)}, u32[]{:S(2)}) collective-permute-start(bf16[4,4,16,1024]{3,2,1,0:T(8,128)(2,1)S(1)} %get-tuple-element.55), channel_id=1, source_target_pairs={{0,1},{1,0},{2,3},{3,2},{4,5},{5,4},{6,7},{7,6},{8,9},{9,8},{10,11... | collective-permute-start | bytes 1572872 | tf_op jit(solution)/shard_map/ppermute | solution.py:213
  107.0 7.1 %collective-permute-start.35 = (bf16[4,4,16,1024]{3,2,1,0:T(8,128)(2,1)S(1)}, bf16[4,4,16,1024]{3,2,1,0:T(8,128)(2,1)S(1)}, u32[]{:S(2)}, u32[]{:S(2)}) collective-permute-start(bf16[4,4,16,1024]{3,2,1,0:T(8,128)(2,1)S(1)} %get-tuple-element.64), channel_id=1, source_target_pairs={{0,1},{1,0},{2,3},{3,2},{4,5},{5,4},{6,7},{7,6},{8,9},{9,8},{10,11... | collective-permute-start | bytes 1572872 | tf_op jit(solution)/shard_map/ppermute | solution.py:213
  108.5 8.9 %collective-permute-start.27 = (bf16[64,1024]{1,0:T(8,128)(2,1)S(1)}, bf16[64,1024]{1,0:T(8,128)(2,1)S(1)}, u32[]{:S(2)}, u32[]{:S(2)}) collective-permute-start(bf16[64,1024]{1,0:T(8,128)(2,1)S(1)} %bitcast.64), channel_id=1, source_target_pairs={{0,4},{2,6},{4,0},{6,2},{8,12},{10,14},{12,8},{14,10},{16,20},{18,... | collective-permute-start | bytes 393224 | tf_op jit(solution)/shard_map/ppermute | solution.py:210
  110.1 7.9 %collective-permute-start.28 = (bf16[64,1024]{1,0:T(8,128)(2,1)S(1)}, bf16[64,1024]{1,0:T(8,128)(2,1)S(1)}, u32[]{:S(2)}, u32[]{:S(2)}) collective-permute-start(bf16[64,1024]{1,0:T(8,128)(2,1)S(1)} %bitcast.63), channel_id=1, source_target_pairs={{0,6},{2,4},{4,2},{6,0},{8,14},{10,12},{12,10},{14,8},{16,22},{18,... | collective-permute-start | bytes 393224 | tf_op jit(solution)/shard_map/ppermute | solution.py:210
  110.6 9.9 %collective-permute-start.26 = (bf16[64,1024]{1,0:T(8,128)(2,1)S(1)}, bf16[64,1024]{1,0:T(8,128)(2,1)S(1)}, u32[]{:S(2)}, u32[]{:S(2)}) collective-permute-start(bf16[64,1024]{1,0:T(8,128)(2,1)S(1)} %bitcast.60), channel_id=1, source_target_pairs={{0,2},{2,0},{4,6},{6,4},{8,10},{10,8},{12,14},{14,12},{16,18},{18,... | collective-permute-start | bytes 393224 | tf_op jit(solution)/shard_map/ppermute | solution.py:210
  112.3 10.7 %collective-permute-start.32 = (bf16[64,1024]{1,0:T(8,128)(2,1)S(1)}, bf16[64,1024]{1,0:T(8,128)(2,1)S(1)}, u32[]{:S(2)}, u32[]{:S(2)}) collective-permute-start(bf16[64,1024]{1,0:T(8,128)(2,1)S(1)} %bitcast.65), channel_id=1, source_target_pairs={{0,4},{2,6},{4,0},{6,2},{8,12},{10,14},{12,8},{14,10},{16,20},{18,... | collective-permute-start | bytes 393224 | tf_op jit(solution)/shard_map/ppermute | solution.py:210
  114.1 9.5 %collective-permute-start.33 = (bf16[64,1024]{1,0:T(8,128)(2,1)S(1)}, bf16[64,1024]{1,0:T(8,128)(2,1)S(1)}, u32[]{:S(2)}, u32[]{:S(2)}) collective-permute-start(bf16[64,1024]{1,0:T(8,128)(2,1)S(1)} %bitcast.61), channel_id=1, source_target_pairs={{0,6},{2,4},{4,2},{6,0},{8,14},{10,12},{12,10},{14,8},{16,22},{18,... | collective-permute-start | bytes 393224 | tf_op jit(solution)/shard_map/ppermute | solution.py:210
  114.9 30.1 %copy-start.1 = (bf16[256,2048]{1,0:T(8,128)(2,1)S(1)}, bf16[256,2048]{1,0:T(8,128)(2,1)}, u32[]{:S(2)}) copy-start(bf16[256,2048]{1,0:T(8,128)(2,1)} %copy-done) | copy-start | bytes 3145732
  114.9 30.1 %copy-start.3 = (bf16[256,2048]{1,0:T(8,128)(2,1)S(1)}, bf16[256,2048]{1,0:T(8,128)(2,1)}, u32[]{:S(2)}) copy-start(bf16[256,2048]{1,0:T(8,128)(2,1)} %copy-done.2) | copy-start | bytes 3145732
  114.9 30.1 %copy-start.5 = (bf16[256,2048]{1,0:T(8,128)(2,1)S(1)}, bf16[256,2048]{1,0:T(8,128)(2,1)}, u32[]{:S(2)}) copy-start(bf16[256,2048]{1,0:T(8,128)(2,1)} %copy-done.4) | copy-start | bytes 3145732
  114.9 30.1 %copy-start.7 = (bf16[4,4,16,2048]{3,2,1,0:T(8,128)(2,1)S(1)}, bf16[4,4,16,2048]{3,2,1,0:T(8,128)(2,1)}, u32[]{:S(2)}) copy-start(bf16[4,4,16,2048]{3,2,1,0:T(8,128)(2,1)} %copy-done.6) | copy-start | bytes 3145732
  117.5 9.1 %collective-permute-start.31 = (bf16[64,1024]{1,0:T(8,128)(2,1)S(1)}, bf16[64,1024]{1,0:T(8,128)(2,1)S(1)}, u32[]{:S(2)}, u32[]{:S(2)}) collective-permute-start(bf16[64,1024]{1,0:T(8,128)(2,1)S(1)} %bitcast.57), channel_id=1, source_target_pairs={{0,2},{2,0},{4,6},{6,4},{8,10},{10,8},{12,14},{14,12},{16,18},{18,... | collective-permute-start | bytes 393224 | tf_op jit(solution)/shard_map/ppermute | solution.py:210
  118.0 10.7 %collective-permute-start.37 = (bf16[64,1024]{1,0:T(8,128)(2,1)S(1)}, bf16[64,1024]{1,0:T(8,128)(2,1)S(1)}, u32[]{:S(2)}, u32[]{:S(2)}) collective-permute-start(bf16[64,1024]{1,0:T(8,128)(2,1)S(1)} %bitcast.59), channel_id=1, source_target_pairs={{0,4},{2,6},{4,0},{6,2},{8,12},{10,14},{12,8},{14,10},{16,20},{18,... | collective-permute-start | bytes 393224 | tf_op jit(solution)/shard_map/ppermute | solution.py:210
  120.5 8.6 %collective-permute-start.38 = (bf16[64,1024]{1,0:T(8,128)(2,1)S(1)}, bf16[64,1024]{1,0:T(8,128)(2,1)S(1)}, u32[]{:S(2)}, u32[]{:S(2)}) collective-permute-start(bf16[64,1024]{1,0:T(8,128)(2,1)S(1)} %bitcast.58), channel_id=1, source_target_pairs={{0,6},{2,4},{4,2},{6,0},{8,14},{10,12},{12,10},{14,8},{16,22},{18,... | collective-permute-start | bytes 393224 | tf_op jit(solution)/shard_map/ppermute | solution.py:210
  123.1 8.6 %collective-permute-start.36 = (bf16[64,1024]{1,0:T(8,128)(2,1)S(1)}, bf16[64,1024]{1,0:T(8,128)(2,1)S(1)}, u32[]{:S(2)}, u32[]{:S(2)}) collective-permute-start(bf16[64,1024]{1,0:T(8,128)(2,1)S(1)} %bitcast.56), channel_id=1, source_target_pairs={{0,2},{2,0},{4,6},{6,4},{8,10},{10,8},{12,14},{14,12},{16,18},{18,... | collective-permute-start | bytes 393224 | tf_op jit(solution)/shard_map/ppermute | solution.py:210
  123.7 20.5 %collective-permute-start.23 = (bf16[64,1024]{1,0:T(8,128)(2,1)S(1)}, bf16[64,1024]{1,0:T(8,128)(2,1)S(1)}, u32[]{:S(2)}, u32[]{:S(2)}) collective-permute-start(bf16[64,1024]{1,0:T(8,128)(2,1)S(1)} %bitcast.62), channel_id=1, source_target_pairs={{0,4},{2,6},{4,0},{6,2},{8,12},{10,14},{12,8},{14,10},{16,20},{18,... | collective-permute-start | bytes 393224 | tf_op jit(solution)/shard_map/ppermute | solution.py:210
  126.5 30.8 %collective-permute-start.24 = (bf16[64,1024]{1,0:T(8,128)(2,1)S(1)}, bf16[64,1024]{1,0:T(8,128)(2,1)S(1)}, u32[]{:S(2)}, u32[]{:S(2)}) collective-permute-start(bf16[64,1024]{1,0:T(8,128)(2,1)S(1)} %bitcast.55), channel_id=1, source_target_pairs={{0,6},{2,4},{4,2},{6,0},{8,14},{10,12},{12,10},{14,8},{16,22},{18,... | collective-permute-start | bytes 393224 | tf_op jit(solution)/shard_map/ppermute | solution.py:210
  128.7 28.6 %collective-permute-start.22 = (bf16[64,1024]{1,0:T(8,128)(2,1)S(1)}, bf16[64,1024]{1,0:T(8,128)(2,1)S(1)}, u32[]{:S(2)}, u32[]{:S(2)}) collective-permute-start(bf16[64,1024]{1,0:T(8,128)(2,1)S(1)} %bitcast.54), channel_id=1, source_target_pairs={{0,2},{2,0},{4,6},{6,4},{8,10},{10,8},{12,14},{14,12},{16,18},{18,... | collective-permute-start | bytes 393224 | tf_op jit(solution)/shard_map/ppermute | solution.py:210
  129.1 28.2 %collective-permute-start.29 = (bf16[128,1024]{1,0:T(8,128)(2,1)S(1)}, bf16[128,1024]{1,0:T(8,128)(2,1)S(1)}, u32[]{:S(2)}, u32[]{:S(2)}) collective-permute-start(bf16[128,1024]{1,0:T(8,128)(2,1)S(1)} %combine.4), channel_id=1, source_target_pairs={{0,24},{2,26},{4,28},{6,30},{8,16},{10,18},{12,20},{14,22},{16,8},... | collective-permute-start | bytes 786440 | tf_op jit(solution)/shard_map/ppermute | solution.py:207
  131.7 26.5 %collective-permute-start.34 = (bf16[128,1024]{1,0:T(8,128)(2,1)S(1)}, bf16[128,1024]{1,0:T(8,128)(2,1)S(1)}, u32[]{:S(2)}, u32[]{:S(2)}) collective-permute-start(bf16[128,1024]{1,0:T(8,128)(2,1)S(1)} %combine.5), channel_id=1, source_target_pairs={{0,16},{2,18},{4,20},{6,22},{8,24},{10,26},{12,28},{14,30},{16,0},... | collective-permute-start | bytes 786440 | tf_op jit(solution)/shard_map/ppermute | solution.py:207
  144.2 14.0 %collective-permute-start.39 = (bf16[128,1024]{1,0:T(8,128)(2,1)S(1)}, bf16[128,1024]{1,0:T(8,128)(2,1)S(1)}, u32[]{:S(2)}, u32[]{:S(2)}) collective-permute-start(bf16[128,1024]{1,0:T(8,128)(2,1)S(1)} %combine.6), channel_id=1, source_target_pairs={{0,8},{2,10},{4,12},{6,14},{8,0},{10,2},{12,4},{14,6},{16,24},{18,... | collective-permute-start | bytes 786440 | tf_op jit(solution)/shard_map/ppermute | solution.py:207
  (6 other events, 9.0 us)

commit v2 on v1

v2 whole, which is shorter than its diff:
```python
import functools

import jax
import jax.numpy as jnp
from jax import lax
from jax.experimental import pallas as pl
from jax.experimental.pallas import tpu as pltpu
from jax.sharding import PartitionSpec as P

EXPERTS = 64
TOPK = 6
CAP = 16
META = 16
F32 = jnp.float32
BF16 = jnp.bfloat16
VMEM_LIMIT = 32 << 20
PAYLOAD_LIMIT = 62 << 20


def outer_extent(mesh):
    line = list(mesh.devices.reshape(mesh.devices.shape[0], -1)[:, 0])
    total = len(line)
    block = 1
    coords = [getattr(device, "coords", None) for device in line]
    if all(c is not None for c in coords):
        for axis in range(len(coords[0])):
            run = 1
            while run < total and coords[run][axis] == coords[0][axis]:
                run += 1
            if run < total:
                block = max(block, run)
    if block == 1:
        while block * block < total:
            block *= 2
    return total // block


def dot(a, b, dims):
    return lax.dot_general(a, b, (dims, ((), ())), preferred_element_type=F32)


def payload_body(where, routes, gates, arms, tokens, cotangent, bias, out, rows_in, bias_in, sems):
    rows, width = rows_in.shape[1:]
    at = pl.multiple_of(where[0] * width, width)
    copies = [
        pltpu.make_async_copy(tokens.at[:, pl.ds(at, width)], rows_in.at[0], sems.at[0]),
        pltpu.make_async_copy(cotangent.at[:, pl.ds(at, width)], rows_in.at[1], sems.at[1]),
        pltpu.make_async_copy(bias.at[:, pl.ds(at, width)], bias_in, sems.at[2]),
    ]
    for copy in copies:
        copy.start()
    ids = lax.broadcasted_iota(jnp.int32, (bias.shape[0], rows), 0)
    pick = (ids == arms[...]).astype(F32).astype(BF16)
    out[2 * rows :, :] = jnp.zeros((META, width), BF16)
    table = [ref[...].astype(F32) for ref in (routes, gates)]
    rest = jnp.zeros((META - 2 * TOPK, rows), F32)
    out[2 * rows :, 0:rows] = jnp.concatenate(table + [rest], axis=0).astype(BF16)
    for copy in copies:
        copy.wait()
    lift = dot(pick, bias_in[...], ((0,), (0,)))
    out[0:rows, :] = (rows_in[0].astype(F32) + lift).astype(BF16)
    out[rows : 2 * rows, :] = rows_in[1]


def choose_body(inner, experts_here, where, *refs):
    outs = refs[-(inner + 1) :]
    payloads = refs[: -(inner + 1)]
    table_out = outs[-1]
    rows = (payloads[0].shape[0] - META) // 2
    width = payloads[0].shape[1]
    if len(payloads) == 1:
        load = lambda a, b, c, d: payloads[0][a:b, c:d]
    else:
        flag = where[3] == 1
        load = lambda a, b, c, d: jnp.where(flag, payloads[0][a:b, c:d], payloads[1][a:b, c:d])
    meta = load(2 * rows, 2 * rows + META, 0, rows).astype(F32)
    count = inner * experts_here
    line = lax.broadcasted_iota(jnp.int32, (count, rows), 0)
    owner = jnp.bitwise_xor(lax.div(line, experts_here), where[2])
    ids = ((where[1] * inner + owner) * experts_here + lax.rem(line, experts_here)).astype(F32)
    named = jnp.zeros((count, rows), F32)
    weight = jnp.zeros((count, rows), F32)
    for k in range(TOPK):
        hit = (ids == meta[k : k + 1, :]).astype(F32)
        named = named + hit
        weight = weight + hit * meta[TOPK + k : TOPK + k + 1, :]
    earlier = (
        lax.broadcasted_iota(jnp.int32, (rows, rows), 0) < lax.broadcasted_iota(jnp.int32, (rows, rows), 1)
    ).astype(F32)
    rank = dot(named.astype(BF16), earlier.astype(BF16), ((1,), (0,)))
    rank = jnp.where(named > 0, rank, -1.0)
    slot = lax.broadcasted_iota(jnp.int32, (count, CAP, rows), 1).astype(F32)
    here = slot == rank[:, None, :]
    table = jnp.where(here, 1.0, 0.0).reshape(count * CAP, rows).astype(BF16)
    scale = jnp.where(here, (weight * (1.0 / 64.0))[:, None, :], 0.0).reshape(count * CAP, rows).astype(BF16)
    table_out[...] = table
    lifted = dot(table, load(0, rows, 0, width), ((1,), (0,))).astype(BF16)
    scaled = dot(scale, load(rows, 2 * rows, 0, width), ((1,), (0,))).astype(BF16)
    part = experts_here * CAP
    for m in range(inner):
        outs[m][:, 0:width] = lifted[m * part : (m + 1) * part]
        outs[m][:, width : 2 * width] = scaled[m * part : (m + 1) * part]


def gathered(refs):
    return jnp.concatenate([ref[...].reshape(-1, ref.shape[-1]) for ref in refs], axis=0)


def rows_body(rounds, pieces, where, *refs):
    n = rounds * pieces
    lifted, scaled = refs[:n], refs[n : 2 * n]
    up, down, hidden_out, pre_out = refs[2 * n : 2 * n + 4]
    outs = refs[2 * n + 4 :]
    width = outs[0].shape[-1]
    at = [pl.multiple_of(jnp.bitwise_xor(where[0], q) * width, width) for q in range(pieces)]

    def project(weight, xs):
        total = None
        for q in range(pieces):
            term = dot(weight[0, :, pl.ds(at[q], width)], gathered(xs[q * rounds : (q + 1) * rounds]), ((1,), (1,)))
            total = term if total is None else total + term
        return total

    preact = project(up, lifted)
    backprop = project(down, scaled)
    s = 1.0 / (1.0 + jnp.exp(-preact))
    hidden_out[0] = (preact * s).astype(BF16)
    pre = (backprop * s * (1.0 + preact * (1.0 - s))).astype(BF16)
    pre_out[0] = pre
    turned = pre.T
    for q in range(pieces):
        part = dot(turned, up[0, :, pl.ds(at[q], width)], ((1,), (0,))).astype(BF16)
        each = part.shape[0] // rounds
        for r in range(rounds):
            ref = outs[q * rounds + r]
            ref[...] = part[r * each : (r + 1) * each].reshape(ref.shape)


def grads_body(rounds, pieces, where, *refs):
    n = rounds * pieces
    hidden, pre, grad_up, grad_down, flag = refs[2 * n :]
    for unit, xs, grad in ((pre, refs[:n], grad_up), (hidden, refs[n : 2 * n], grad_down)):
        for q in range(pieces):
            width = xs[0].shape[-1]
            at = pl.multiple_of(jnp.bitwise_xor(where[0], q) * width, width)
            x = gathered(xs[q * rounds : (q + 1) * rounds])
            grad[0, :, pl.ds(at, width)] = dot(unit[0], x, ((1,), (0,))).astype(BF16)
    flag[...] = jnp.zeros(flag.shape, F32)


def combine_body(blocks, out_dtype, extra, *refs):
    table, out = refs[0], refs[-1]
    rows = jnp.concatenate([ref[...] for ref in refs[1 : 1 + blocks]], axis=0)
    total = dot(table[...], rows, ((0,), (0,)))
    for ref in refs[1 + blocks : 1 + blocks + extra]:
        total = total + ref[...].astype(F32)
    out[...] = total.astype(out_dtype)


def local(outer, tokens, arms, arm_bias, routes, gates, up_weight, down_weight, cotangent):
    count, features = tokens.shape
    here, hidden_width, _ = up_weight.shape
    inner = lax.axis_size("dp") // outer
    pieces = lax.axis_size("expert")
    width = features // pieces
    part = here * CAP
    plane = inner * part
    line = outer * inner * CAP
    dp_index = lax.axis_index("dp")
    core = lax.axis_index("expert")
    z_index = dp_index // inner
    edge = jnp.logical_or(z_index == 0, z_index == outer - 1)
    where = jnp.stack([core, z_index, dp_index % inner, edge.astype(jnp.int32)]).astype(jnp.int32)
    smem = pl.BlockSpec(memory_space=pltpu.SMEM)
    vmem = pl.BlockSpec(memory_space=pltpu.VMEM)
    params = pltpu.CompilerParams(vmem_limit_bytes=VMEM_LIMIT)
    shape = jax.ShapeDtypeStruct

    def cost(flops, moved):
        return pl.CostEstimate(flops=int(flops), bytes_accessed=int(moved), transcendentals=0)

    hbm = pl.BlockSpec(memory_space=pltpu.HBM)
    payload = pl.pallas_call(
        payload_body,
        in_specs=[smem, vmem, vmem, vmem, hbm, hbm, hbm],
        out_specs=vmem,
        out_shape=shape((2 * count + META, width), BF16),
        scratch_shapes=[
            pltpu.VMEM((2, count, width), BF16),
            pltpu.VMEM((arm_bias.shape[0], width), BF16),
            pltpu.SemaphoreType.DMA((3,)),
        ],
        compiler_params=pltpu.CompilerParams(vmem_limit_bytes=PAYLOAD_LIMIT),
        name="payload",
    )(where, routes.T, gates.T, arms.reshape(1, count), tokens, cotangent, arm_bias)

    def across(value, m):
        return lax.ppermute(value, "dp", [(i, i ^ (m * inner)) for i in range(outer * inner)])

    def within(value, m):
        return lax.ppermute(value, "dp", [(i, i ^ m) for i in range(outer * inner)])

    def core_swap(value, q):
        return lax.ppermute(value, "expert", [(i, i ^ q) for i in range(pieces)])

    def choose(candidates):
        outs = pl.pallas_call(
            functools.partial(choose_body, inner, here),
            in_specs=[smem] + [vmem] * len(candidates),
            out_specs=[vmem] * (inner + 1),
            out_shape=[shape((part, 2 * width), BF16)] * inner + [shape((plane, count), BF16)],
            compiler_params=params,
            cost_estimate=cost(4 * plane * count * width, 6 * plane * width),
            name="choose",
        )(where, *candidates)
        return outs[:-1], outs[-1]

    def after(value, *others):
        return lax.optimization_barrier((value, *others))[0]

    tables, owned = [], []

    def spread(blocks):
        return [blocks[0]] + [within(blocks[m], m) for m in range(1, inner)]

    def share(arrived):
        mine = jnp.concatenate(arrived, axis=0).reshape(inner, here, CAP, 2 * width)
        owned.append([mine] + [core_swap(mine, q) for q in range(1, pieces)])

    def pick(candidates):
        blocks, table = choose(candidates)
        tables.append(table)
        return blocks

    if outer == 4:
        middle = [(i, i ^ (3 * inner)) for i in range(inner, 3 * inner)]
        outward = [(i, i ^ inner) for i in range(inner, 3 * inner)]
        near = across(payload, 1)
        mid = lax.ppermute(payload, "dp", middle)
        first = spread(pick((payload,)))
        second = pick((near,))
        near, mid, first, second = lax.optimization_barrier((near, mid, first, second))
        share(first)
        far = lax.ppermute(near, "dp", middle)
        out_mid = lax.ppermute(mid, "dp", outward)
        second = spread(second)
        third = pick((out_mid, far))
        far, second, third = lax.optimization_barrier((far, second, third))
        share(second)
        out_far = lax.ppermute(far, "dp", outward)
        third = spread(third)
        fourth = pick((out_far, mid))
        third, fourth = lax.optimization_barrier((third, fourth))
        share(third)
        share(spread(fourth))
    else:
        for m in range(outer):
            share(spread(pick((across(payload, m) if m else payload,))))

    rows_in = [owned[r][q] for q in range(pieces) for r in range(outer)]
    n_in = len(rows_in)
    lifted_spec = [pl.BlockSpec((inner, 1, CAP, width), lambda e: (0, e, 0, 0))] * n_in
    scaled_spec = [pl.BlockSpec((inner, 1, CAP, width), lambda e: (0, e, 0, 1))] * n_in
    weight_spec = pl.BlockSpec((1, hidden_width, features), lambda e: (e, 0, 0))
    unit_spec = pl.BlockSpec((1, hidden_width, line), lambda e: (e, 0, 0))
    weight_bytes = 2 * here * hidden_width * features
    row_bytes = 2 * here * line * features
    flops = 2 * here * line * hidden_width * features
    unit_shape = (here, hidden_width, line)
    back = pl.pallas_call(
        functools.partial(rows_body, outer, pieces),
        grid=(here,),
        in_specs=[smem] + lifted_spec + scaled_spec + [weight_spec, weight_spec],
        out_specs=[unit_spec, unit_spec] + lifted_spec,
        out_shape=[shape(unit_shape, BF16)] * 2 + [shape((inner, here, CAP, width), BF16)] * n_in,
        compiler_params=params,
        cost_estimate=cost(3 * flops, 2 * weight_bytes + 3 * row_bytes),
        name="rows",
    )(where, *rows_in, *rows_in, up_weight, down_weight)
    hidden, pre, partial = back[0], back[1], back[2:]
    def weight_grads(ordered):
        return pl.pallas_call(
            functools.partial(grads_body, outer, pieces),
            grid=(here,),
            in_specs=[smem] + lifted_spec + scaled_spec + [unit_spec, unit_spec],
            out_specs=[weight_spec, weight_spec, pl.BlockSpec((8, 128), lambda e: (0, 0))],
            out_shape=[shape(up_weight.shape, BF16)] * 2 + [shape((8, 128), F32)],
            compiler_params=params,
            cost_estimate=cost(2 * flops, 2 * weight_bytes + 2 * row_bytes),
            name="weight_grads",
        )(ordered, *rows_in, *rows_in, hidden, pre)

    def combine(r, blocks, extra, dtype):
        return pl.pallas_call(
            functools.partial(combine_body, len(blocks), dtype, len(extra)),
            in_specs=[vmem] * (1 + len(blocks) + len(extra)),
            out_specs=vmem,
            out_shape=shape((count, width), dtype),
            compiler_params=params,
            cost_estimate=cost(2 * plane * count * width, 2 * plane * width),
            name="combine",
        )(tables[r], *blocks, *extra)

    sums = []
    swapped = [[core_swap(partial[q * outer + r], q) for q in range(1, pieces)] for r in range(outer)]
    ready = [None] * outer
    for r in range(outer):
        total = partial[r].astype(F32)
        for value in swapped[r]:
            total = total + value.astype(F32)
        ready[r] = total.astype(BF16).reshape(inner, part, width)
    grad_up, grad_down, flag = weight_grads(where)
    for r in reversed(range(outer)):
        blocks = [ready[r][0]] + [within(ready[r][m], m) for m in range(1, inner)]
        if r:
            blocks[-1], ready[r - 1] = lax.optimization_barrier((blocks[-1], ready[r - 1]))
            sums.append(across(combine(r, blocks, [], BF16), r))
        else:
            grad_tokens = combine(0, blocks, sums, F32)
    return (grad_tokens, grad_up, grad_down)


def solution(mesh):
    in_specs = (
        P("dp", None),
        P("dp"),
        P(),
        P("dp", None),
        P("dp", None),
        P("dp", "expert", None),
        P("dp", "expert", None),
        P("dp", None),
    )
    out_specs = (P("dp", "expert"), P("dp", "expert", None), P("dp", "expert", None))
    return jax.shard_map(
        functools.partial(local, outer_extent(mesh)), mesh=mesh, in_specs=in_specs, out_specs=out_specs, check_vma=False
    )
```

time: 160 us -> 137 us (0.86)
  Pallas kernels: 45.5 us -> 33.5 us
  starting transfers between devices: 55.6 us -> 47.9 us
  local copies, waits for them, and re-layouts: 4.06 us -> 1.85 us
    pallas_call x4 -> x3, Pallas kernels: 39.3 us -> 27.3 us  [the longest x1 14.7 us: local(): pl.pallas_call(functools.partial(rows_body, outer, pieces), grid=(here,),...]
    ppermute x1, waiting for transfers between devices: 0.59 us -> 8.89 us  [local(): out_far = lax.ppermute(far, 'dp', outward)]
    ppermute x4, waiting for transfers between devices: 12.8 us -> 6.61 us  [across(): lax.ppermute(value, 'dp', [(i, i ^ m * inner) for i in range(outer * inne...]
    ppermute x24, waiting for transfers between devices: 23.9 us -> 18.4 us  [within(): return lax.ppermute(value, 'dp', [(i, i ^ m) for i in range(outer * inner)])]
    ppermute x4, starting transfers between devices: 18.6 us -> 13.8 us  [across(): lax.ppermute(value, 'dp', [(i, i ^ m * inner) for i in range(outer * inne...]
    ppermute x1, waiting for transfers between devices: 9.56 us -> 13 us  [local(): out_mid = lax.ppermute(mid, 'dp', outward)]
    ppermute x24, starting transfers between devices: 31.4 us -> 28.8 us  [within(): return lax.ppermute(value, 'dp', [(i, i ^ m) for i in range(outer * inner)])]
    unnamed x28 -> x4, local copies, waits for them, and re-layouts: 3.81 us -> 1.71 us
  transfers between devices with their start and end apart: 40 -> 40, of which waited for: 15 -> 11; matrix products, arithmetic and copies ran while one was open for 1% -> 1% of each run, Pallas kernels for 11% -> 11%
where the time goes in v2:
time: 137 us; the launch traced here: 136 us
  waiting for transfers between devices  50.4 us (37%)
  starting transfers between devices  47.9 us (35%)
  Pallas kernels  33.5 us (24%)
  local copies, waits for them, and re-layouts  1.85 us (1%)
  other arithmetic  1.81 us (1%)
    ppermute x24, starting transfers between devices, within(): return lax.ppermute(value, 'dp', [(i, i ^ m) for i in range(outer * inner)])  28.8 us
    ppermute x24, waiting for transfers between devices, within(): return lax.ppermute(value, 'dp', [(i, i ^ m) for i in range(outer * inner)])  18.4 us
    pallas_call x1, Pallas kernels, local(): pl.pallas_call(functools.partial(rows_body, outer, pieces), grid=(here,),...  14.7 us
    ppermute x4, starting transfers between devices, across(): lax.ppermute(value, 'dp', [(i, i ^ m * inner) for i in range(outer * inne...  13.8 us
    ppermute x1, waiting for transfers between devices, local(): out_mid = lax.ppermute(mid, 'dp', outward)  13 us
    pallas_call x1, Pallas kernels, weight_grads(): pl.pallas_call(functools.partial(grads_body, outer, pieces), grid=(here,)...  9.72 us
    ppermute x1, waiting for transfers between devices, local(): out_far = lax.ppermute(far, 'dp', outward)  8.89 us
    ppermute x4, waiting for transfers between devices, across(): lax.ppermute(value, 'dp', [(i, i ^ m * inner) for i in range(outer * inne...  6.61 us
  transfers between devices with their start and end apart: 40, of which 11 were waited for; matrix products, arithmetic and copies ran while one was open for 1% of the time, Pallas kernels for 11%

profile of v2, /device:TPU:0, one launch (start us, length us, event | category | flops | bytes accessed | tf_op | source)
XLA Modules:
  0.0 136.4 jit_solution(10586032282194845944)
XLA Ops:
  0.7 0.6 pad_add_fusion.where
  1.3 2.9 %payload.1.refs_0_ = bf16[272,1024]{1,0:T(8,128)(2,1)} custom-call(s32[4]{0:T(128)} %pad_add_fusion.where, s32[6,128]{1,0:T(8,128)} %bitcast.69, s32[6,128]{1,0:T(8,128)} %bitcast.70, s32[1,128]{1,0:T(1,128)} %bitcast.71, bf16[128,2048]{1,0:T(8,128)(2,1)} %tokens.1, bf16[128,2048]{1,0:T(8,128)(2,1)} %cotangent.1, bf16[4,2048]{1,0:T(4,128)(2,1)} %bias.1), custom_call_target="tpu_custom_call" | custom-call | tf_op jit(solution)/shard_map/payload/pallas_call | solution.py:183
  4.2 3.1 %collective-permute-start = (bf16[272,1024]{1,0:T(8,128)(2,1)}, bf16[272,1024]{1,0:T(8,128)(2,1)S(1)}, u32[]{:S(2)}, u32[]{:S(2)}) collective-permute-start(bf16[272,1024]{1,0:T(8,128)(2,1)} %payload.1.refs_0_), channel_id=1, source_target_pairs={{0,8},{2,10},{4,12},{6,14},{8,0},{10,2},{12,4},{14,6},{16,24},{18,... | collective-permute-start | bytes 1671176 | tf_op jit(solution)/shard_map/ppermute | solution.py:198
  7.3 0.7 collective-permute-start.1
  8.0 1.0 copy-done
  9.1 0.7 copy-done.1
  9.7 1.1 choose.4
  10.8 1.6 %collective-permute-start.2 = (bf16[64,2048]{1,0:T(8,128)(2,1)S(1)}, bf16[64,2048]{1,0:T(8,128)(2,1)S(1)}, u32[]{:S(2)}, u32[]{:S(2)}) collective-permute-start(bf16[64,2048]{1,0:T(8,128)(2,1)S(1)} %get-tuple-element.70), channel_id=1, source_target_pairs={{0,2},{2,0},{4,6},{6,4},{8,10},{10,8},{12,14},{14,12},{16,18},{18,... | collective-permute-start | bytes 786440 | tf_op jit(solution)/shard_map/ppermute | solution.py:201
  12.4 1.5 %collective-permute-start.3 = (bf16[64,2048]{1,0:T(8,128)(2,1)S(1)}, bf16[64,2048]{1,0:T(8,128)(2,1)S(1)}, u32[]{:S(2)}, u32[]{:S(2)}) collective-permute-start(bf16[64,2048]{1,0:T(8,128)(2,1)S(1)} %get-tuple-element.71), channel_id=1, source_target_pairs={{0,4},{2,6},{4,0},{6,2},{8,12},{10,14},{12,8},{14,10},{16,20},{18,... | collective-permute-start | bytes 786440 | tf_op jit(solution)/shard_map/ppermute | solution.py:201
  14.4 5.8 %collective-permute-done.refs_0_ = bf16[272,1024]{1,0:T(8,128)(2,1)S(1)} collective-permute-done((bf16[272,1024]{1,0:T(8,128)(2,1)}, bf16[272,1024]{1,0:T(8,128)(2,1)S(1)}, u32[]{:S(2)}, u32[]{:S(2)}) %collective-permute-start) | collective-permute-done | bytes 557088 | tf_op jit(solution)/shard_map/ppermute | solution.py:198
  20.1 1.1 choose.5
  21.2 4.2 %collective-permute-done.3 = bf16[64,2048]{1,0:T(8,128)(2,1)S(1)} collective-permute-done((bf16[64,2048]{1,0:T(8,128)(2,1)S(1)}, bf16[64,2048]{1,0:T(8,128)(2,1)S(1)}, u32[]{:S(2)}, u32[]{:S(2)}) %collective-permute-start.3) | collective-permute-done | bytes 262176 | tf_op jit(solution)/shard_map/ppermute | solution.py:201
  25.5 0.7 collective-permute-start.5
  26.2 1.3 collective-permute-start.9
  27.5 1.3 collective-permute-start.6
  28.8 0.8 collective-permute-start.7
  29.6 1.4 %collective-permute-start.8 = (bf16[64,2048]{1,0:T(8,128)(2,1)S(1)}, bf16[64,2048]{1,0:T(8,128)(2,1)S(1)}, u32[]{:S(2)}, u32[]{:S(2)}) collective-permute-start(bf16[64,2048]{1,0:T(8,128)(2,1)S(1)} %get-tuple-element.85), channel_id=1, source_target_pairs={{0,6},{2,4},{4,2},{6,0},{8,14},{10,12},{12,10},{14,8},{16,22},{18,... | collective-permute-start | bytes 786440 | tf_op jit(solution)/shard_map/ppermute | solution.py:201
  31.0 13.0 %collective-permute-done.9.refs_0_ = bf16[272,1024]{1,0:T(8,128)(2,1)S(1)} collective-permute-done((bf16[272,1024]{1,0:T(8,128)(2,1)S(1)}, bf16[272,1024]{1,0:T(8,128)(2,1)S(1)}, u32[]{:S(2)}, u32[]{:S(2)}) %collective-permute-start.9) | collective-permute-done | bytes 557088 | tf_op jit(solution)/shard_map/ppermute | solution.py:245
  44.0 1.1 choose.6
  45.1 1.3 collective-permute-start.13
  46.4 1.5 %collective-permute-start.10 = (bf16[64,2048]{1,0:T(8,128)(2,1)S(1)}, bf16[64,2048]{1,0:T(8,128)(2,1)S(1)}, u32[]{:S(2)}, u32[]{:S(2)}) collective-permute-start(bf16[64,2048]{1,0:T(8,128)(2,1)S(1)} %get-tuple-element.96), channel_id=1, source_target_pairs={{0,2},{2,0},{4,6},{6,4},{8,10},{10,8},{12,14},{14,12},{16,18},{18,... | collective-permute-start | bytes 786440 | tf_op jit(solution)/shard_map/ppermute | solution.py:201
  48.5 1.5 %collective-permute-start.12 = (bf16[64,2048]{1,0:T(8,128)(2,1)S(1)}, bf16[64,2048]{1,0:T(8,128)(2,1)S(1)}, u32[]{:S(2)}, u32[]{:S(2)}) collective-permute-start(bf16[64,2048]{1,0:T(8,128)(2,1)S(1)} %get-tuple-element.98), channel_id=1, source_target_pairs={{0,6},{2,4},{4,2},{6,0},{8,14},{10,12},{12,10},{14,8},{16,22},{18,... | collective-permute-start | bytes 786440 | tf_op jit(solution)/shard_map/ppermute | solution.py:201
  50.2 8.9 %collective-permute-done.13.refs_0_ = bf16[272,1024]{1,0:T(8,128)(2,1)S(1)} collective-permute-done((bf16[272,1024]{1,0:T(8,128)(2,1)S(1)}, bf16[272,1024]{1,0:T(8,128)(2,1)S(1)}, u32[]{:S(2)}, u32[]{:S(2)}) %collective-permute-start.13) | collective-permute-done | bytes 557088 | tf_op jit(solution)/shard_map/ppermute | solution.py:250
  59.0 1.1 choose.7
  60.2 1.7 %collective-permute-start.14 = (bf16[64,2048]{1,0:T(8,128)(2,1)S(1)}, bf16[64,2048]{1,0:T(8,128)(2,1)S(1)}, u32[]{:S(2)}, u32[]{:S(2)}) collective-permute-start(bf16[64,2048]{1,0:T(8,128)(2,1)S(1)} %get-tuple-element.109), channel_id=1, source_target_pairs={{0,2},{2,0},{4,6},{6,4},{8,10},{10,8},{12,14},{14,12},{16,18},{18,... | collective-permute-start | bytes 786440 | tf_op jit(solution)/shard_map/ppermute | solution.py:201
  62.2 1.6 %collective-permute-start.16 = (bf16[64,2048]{1,0:T(8,128)(2,1)S(1)}, bf16[64,2048]{1,0:T(8,128)(2,1)S(1)}, u32[]{:S(2)}, u32[]{:S(2)}) collective-permute-start(bf16[64,2048]{1,0:T(8,128)(2,1)S(1)} %get-tuple-element.111), channel_id=1, source_target_pairs={{0,6},{2,4},{4,2},{6,0},{8,14},{10,12},{12,10},{14,8},{16,22},{18,... | collective-permute-start | bytes 786440 | tf_op jit(solution)/shard_map/ppermute | solution.py:201
  64.0 4.0 %collective-permute-done.14 = bf16[64,2048]{1,0:T(8,128)(2,1)S(1)} collective-permute-done((bf16[64,2048]{1,0:T(8,128)(2,1)S(1)}, bf16[64,2048]{1,0:T(8,128)(2,1)S(1)}, u32[]{:S(2)}, u32[]{:S(2)}) %collective-permute-start.14) | collective-permute-done | bytes 262176 | tf_op jit(solution)/shard_map/ppermute | solution.py:201
  68.0 4.2 %collective-permute-done.15 = bf16[64,2048]{1,0:T(8,128)(2,1)S(1)} collective-permute-done((bf16[64,2048]{1,0:T(8,128)(2,1)S(1)}, bf16[64,2048]{1,0:T(8,128)(2,1)S(1)}, u32[]{:S(2)}, u32[]{:S(2)}) %collective-permute-start.15) | collective-permute-done | bytes 262176 | tf_op jit(solution)/shard_map/ppermute | solution.py:201
  72.5 2.6 %collective-permute-done.20.refs_7_.refs_15_ = bf16[4,4,16,2048]{3,2,1,0:T(8,128)(2,1)S(1)} collective-permute-done((bf16[4,4,16,2048]{3,2,1,0:T(8,128)(2,1)S(1)}, bf16[4,4,16,2048]{3,2,1,0:T(8,128)(2,1)S(1)}, u32[]{:S(2)}, u32[]{:S(2)}) %collective-permute-start.20) | collective-permute-done | bytes 1048608 | tf_op jit(solution)/shard_map/ppermute | solution.py:204
  75.1 14.7 %rows.1 = (bf16[4,704,256]{2,1,0:T(8,128)(2,1)S(1)}, bf16[4,704,256]{2,1,0:T(8,128)(2,1)S(1)}, bf16[4,4,16,1024]{3,2,1,0:T(8,128)(2,1)S(1)}, bf16[4,4,16,1024]{3...) custom-call(s32[4]{0:T(128)S(1)} %copy-done.1, ...), custom_call_target="tpu_custom_call" | custom-call | flops 8858370048 | bytes 35651584 | tf_op jit(solution)/shard_map/rows/pallas_call | solution.py:270
  90.9 0.9 collective-permute-done.21
  92.4 1.4 %collective-permute-start.32 = (bf16[64,1024]{1,0:T(8,128)(2,1)S(1)}, bf16[64,1024]{1,0:T(8,128)(2,1)S(1)}, u32[]{:S(2)}, u32[]{:S(2)}) collective-permute-start(bf16[64,1024]{1,0:T(8,128)(2,1)S(1)} %bitcast.66), channel_id=1, source_target_pairs={{0,4},{2,6},{4,0},{6,2},{8,12},{10,14},{12,8},{14,10},{16,20},{18,... | collective-permute-start | bytes 393224 | tf_op jit(solution)/shard_map/ppermute | solution.py:201
  93.8 1.8 %collective-permute-start.22 = (bf16[64,1024]{1,0:T(8,128)(2,1)S(1)}, bf16[64,1024]{1,0:T(8,128)(2,1)S(1)}, u32[]{:S(2)}, u32[]{:S(2)}) collective-permute-start(bf16[64,1024]{1,0:T(8,128)(2,1)S(1)} %bitcast.68), channel_id=1, source_target_pairs={{0,6},{2,4},{4,2},{6,0},{8,14},{10,12},{12,10},{14,8},{16,22},{18,... | collective-permute-start | bytes 393224 | tf_op jit(solution)/shard_map/ppermute | solution.py:201
  95.8 4.5 %collective-permute-done.22.refs_4_ = bf16[64,1024]{1,0:T(8,128)(2,1)S(1)} collective-permute-done((bf16[64,1024]{1,0:T(8,128)(2,1)S(1)}, bf16[64,1024]{1,0:T(8,128)(2,1)S(1)}, u32[]{:S(2)}, u32[]{:S(2)}) %collective-permute-start.22) | collective-permute-done | bytes 131104 | tf_op jit(solution)/shard_map/ppermute | solution.py:201
  100.3 1.6 %collective-permute-start.24 = (bf16[64,1024]{1,0:T(8,128)(2,1)S(1)}, bf16[64,1024]{1,0:T(8,128)(2,1)S(1)}, u32[]{:S(2)}, u32[]{:S(2)}) collective-permute-start(bf16[64,1024]{1,0:T(8,128)(2,1)S(1)} %get-tuple-element.140), channel_id=1, source_target_pairs={{0,6},{2,4},{4,2},{6,0},{8,14},{10,12},{12,10},{14,8},{16,22},{18,... | collective-permute-start | bytes 393224 | tf_op jit(solution)/shard_map/ppermute | solution.py:201
  102.1 1.4 %collective-permute-start.35 = (bf16[64,1024]{1,0:T(8,128)(2,1)S(1)}, bf16[64,1024]{1,0:T(8,128)(2,1)S(1)}, u32[]{:S(2)}, u32[]{:S(2)}) collective-permute-start(bf16[64,1024]{1,0:T(8,128)(2,1)S(1)} %get-tuple-element.137), channel_id=1, source_target_pairs={{0,4},{2,6},{4,0},{6,2},{8,12},{10,14},{12,8},{14,10},{16,20},{18,... | collective-permute-start | bytes 393224 | tf_op jit(solution)/shard_map/ppermute | solution.py:201
  104.4 1.8 %collective-permute-start.33 = (bf16[128,1024]{1,0:T(8,128)(2,1)S(1)}, bf16[128,1024]{1,0:T(8,128)(2,1)S(1)}, u32[]{:S(2)}, u32[]{:S(2)}) collective-permute-start(bf16[128,1024]{1,0:T(8,128)(2,1)S(1)} %combine.4), channel_id=1, source_target_pairs={{0,24},{2,26},{4,28},{6,30},{8,16},{10,18},{12,20},{14,22},{16,8},... | collective-permute-start | bytes 786440 | tf_op jit(solution)/shard_map/ppermute | solution.py:198
  106.2 1.4 %collective-permute-done.24.refs_4_ = bf16[64,1024]{1,0:T(8,128)(2,1)S(1)} collective-permute-done((bf16[64,1024]{1,0:T(8,128)(2,1)S(1)}, bf16[64,1024]{1,0:T(8,128)(2,1)S(1)}, u32[]{:S(2)}, u32[]{:S(2)}) %collective-permute-start.24) | collective-permute-done | bytes 131104 | tf_op jit(solution)/shard_map/ppermute | solution.py:201
  107.6 1.7 %collective-permute-start.26 = (bf16[64,1024]{1,0:T(8,128)(2,1)S(1)}, bf16[64,1024]{1,0:T(8,128)(2,1)S(1)}, u32[]{:S(2)}, u32[]{:S(2)}) collective-permute-start(bf16[64,1024]{1,0:T(8,128)(2,1)S(1)} %get-tuple-element.136), channel_id=1, source_target_pairs={{0,6},{2,4},{4,2},{6,0},{8,14},{10,12},{12,10},{14,8},{16,22},{18,... | collective-permute-start | bytes 393224 | tf_op jit(solution)/shard_map/ppermute | solution.py:201
  109.5 1.1 collective-permute-start.38
  110.7 0.8 collective-permute-start.37
  111.7 4.0 %collective-permute-start.36 = (bf16[128,1024]{1,0:T(8,128)(2,1)S(1)}, bf16[128,1024]{1,0:T(8,128)(2,1)S(1)}, u32[]{:S(2)}, u32[]{:S(2)}) collective-permute-start(bf16[128,1024]{1,0:T(8,128)(2,1)S(1)} %combine.5), channel_id=1, source_target_pairs={{0,16},{2,18},{4,20},{6,22},{8,24},{10,26},{12,28},{14,30},{16,0},... | collective-permute-start | bytes 786440 | tf_op jit(solution)/shard_map/ppermute | solution.py:198
  115.7 2.2 %collective-permute-start.30 = (bf16[64,1024]{1,0:T(8,128)(2,1)S(1)}, bf16[64,1024]{1,0:T(8,128)(2,1)S(1)}, u32[]{:S(2)}, u32[]{:S(2)}) collective-permute-start(bf16[64,1024]{1,0:T(8,128)(2,1)S(1)} %get-tuple-element.145), channel_id=1, source_target_pairs={{0,6},{2,4},{4,2},{6,0},{8,14},{10,12},{12,10},{14,8},{16,22},{18,... | collective-permute-start | bytes 393224 | tf_op jit(solution)/shard_map/ppermute | solution.py:201
  118.3 1.2 collective-permute-start.28
  119.8 5.0 %collective-permute-start.39 = (bf16[128,1024]{1,0:T(8,128)(2,1)S(1)}, bf16[128,1024]{1,0:T(8,128)(2,1)S(1)}, u32[]{:S(2)}, u32[]{:S(2)}) collective-permute-start(bf16[128,1024]{1,0:T(8,128)(2,1)S(1)} %combine.6), channel_id=1, source_target_pairs={{0,8},{2,10},{4,12},{6,14},{8,0},{10,2},{12,4},{14,6},{16,24},{18,... | collective-permute-start | bytes 786440 | tf_op jit(solution)/shard_map/ppermute | solution.py:198
  124.8 9.7 %weight_grads.1 = (bf16[4,704,2048]{2,1,0:T(8,128)(2,1)}, bf16[4,704,2048]{2,1,0:T(8,128)(2,1)}, f32[8,128]{1,0:T(8,128)}) custom-call(s32[4]{0:T(128)S(1)} %copy-done.1, bf16[4,4,16,2048]{3,2,1,0:T(8,128)(2,1)S(1)} %bitcast.45, bf16[4,4,16,2048]{3,2,1,0:T(8,128)(2,1)S(1)} %bitcast.50, bf16[4,4,16,2048]{3,2,1,0:T(8,128)(2,1)S(1)} %bitcast.55, ...), custom_call_target="tpu_custom_call" | custom-call | flops 5905580032 | bytes 31457280 | tf_op jit(solution)/shard_map/weight_grads/pallas_call | solution.py:282
  134.5 0.8 collective-permute-done.39.refs_7_
  135.4 1.1 combine.7
  (60 shorter events, 6.0 us)
Async XLA Ops:
  4.2 15.9 %collective-permute-start = (bf16[272,1024]{1,0:T(8,128)(2,1)}, bf16[272,1024]{1,0:T(8,128)(2,1)S(1)}, u32[]{:S(2)}, u32[]{:S(2)}) collective-permute-start(bf16[272,1024]{1,0:T(8,128)(2,1)} %payload.1.refs_0_), channel_id=1, source_target_pairs={{0,8},{2,10},{4,12},{6,14},{8,0},{10,2},{12,4},{14,6},{16,24},{18,... | collective-permute-start | bytes 1671176 | tf_op jit(solution)/shard_map/ppermute | solution.py:198
  7.3 18.2 %collective-permute-start.1 = (bf16[272,1024]{1,0:T(8,128)(2,1)}, bf16[272,1024]{1,0:T(8,128)(2,1)S(1)}, u32[]{:S(2)}, u32[]{:S(2)}) collective-permute-start(bf16[272,1024]{1,0:T(8,128)(2,1)} %payload.1.refs_0_), channel_id=1, source_target_pairs={{8,16},{10,18},{12,20},{14,22},{16,8},{18,10},{20,12},{22,14},{9,1... | collective-permute-start | bytes 1671176 | tf_op jit(solution)/shard_map/ppermute | solution.py:239
  8.0 1.1 copy-start
  9.1 0.7 copy-start.1
  10.8 10.4 %collective-permute-start.2 = (bf16[64,2048]{1,0:T(8,128)(2,1)S(1)}, bf16[64,2048]{1,0:T(8,128)(2,1)S(1)}, u32[]{:S(2)}, u32[]{:S(2)}) collective-permute-start(bf16[64,2048]{1,0:T(8,128)(2,1)S(1)} %get-tuple-element.70), channel_id=1, source_target_pairs={{0,2},{2,0},{4,6},{6,4},{8,10},{10,8},{12,14},{14,12},{16,18},{18,... | collective-permute-start | bytes 786440 | tf_op jit(solution)/shard_map/ppermute | solution.py:201
  12.4 13.1 %collective-permute-start.3 = (bf16[64,2048]{1,0:T(8,128)(2,1)S(1)}, bf16[64,2048]{1,0:T(8,128)(2,1)S(1)}, u32[]{:S(2)}, u32[]{:S(2)}) collective-permute-start(bf16[64,2048]{1,0:T(8,128)(2,1)S(1)} %get-tuple-element.71), channel_id=1, source_target_pairs={{0,4},{2,6},{4,0},{6,2},{8,12},{10,14},{12,8},{14,10},{16,20},{18,... | collective-permute-start | bytes 786440 | tf_op jit(solution)/shard_map/ppermute | solution.py:201
  13.9 11.6 %collective-permute-start.4 = (bf16[64,2048]{1,0:T(8,128)(2,1)S(1)}, bf16[64,2048]{1,0:T(8,128)(2,1)S(1)}, u32[]{:S(2)}, u32[]{:S(2)}) collective-permute-start(bf16[64,2048]{1,0:T(8,128)(2,1)S(1)} %get-tuple-element.72), channel_id=1, source_target_pairs={{0,6},{2,4},{4,2},{6,0},{8,14},{10,12},{12,10},{14,8},{16,22},{18,... | collective-permute-start | bytes 786440 | tf_op jit(solution)/shard_map/ppermute | solution.py:201
  25.5 5.6 %collective-permute-start.5 = (bf16[272,1024]{1,0:T(8,128)(2,1)S(1)}, bf16[272,1024]{1,0:T(8,128)(2,1)S(1)}, u32[]{:S(2)}, u32[]{:S(2)}) collective-permute-start(bf16[272,1024]{1,0:T(8,128)(2,1)S(1)} %collective-permute-done.refs_0_), channel_id=1, source_target_pairs={{8,16},{10,18},{12,20},{14,22},{16,8},{18,10},{20,12},{22,14},{9,1... | collective-permute-start | bytes 1671176 | tf_op jit(solution)/shard_map/ppermute | solution.py:244
  26.2 17.8 %collective-permute-start.9 = (bf16[272,1024]{1,0:T(8,128)(2,1)S(1)}, bf16[272,1024]{1,0:T(8,128)(2,1)S(1)}, u32[]{:S(2)}, u32[]{:S(2)}) collective-permute-start(bf16[272,1024]{1,0:T(8,128)(2,1)S(1)} %collective-permute-done.1.refs_1_), channel_id=1, source_target_pairs={{8,0},{10,2},{12,4},{14,6},{16,24},{18,26},{20,28},{22,30},{9,1},{... | collective-permute-start | bytes 1671176 | tf_op jit(solution)/shard_map/ppermute | solution.py:245
  27.5 17.6 %collective-permute-start.6 = (bf16[64,2048]{1,0:T(8,128)(2,1)S(1)}, bf16[64,2048]{1,0:T(8,128)(2,1)S(1)}, u32[]{:S(2)}, u32[]{:S(2)}) collective-permute-start(bf16[64,2048]{1,0:T(8,128)(2,1)S(1)} %get-tuple-element.83), channel_id=1, source_target_pairs={{0,2},{2,0},{4,6},{6,4},{8,10},{10,8},{12,14},{14,12},{16,18},{18,... | collective-permute-start | bytes 786440 | tf_op jit(solution)/shard_map/ppermute | solution.py:201
  28.8 16.3 %collective-permute-start.7 = (bf16[64,2048]{1,0:T(8,128)(2,1)S(1)}, bf16[64,2048]{1,0:T(8,128)(2,1)S(1)}, u32[]{:S(2)}, u32[]{:S(2)}) collective-permute-start(bf16[64,2048]{1,0:T(8,128)(2,1)S(1)} %get-tuple-element.84), channel_id=1, source_target_pairs={{0,4},{2,6},{4,0},{6,2},{8,12},{10,14},{12,8},{14,10},{16,20},{18,... | collective-permute-start | bytes 786440 | tf_op jit(solution)/shard_map/ppermute | solution.py:201
  29.6 15.5 %collective-permute-start.8 = (bf16[64,2048]{1,0:T(8,128)(2,1)S(1)}, bf16[64,2048]{1,0:T(8,128)(2,1)S(1)}, u32[]{:S(2)}, u32[]{:S(2)}) collective-permute-start(bf16[64,2048]{1,0:T(8,128)(2,1)S(1)} %get-tuple-element.85), channel_id=1, source_target_pairs={{0,6},{2,4},{4,2},{6,0},{8,14},{10,12},{12,10},{14,8},{16,22},{18,... | collective-permute-start | bytes 786440 | tf_op jit(solution)/shard_map/ppermute | solution.py:201
  45.1 13.9 %collective-permute-start.13 = (bf16[272,1024]{1,0:T(8,128)(2,1)S(1)}, bf16[272,1024]{1,0:T(8,128)(2,1)S(1)}, u32[]{:S(2)}, u32[]{:S(2)}) collective-permute-start(bf16[272,1024]{1,0:T(8,128)(2,1)S(1)} %collective-permute-done.5.refs_1_), channel_id=1, source_target_pairs={{8,0},{10,2},{12,4},{14,6},{16,24},{18,26},{20,28},{22,30},{9,1},{... | collective-permute-start | bytes 1671176 | tf_op jit(solution)/shard_map/ppermute | solution.py:250
  46.4 13.7 %collective-permute-start.10 = (bf16[64,2048]{1,0:T(8,128)(2,1)S(1)}, bf16[64,2048]{1,0:T(8,128)(2,1)S(1)}, u32[]{:S(2)}, u32[]{:S(2)}) collective-permute-start(bf16[64,2048]{1,0:T(8,128)(2,1)S(1)} %get-tuple-element.96), channel_id=1, source_target_pairs={{0,2},{2,0},{4,6},{6,4},{8,10},{10,8},{12,14},{14,12},{16,18},{18,... | collective-permute-start | bytes 786440 | tf_op jit(solution)/shard_map/ppermute | solution.py:201
  47.9 12.2 %collective-permute-start.11 = (bf16[64,2048]{1,0:T(8,128)(2,1)S(1)}, bf16[64,2048]{1,0:T(8,128)(2,1)S(1)}, u32[]{:S(2)}, u32[]{:S(2)}) collective-permute-start(bf16[64,2048]{1,0:T(8,128)(2,1)S(1)} %get-tuple-element.97), channel_id=1, source_target_pairs={{0,4},{2,6},{4,0},{6,2},{8,12},{10,14},{12,8},{14,10},{16,20},{18,... | collective-permute-start | bytes 786440 | tf_op jit(solution)/shard_map/ppermute | solution.py:201
  48.5 11.7 %collective-permute-start.12 = (bf16[64,2048]{1,0:T(8,128)(2,1)S(1)}, bf16[64,2048]{1,0:T(8,128)(2,1)S(1)}, u32[]{:S(2)}, u32[]{:S(2)}) collective-permute-start(bf16[64,2048]{1,0:T(8,128)(2,1)S(1)} %get-tuple-element.98), channel_id=1, source_target_pairs={{0,6},{2,4},{4,2},{6,0},{8,14},{10,12},{12,10},{14,8},{16,22},{18,... | collective-permute-start | bytes 786440 | tf_op jit(solution)/shard_map/ppermute | solution.py:201
  50.1 22.4 %collective-permute-start.17 = (bf16[4,4,16,2048]{3,2,1,0:T(8,128)(2,1)S(1)}, bf16[4,4,16,2048]{3,2,1,0:T(8,128)(2,1)S(1)}, u32[]{:S(2)}, u32[]{:S(2)}) collective-permute-start(bf16[4,4,16,2048]{3,2,1,0:T(8,128)(2,1)S(1)} %bitcast.42), channel_id=1, source_target_pairs={{0,1},{1,0},{2,3},{3,2},{4,5},{5,4},{6,7},{7,6},{8,9},{9,8},{10,11... | collective-permute-start | bytes 3145736 | tf_op jit(solution)/shard_map/ppermute | solution.py:204
  60.2 7.8 %collective-permute-start.14 = (bf16[64,2048]{1,0:T(8,128)(2,1)S(1)}, bf16[64,2048]{1,0:T(8,128)(2,1)S(1)}, u32[]{:S(2)}, u32[]{:S(2)}) collective-permute-start(bf16[64,2048]{1,0:T(8,128)(2,1)S(1)} %get-tuple-element.109), channel_id=1, source_target_pairs={{0,2},{2,0},{4,6},{6,4},{8,10},{10,8},{12,14},{14,12},{16,18},{18,... | collective-permute-start | bytes 786440 | tf_op jit(solution)/shard_map/ppermute | solution.py:201
  61.9 10.4 %collective-permute-start.15 = (bf16[64,2048]{1,0:T(8,128)(2,1)S(1)}, bf16[64,2048]{1,0:T(8,128)(2,1)S(1)}, u32[]{:S(2)}, u32[]{:S(2)}) collective-permute-start(bf16[64,2048]{1,0:T(8,128)(2,1)S(1)} %get-tuple-element.110), channel_id=1, source_target_pairs={{0,4},{2,6},{4,0},{6,2},{8,12},{10,14},{12,8},{14,10},{16,20},{18,... | collective-permute-start | bytes 786440 | tf_op jit(solution)/shard_map/ppermute | solution.py:201
  62.2 10.1 %collective-permute-start.16 = (bf16[64,2048]{1,0:T(8,128)(2,1)S(1)}, bf16[64,2048]{1,0:T(8,128)(2,1)S(1)}, u32[]{:S(2)}, u32[]{:S(2)}) collective-permute-start(bf16[64,2048]{1,0:T(8,128)(2,1)S(1)} %get-tuple-element.111), channel_id=1, source_target_pairs={{0,6},{2,4},{4,2},{6,0},{8,14},{10,12},{12,10},{14,8},{16,22},{18,... | collective-permute-start | bytes 786440 | tf_op jit(solution)/shard_map/ppermute | solution.py:201
  63.8 8.6 %collective-permute-start.18 = (bf16[4,4,16,2048]{3,2,1,0:T(8,128)(2,1)S(1)}, bf16[4,4,16,2048]{3,2,1,0:T(8,128)(2,1)S(1)}, u32[]{:S(2)}, u32[]{:S(2)}) collective-permute-start(bf16[4,4,16,2048]{3,2,1,0:T(8,128)(2,1)S(1)} %bitcast.47), channel_id=1, source_target_pairs={{0,1},{1,0},{2,3},{3,2},{4,5},{5,4},{6,7},{7,6},{8,9},{9,8},{10,11... | collective-permute-start | bytes 3145736 | tf_op jit(solution)/shard_map/ppermute | solution.py:204
  68.0 4.4 %collective-permute-start.19 = (bf16[4,4,16,2048]{3,2,1,0:T(8,128)(2,1)S(1)}, bf16[4,4,16,2048]{3,2,1,0:T(8,128)(2,1)S(1)}, u32[]{:S(2)}, u32[]{:S(2)}) collective-permute-start(bf16[4,4,16,2048]{3,2,1,0:T(8,128)(2,1)S(1)} %bitcast.52), channel_id=1, source_target_pairs={{0,1},{1,0},{2,3},{3,2},{4,5},{5,4},{6,7},{7,6},{8,9},{9,8},{10,11... | collective-permute-start | bytes 3145736 | tf_op jit(solution)/shard_map/ppermute | solution.py:204
  72.4 2.7 %collective-permute-start.20 = (bf16[4,4,16,2048]{3,2,1,0:T(8,128)(2,1)S(1)}, bf16[4,4,16,2048]{3,2,1,0:T(8,128)(2,1)S(1)}, u32[]{:S(2)}, u32[]{:S(2)}) collective-permute-start(bf16[4,4,16,2048]{3,2,1,0:T(8,128)(2,1)S(1)} %bitcast.57), channel_id=1, source_target_pairs={{0,1},{1,0},{2,3},{3,2},{4,5},{5,4},{6,7},{7,6},{8,9},{9,8},{10,11... | collective-permute-start | bytes 3145736 | tf_op jit(solution)/shard_map/ppermute | solution.py:204
  89.8 2.0 %collective-permute-start.21 = (bf16[4,4,16,1024]{3,2,1,0:T(8,128)(2,1)S(1)}, bf16[4,4,16,1024]{3,2,1,0:T(8,128)(2,1)S(1)}, u32[]{:S(2)}, u32[]{:S(2)}) collective-permute-start(bf16[4,4,16,1024]{3,2,1,0:T(8,128)(2,1)S(1)} %get-tuple-element.113), channel_id=1, source_target_pairs={{0,1},{1,0},{2,3},{3,2},{4,5},{5,4},{6,7},{7,6},{8,9},{9,8},{10,11... | collective-permute-start | bytes 1572872 | tf_op jit(solution)/shard_map/ppermute | solution.py:204
  90.0 3.8 %collective-permute-start.23 = (bf16[4,4,16,1024]{3,2,1,0:T(8,128)(2,1)S(1)}, bf16[4,4,16,1024]{3,2,1,0:T(8,128)(2,1)S(1)}, u32[]{:S(2)}, u32[]{:S(2)}) collective-permute-start(bf16[4,4,16,1024]{3,2,1,0:T(8,128)(2,1)S(1)} %get-tuple-element.115), channel_id=1, source_target_pairs={{0,1},{1,0},{2,3},{3,2},{4,5},{5,4},{6,7},{7,6},{8,9},{9,8},{10,11... | collective-permute-start | bytes 1572872 | tf_op jit(solution)/shard_map/ppermute | solution.py:204
  90.4 11.5 %collective-permute-start.25 = (bf16[4,4,16,1024]{3,2,1,0:T(8,128)(2,1)S(1)}, bf16[4,4,16,1024]{3,2,1,0:T(8,128)(2,1)S(1)}, u32[]{:S(2)}, u32[]{:S(2)}) collective-permute-start(bf16[4,4,16,1024]{3,2,1,0:T(8,128)(2,1)S(1)} %get-tuple-element.118), channel_id=1, source_target_pairs={{0,1},{1,0},{2,3},{3,2},{4,5},{5,4},{6,7},{7,6},{8,9},{9,8},{10,11... | collective-permute-start | bytes 1572872 | tf_op jit(solution)/shard_map/ppermute | solution.py:204
  90.5 18.9 %collective-permute-start.27 = (bf16[4,4,16,1024]{3,2,1,0:T(8,128)(2,1)S(1)}, bf16[4,4,16,1024]{3,2,1,0:T(8,128)(2,1)S(1)}, u32[]{:S(2)}, u32[]{:S(2)}) collective-permute-start(bf16[4,4,16,1024]{3,2,1,0:T(8,128)(2,1)S(1)} %get-tuple-element.121), channel_id=1, source_target_pairs={{0,1},{1,0},{2,3},{3,2},{4,5},{5,4},{6,7},{7,6},{8,9},{9,8},{10,11... | collective-permute-start | bytes 1572872 | tf_op jit(solution)/shard_map/ppermute | solution.py:204
  92.0 11.5 %collective-permute-start.31 = (bf16[64,1024]{1,0:T(8,128)(2,1)S(1)}, bf16[64,1024]{1,0:T(8,128)(2,1)S(1)}, u32[]{:S(2)}, u32[]{:S(2)}) collective-permute-start(bf16[64,1024]{1,0:T(8,128)(2,1)S(1)} %bitcast.67), channel_id=1, source_target_pairs={{0,2},{2,0},{4,6},{6,4},{8,10},{10,8},{12,14},{14,12},{16,18},{18,... | collective-permute-start | bytes 393224 | tf_op jit(solution)/shard_map/ppermute | solution.py:201
  92.4 11.7 %collective-permute-start.32 = (bf16[64,1024]{1,0:T(8,128)(2,1)S(1)}, bf16[64,1024]{1,0:T(8,128)(2,1)S(1)}, u32[]{:S(2)}, u32[]{:S(2)}) collective-permute-start(bf16[64,1024]{1,0:T(8,128)(2,1)S(1)} %bitcast.66), channel_id=1, source_target_pairs={{0,4},{2,6},{4,0},{6,2},{8,12},{10,14},{12,8},{14,10},{16,20},{18,... | collective-permute-start | bytes 393224 | tf_op jit(solution)/shard_map/ppermute | solution.py:201
  93.8 6.4 %collective-permute-start.22 = (bf16[64,1024]{1,0:T(8,128)(2,1)S(1)}, bf16[64,1024]{1,0:T(8,128)(2,1)S(1)}, u32[]{:S(2)}, u32[]{:S(2)}) collective-permute-start(bf16[64,1024]{1,0:T(8,128)(2,1)S(1)} %bitcast.68), channel_id=1, source_target_pairs={{0,6},{2,4},{4,2},{6,0},{8,14},{10,12},{12,10},{14,8},{16,22},{18,... | collective-permute-start | bytes 393224 | tf_op jit(solution)/shard_map/ppermute | solution.py:201
  100.3 7.3 %collective-permute-start.24 = (bf16[64,1024]{1,0:T(8,128)(2,1)S(1)}, bf16[64,1024]{1,0:T(8,128)(2,1)S(1)}, u32[]{:S(2)}, u32[]{:S(2)}) collective-permute-start(bf16[64,1024]{1,0:T(8,128)(2,1)S(1)} %get-tuple-element.140), channel_id=1, source_target_pairs={{0,6},{2,4},{4,2},{6,0},{8,14},{10,12},{12,10},{14,8},{16,22},{18,... | collective-permute-start | bytes 393224 | tf_op jit(solution)/shard_map/ppermute | solution.py:201
  102.1 8.6 %collective-permute-start.35 = (bf16[64,1024]{1,0:T(8,128)(2,1)S(1)}, bf16[64,1024]{1,0:T(8,128)(2,1)S(1)}, u32[]{:S(2)}, u32[]{:S(2)}) collective-permute-start(bf16[64,1024]{1,0:T(8,128)(2,1)S(1)} %get-tuple-element.137), channel_id=1, source_target_pairs={{0,4},{2,6},{4,0},{6,2},{8,12},{10,14},{12,8},{14,10},{16,20},{18,... | collective-permute-start | bytes 393224 | tf_op jit(solution)/shard_map/ppermute | solution.py:201
  103.5 7.9 %collective-permute-start.34 = (bf16[64,1024]{1,0:T(8,128)(2,1)S(1)}, bf16[64,1024]{1,0:T(8,128)(2,1)S(1)}, u32[]{:S(2)}, u32[]{:S(2)}) collective-permute-start(bf16[64,1024]{1,0:T(8,128)(2,1)S(1)} %get-tuple-element.138), channel_id=1, source_target_pairs={{0,2},{2,0},{4,6},{6,4},{8,10},{10,8},{12,14},{14,12},{16,18},{18,... | collective-permute-start | bytes 393224 | tf_op jit(solution)/shard_map/ppermute | solution.py:201
  104.4 15.4 %collective-permute-start.33 = (bf16[128,1024]{1,0:T(8,128)(2,1)S(1)}, bf16[128,1024]{1,0:T(8,128)(2,1)S(1)}, u32[]{:S(2)}, u32[]{:S(2)}) collective-permute-start(bf16[128,1024]{1,0:T(8,128)(2,1)S(1)} %combine.4), channel_id=1, source_target_pairs={{0,24},{2,26},{4,28},{6,30},{8,16},{10,18},{12,20},{14,22},{16,8},... | collective-permute-start | bytes 786440 | tf_op jit(solution)/shard_map/ppermute | solution.py:198
  107.6 8.1 %collective-permute-start.26 = (bf16[64,1024]{1,0:T(8,128)(2,1)S(1)}, bf16[64,1024]{1,0:T(8,128)(2,1)S(1)}, u32[]{:S(2)}, u32[]{:S(2)}) collective-permute-start(bf16[64,1024]{1,0:T(8,128)(2,1)S(1)} %get-tuple-element.136), channel_id=1, source_target_pairs={{0,6},{2,4},{4,2},{6,0},{8,14},{10,12},{12,10},{14,8},{16,22},{18,... | collective-permute-start | bytes 393224 | tf_op jit(solution)/shard_map/ppermute | solution.py:201
  109.5 8.4 %collective-permute-start.38 = (bf16[64,1024]{1,0:T(8,128)(2,1)S(1)}, bf16[64,1024]{1,0:T(8,128)(2,1)S(1)}, u32[]{:S(2)}, u32[]{:S(2)}) collective-permute-start(bf16[64,1024]{1,0:T(8,128)(2,1)S(1)} %get-tuple-element.133), channel_id=1, source_target_pairs={{0,4},{2,6},{4,0},{6,2},{8,12},{10,14},{12,8},{14,10},{16,20},{18,... | collective-permute-start | bytes 393224 | tf_op jit(solution)/shard_map/ppermute | solution.py:201
  110.7 7.6 %collective-permute-start.37 = (bf16[64,1024]{1,0:T(8,128)(2,1)S(1)}, bf16[64,1024]{1,0:T(8,128)(2,1)S(1)}, u32[]{:S(2)}, u32[]{:S(2)}) collective-permute-start(bf16[64,1024]{1,0:T(8,128)(2,1)S(1)} %get-tuple-element.134), channel_id=1, source_target_pairs={{0,2},{2,0},{4,6},{6,4},{8,10},{10,8},{12,14},{14,12},{16,18},{18,... | collective-permute-start | bytes 393224 | tf_op jit(solution)/shard_map/ppermute | solution.py:201
  111.7 22.8 %collective-permute-start.36 = (bf16[128,1024]{1,0:T(8,128)(2,1)S(1)}, bf16[128,1024]{1,0:T(8,128)(2,1)S(1)}, u32[]{:S(2)}, u32[]{:S(2)}) collective-permute-start(bf16[128,1024]{1,0:T(8,128)(2,1)S(1)} %combine.5), channel_id=1, source_target_pairs={{0,16},{2,18},{4,20},{6,22},{8,24},{10,26},{12,28},{14,30},{16,0},... | collective-permute-start | bytes 786440 | tf_op jit(solution)/shard_map/ppermute | solution.py:198
  115.7 18.8 %collective-permute-start.30 = (bf16[64,1024]{1,0:T(8,128)(2,1)S(1)}, bf16[64,1024]{1,0:T(8,128)(2,1)S(1)}, u32[]{:S(2)}, u32[]{:S(2)}) collective-permute-start(bf16[64,1024]{1,0:T(8,128)(2,1)S(1)} %get-tuple-element.145), channel_id=1, source_target_pairs={{0,6},{2,4},{4,2},{6,0},{8,14},{10,12},{12,10},{14,8},{16,22},{18,... | collective-permute-start | bytes 393224 | tf_op jit(solution)/shard_map/ppermute | solution.py:201
  118.0 16.5 %collective-permute-start.29 = (bf16[64,1024]{1,0:T(8,128)(2,1)S(1)}, bf16[64,1024]{1,0:T(8,128)(2,1)S(1)}, u32[]{:S(2)}, u32[]{:S(2)}) collective-permute-start(bf16[64,1024]{1,0:T(8,128)(2,1)S(1)} %get-tuple-element.146), channel_id=1, source_target_pairs={{0,4},{2,6},{4,0},{6,2},{8,12},{10,14},{12,8},{14,10},{16,20},{18,... | collective-permute-start | bytes 393224 | tf_op jit(solution)/shard_map/ppermute | solution.py:201
  118.3 16.3 %collective-permute-start.28 = (bf16[64,1024]{1,0:T(8,128)(2,1)S(1)}, bf16[64,1024]{1,0:T(8,128)(2,1)S(1)}, u32[]{:S(2)}, u32[]{:S(2)}) collective-permute-start(bf16[64,1024]{1,0:T(8,128)(2,1)S(1)} %get-tuple-element.147), channel_id=1, source_target_pairs={{0,2},{2,0},{4,6},{6,4},{8,10},{10,8},{12,14},{14,12},{16,18},{18,... | collective-permute-start | bytes 393224 | tf_op jit(solution)/shard_map/ppermute | solution.py:201
  119.8 15.6 %collective-permute-start.39 = (bf16[128,1024]{1,0:T(8,128)(2,1)S(1)}, bf16[128,1024]{1,0:T(8,128)(2,1)S(1)}, u32[]{:S(2)}, u32[]{:S(2)}) collective-permute-start(bf16[128,1024]{1,0:T(8,128)(2,1)S(1)} %combine.6), channel_id=1, source_target_pairs={{0,8},{2,10},{4,12},{6,14},{8,0},{10,2},{12,4},{14,6},{16,24},{18,... | collective-permute-start | bytes 786440 | tf_op jit(solution)/shard_map/ppermute | solution.py:198

commit v3 on v2

--- a/solution.py
+++ b/solution.py
@@ -39,7 +39,10 @@
     return lax.dot_general(a, b, (dims, ((), ())), preferred_element_type=F32)
 
 
-def payload_body(where, routes, gates, arms, tokens, cotangent, bias, out, rows_in, bias_in, sems):
+def payload_body(inner, experts_here, routes, gates, arms, tokens, cotangent, bias, out, *refs):
+    rows_in, bias_in, sems = refs[inner + 1 :]
+    dp_index = lax.axis_index("dp")
+    where = [lax.axis_index("expert"), lax.div(dp_index, inner), lax.rem(dp_index, inner)]
     rows, width = rows_in.shape[1:]
     at = pl.multiple_of(where[0] * width, width)
     copies = [
@@ -60,6 +63,7 @@
     lift = dot(pick, bias_in[...], ((0,), (0,)))
     out[0:rows, :] = (rows_in[0].astype(F32) + lift).astype(BF16)
     out[rows : 2 * rows, :] = rows_in[1]
+    choose_body(inner, experts_here, where, out, *refs[: inner + 1])
 
 
 def choose_body(inner, experts_here, where, *refs):
@@ -138,7 +142,7 @@
 
 def grads_body(rounds, pieces, where, *refs):
     n = rounds * pieces
-    hidden, pre, grad_up, grad_down, flag = refs[2 * n :]
+    hidden, pre, _, grad_up, grad_down, flag = refs[2 * n :]
     for unit, xs, grad in ((pre, refs[:n], grad_up), (hidden, refs[n : 2 * n], grad_down)):
         for q in range(pieces):
             width = xs[0].shape[-1]
@@ -148,13 +152,12 @@
     flag[...] = jnp.zeros(flag.shape, F32)
 
 
-def combine_body(blocks, out_dtype, extra, *refs):
-    table, out = refs[0], refs[-1]
-    rows = jnp.concatenate([ref[...] for ref in refs[1 : 1 + blocks]], axis=0)
-    total = dot(table[...], rows, ((0,), (0,)))
-    for ref in refs[1 + blocks : 1 + blocks + extra]:
-        total = total + ref[...].astype(F32)
-    out[...] = total.astype(out_dtype)
+def combine_body(blocks, groups, *refs):
+    tables, rows, outs = refs[:groups], refs[groups : groups + blocks], refs[-groups:]
+    part = rows[0].shape[0] // groups
+    for g in range(groups):
+        mine = jnp.concatenate([ref[g * part : (g + 1) * part, :] for ref in rows], axis=0)
+        outs[g][...] = dot(tables[g][...], mine, ((0,), (0,))).astype(outs[g].dtype)
 
 
 def local(outer, tokens, arms, arm_bias, routes, gates, up_weight, down_weight, cotangent):
@@ -180,11 +183,12 @@
         return pl.CostEstimate(flops=int(flops), bytes_accessed=int(moved), transcendentals=0)
 
     hbm = pl.BlockSpec(memory_space=pltpu.HBM)
-    payload = pl.pallas_call(
-        payload_body,
-        in_specs=[smem, vmem, vmem, vmem, hbm, hbm, hbm],
-        out_specs=vmem,
-        out_shape=shape((2 * count + META, width), BF16),
+    chosen_shape = [shape((part, 2 * width), BF16)] * inner + [shape((plane, count), BF16)]
+    payload, *own = pl.pallas_call(
+        functools.partial(payload_body, inner, here),
+        in_specs=[vmem, vmem, vmem, hbm, hbm, hbm],
+        out_specs=[vmem] * (inner + 2),
+        out_shape=[shape((2 * count + META, width), BF16), *chosen_shape],
         scratch_shapes=[
             pltpu.VMEM((2, count, width), BF16),
             pltpu.VMEM((arm_bias.shape[0], width), BF16),
@@ -192,7 +196,7 @@
         ],
         compiler_params=pltpu.CompilerParams(vmem_limit_bytes=PAYLOAD_LIMIT),
         name="payload",
-    )(where, routes.T, gates.T, arms.reshape(1, count), tokens, cotangent, arm_bias)
+    )(routes.T, gates.T, arms.reshape(1, count), tokens, cotangent, arm_bias)
 
     def across(value, m):
         return lax.ppermute(value, "dp", [(i, i ^ (m * inner)) for i in range(outer * inner)])
@@ -208,17 +212,15 @@
             functools.partial(choose_body, inner, here),
             in_specs=[smem] + [vmem] * len(candidates),
             out_specs=[vmem] * (inner + 1),
-            out_shape=[shape((part, 2 * width), BF16)] * inner + [shape((plane, count), BF16)],
+            out_shape=chosen_shape,
             compiler_params=params,
             cost_estimate=cost(4 * plane * count * width, 6 * plane * width),
             name="choose",
         )(where, *candidates)
-        return outs[:-1], outs[-1]
-
-    def after(value, *others):
-        return lax.optimization_barrier((value, *others))[0]
-
-    tables, owned = [], []
+        tables.append(outs[-1])
+        return outs[:-1]
+
+    tables, owned = [own[-1]], []
 
     def spread(blocks):
         return [blocks[0]] + [within(blocks[m], m) for m in range(1, inner)]
@@ -227,35 +229,36 @@
         mine = jnp.concatenate(arrived, axis=0).reshape(inner, here, CAP, 2 * width)
         owned.append([mine] + [core_swap(mine, q) for q in range(1, pieces)])
 
-    def pick(candidates):
-        blocks, table = choose(candidates)
-        tables.append(table)
-        return blocks
+    def chained(blocks, arrived):
+        sent, arrived = lax.optimization_barrier((blocks[1:], arrived))
+        share(arrived)
+        return [blocks[0]] + [within(sent[m - 1], m) for m in range(1, inner)]
+
+    def held(values, arrived):
+        values, arrived[1:] = lax.optimization_barrier((values, arrived[1:]))
+        return values
 
     if outer == 4:
         middle = [(i, i ^ (3 * inner)) for i in range(inner, 3 * inner)]
         outward = [(i, i ^ inner) for i in range(inner, 3 * inner)]
         near = across(payload, 1)
         mid = lax.ppermute(payload, "dp", middle)
-        first = spread(pick((payload,)))
-        second = pick((near,))
-        near, mid, first, second = lax.optimization_barrier((near, mid, first, second))
-        share(first)
+        first = spread(own[:-1])
+        near, mid = held([near, mid], first)
+        second = choose((near,))
         far = lax.ppermute(near, "dp", middle)
         out_mid = lax.ppermute(mid, "dp", outward)
-        second = spread(second)
-        third = pick((out_mid, far))
-        far, second, third = lax.optimization_barrier((far, second, third))
-        share(second)
+        second = chained(second, first)
+        far, out_mid = held([far, out_mid], second)
+        third = choose((out_mid, far))
         out_far = lax.ppermute(far, "dp", outward)
-        third = spread(third)
-        fourth = pick((out_far, mid))
-        third, fourth = lax.optimization_barrier((third, fourth))
-        share(third)
-        share(spread(fourth))
+        third = chained(third, second)
+        fourth = choose((out_far, mid))
+        fourth = chained(fourth, third)
+        share(fourth)
     else:
         for m in range(outer):
-            share(spread(pick((across(payload, m) if m else payload,))))
+            share(spread(choose((across(payload, m),)) if m else own[:-1]))
 
     rows_in = [owned[r][q] for q in range(pieces) for r in range(outer)]
     n_in = len(rows_in)
@@ -278,45 +281,62 @@
         name="rows",
     )(where, *rows_in, *rows_in, up_weight, down_weight)
     hidden, pre, partial = back[0], back[1], back[2:]
-    def weight_grads(ordered):
+    any_place = pl.BlockSpec(memory_space=pl.ANY)
+
+    def weight_grads(earlier):
         return pl.pallas_call(
             functools.partial(grads_body, outer, pieces),
             grid=(here,),
-            in_specs=[smem] + lifted_spec + scaled_spec + [unit_spec, unit_spec],
+            in_specs=[smem] + lifted_spec + scaled_spec + [unit_spec, unit_spec, any_place],
             out_specs=[weight_spec, weight_spec, pl.BlockSpec((8, 128), lambda e: (0, 0))],
             out_shape=[shape(up_weight.shape, BF16)] * 2 + [shape((8, 128), F32)],
             compiler_params=params,
             cost_estimate=cost(2 * flops, 2 * weight_bytes + 2 * row_bytes),
             name="weight_grads",
-        )(ordered, *rows_in, *rows_in, hidden, pre)
-
-    def combine(r, blocks, extra, dtype):
+        )(where, *rows_in, *rows_in, hidden, pre, earlier)
+
+    def combine(group, blocks, earlier):
         return pl.pallas_call(
-            functools.partial(combine_body, len(blocks), dtype, len(extra)),
-            in_specs=[vmem] * (1 + len(blocks) + len(extra)),
-            out_specs=vmem,
-            out_shape=shape((count, width), dtype),
+            functools.partial(combine_body, len(blocks), len(group)),
+            in_specs=[vmem] * (len(group) + len(blocks)) + [any_place] * len(earlier),
+            out_specs=[vmem] * len(group),
+            out_shape=[shape((count, width), BF16 if r else F32) for r in group],
             compiler_params=params,
-            cost_estimate=cost(2 * plane * count * width, 2 * plane * width),
+            cost_estimate=cost(2 * len(group) * plane * count * width, 2 * len(group) * plane * width),
             name="combine",
-        )(tables[r], *blocks, *extra)
-
-    sums = []
+        )(*[tables[r] for r in group], *blocks, *earlier)
+
     swapped = [[core_swap(partial[q * outer + r], q) for q in range(1, pieces)] for r in range(outer)]
-    ready = [None] * outer
-    for r in range(outer):
-        total = partial[r].astype(F32)
-        for value in swapped[r]:
-            total = total + value.astype(F32)
-        ready[r] = total.astype(BF16).reshape(inner, part, width)
-    grad_up, grad_down, flag = weight_grads(where)
-    for r in reversed(range(outer)):
-        blocks = [ready[r][0]] + [within(ready[r][m], m) for m in range(1, inner)]
-        if r:
-            blocks[-1], ready[r - 1] = lax.optimization_barrier((blocks[-1], ready[r - 1]))
-            sums.append(across(combine(r, blocks, [], BF16), r))
-        else:
-            grad_tokens = combine(0, blocks, sums, F32)
+    groups = [list(g) for g in ([outer - 1], range(outer - 2, 0, -1), [0]) if len(g) and g[0] < outer]
+    groups = groups if outer > 1 else [[0]]
+    ready = []
+    for group in groups:
+        rows = []
+        for r in group:
+            total = partial[r].astype(F32)
+            for value in swapped[r]:
+                total = total + value.astype(F32)
+            rows.append(total.astype(BF16).reshape(inner, part, width))
+        ready.append([jnp.concatenate([row[m] for row in rows], axis=0) for m in range(inner)])
+    sums, flag = [], []
+    for i, group in enumerate(groups):
+        blocks = [ready[i][0]] + [within(ready[i][m], m) for m in range(1, inner)]
+        if i + 1 < len(groups):
+            blocks[-1], ready[i + 1][1:] = lax.optimization_barrier((blocks[-1], ready[i + 1][1:]))
+        if i == 1:
+            grad_up, grad_down, flag = weight_grads(sent)
+            flag = [flag]
+        done = combine(group, blocks, flag)
+        for r, value in zip(group, done):
+            if r:
+                sent = value
+                sums.append(across(value, r))
+            else:
+                grad_tokens = value
+    if not flag:
+        grad_up, grad_down, _ = weight_grads(grad_tokens)
+    for value in sums:
+        grad_tokens = grad_tokens + value.astype(F32)
     return (grad_tokens, grad_up, grad_down)
 
 

time: 137 us -> 130 us (0.949)
  starting transfers between devices: 47.9 us -> 38.9 us
  waiting for transfers between devices: 50.4 us -> 53.6 us
  local copies, waits for them, and re-layouts: 1.85 us -> 0.17 us
    ppermute x24 -> x21, waiting for transfers between devices: 18.4 us -> 37 us  [within(): return lax.ppermute(value, 'dp', [(i, i ^ m) for i in range(outer * inner)])]
    ppermute x1, waiting for transfers between devices: 13 us -> 1.8 us  [local(): out_mid = lax.ppermute(mid, 'dp', outward)]
    ppermute x4, starting transfers between devices: 13.8 us -> 8.24 us  [across(): lax.ppermute(value, 'dp', [(i, i ^ m * inner) for i in range(outer * inne...]
    ppermute x24 -> x21, starting transfers between devices: 28.8 us -> 25.4 us  [within(): return lax.ppermute(value, 'dp', [(i, i ^ m) for i in range(outer * inner)])]
    ppermute x4, waiting for transfers between devices: 6.61 us -> 3.96 us  [across(): lax.ppermute(value, 'dp', [(i, i ^ m * inner) for i in range(outer * inne...]
    ppermute x1, waiting for transfers between devices: 8.89 us -> 6.86 us  [local(): out_far = lax.ppermute(far, 'dp', outward)]
    unnamed x4 -> x2, local copies, waits for them, and re-layouts: 1.71 us -> 0.01 us
    pallas_call x4 -> x3, Pallas kernels: 4.35 us -> 3.27 us  [choose(): pl.pallas_call(functools.partial(choose_body, inner, here), in_specs=[sme...]
  transfers between devices with their start and end apart: 40 -> 37, of which waited for: 11 -> 18; matrix products, arithmetic and copies ran while one was open for 1% -> 2% of each run, Pallas kernels for 11% -> 11%
where the time goes in v3:
time: 130 us
  waiting for transfers between devices  53.6 us (41%)
  starting transfers between devices  38.9 us (30%)
  Pallas kernels  32.9 us (25%)
  other arithmetic  3.15 us (2%)
    ppermute x21, waiting for transfers between devices, within(): return lax.ppermute(value, 'dp', [(i, i ^ m) for i in range(outer * inner)])  37 us
    ppermute x21, starting transfers between devices, within(): return lax.ppermute(value, 'dp', [(i, i ^ m) for i in range(outer * inner)])  25.4 us
    pallas_call x1, Pallas kernels, local(): pl.pallas_call(functools.partial(rows_body, outer, pieces), grid=(here,),...  14.7 us
    pallas_call x1, Pallas kernels, weight_grads(): pl.pallas_call(functools.partial(grads_body, outer, pieces), grid=(here,)...  10.8 us
    ppermute x4, starting transfers between devices, across(): lax.ppermute(value, 'dp', [(i, i ^ m * inner) for i in range(outer * inne...  8.24 us
    ppermute x1, waiting for transfers between devices, local(): out_far = lax.ppermute(far, 'dp', outward)  6.86 us
    ppermute x8, waiting for transfers between devices, core_swap(): return lax.ppermute(value, 'expert', [(i, i ^ q) for i in range(pieces)])  4.02 us
    ppermute x4, waiting for transfers between devices, across(): lax.ppermute(value, 'dp', [(i, i ^ m * inner) for i in range(outer * inne...  3.96 us
  transfers between devices with their start and end apart: 37, of which 18 were waited for; matrix products, arithmetic and copies ran while one was open for 2% of the time, Pallas kernels for 11%

profile of v3, /device:TPU:0, one launch (start us, length us, event | category | flops | bytes accessed | tf_op | source)
XLA Modules:
  0.0 129.7 jit_solution(15645550473667735389)
XLA Ops:
  0.6 3.4 %payload.1 = (bf16[272,1024]{1,0:T(8,128)(2,1)}, bf16[64,2048]{1,0:T(8,128)(2,1)}, bf16[64,2048]{1,0:T(8,128)(2,1)}, bf16[64,2048]{1,0:T(8,128)(2,1)}, bf16[64,2...) custom-call(s32[6,128]{1,0:T(8,128)} %bitcast.63, s32[6,128]{1,0:T(8,128)} %bitcast.64, s32[1,128]{1,0:T(1,128)} %bitcast.65, ...), custom_call_target="tpu_custom_call" | custom-call | tf_op jit(solution)/shard_map/payload/pallas_call | solution.py:187
  4.0 3.1 %collective-permute-start = (bf16[272,1024]{1,0:T(8,128)(2,1)}, bf16[272,1024]{1,0:T(8,128)(2,1)S(1)}, u32[]{:S(2)}, u32[]{:S(2)}) collective-permute-start(bf16[272,1024]{1,0:T(8,128)(2,1)} %get-tuple-element.79), channel_id=1, source_target_pairs={{0,8},{2,10},{4,12},{6,14},{8,0},{10,2},{12,4},{14,6},{16,24},{18,... | collective-permute-start | bytes 1671176 | tf_op jit(solution)/shard_map/ppermute | solution.py:202
  7.1 0.7 collective-permute-start.1
  7.8 1.6 %collective-permute-start.2 = (bf16[64,2048]{1,0:T(8,128)(2,1)}, bf16[64,2048]{1,0:T(8,128)(2,1)S(1)}, u32[]{:S(2)}, u32[]{:S(2)}) collective-permute-start(bf16[64,2048]{1,0:T(8,128)(2,1)} %get-tuple-element.80), channel_id=1, source_target_pairs={{0,2},{2,0},{4,6},{6,4},{8,10},{10,8},{12,14},{14,12},{16,18},{18,... | collective-permute-start | bytes 786440 | tf_op jit(solution)/shard_map/ppermute | solution.py:205
  9.3 1.5 %collective-permute-start.3 = (bf16[64,2048]{1,0:T(8,128)(2,1)}, bf16[64,2048]{1,0:T(8,128)(2,1)S(1)}, u32[]{:S(2)}, u32[]{:S(2)}) collective-permute-start(bf16[64,2048]{1,0:T(8,128)(2,1)} %get-tuple-element.81), channel_id=1, source_target_pairs={{0,4},{2,6},{4,0},{6,2},{8,12},{10,14},{12,8},{14,10},{16,20},{18,... | collective-permute-start | bytes 786440 | tf_op jit(solution)/shard_map/ppermute | solution.py:205
  11.3 6.0 %collective-permute-done.2 = bf16[64,2048]{1,0:T(8,128)(2,1)S(1)} collective-permute-done((bf16[64,2048]{1,0:T(8,128)(2,1)}, bf16[64,2048]{1,0:T(8,128)(2,1)S(1)}, u32[]{:S(2)}, u32[]{:S(2)}) %collective-permute-start.2) | collective-permute-done | bytes 262176 | tf_op jit(solution)/shard_map/ppermute | solution.py:205
  17.3 5.4 %collective-permute-done.3 = bf16[64,2048]{1,0:T(8,128)(2,1)S(1)} collective-permute-done((bf16[64,2048]{1,0:T(8,128)(2,1)}, bf16[64,2048]{1,0:T(8,128)(2,1)S(1)}, u32[]{:S(2)}, u32[]{:S(2)}) %collective-permute-start.3) | collective-permute-done | bytes 262176 | tf_op jit(solution)/shard_map/ppermute | solution.py:205
  22.7 0.7 collective-permute-start.5
  23.4 1.3 collective-permute-start.6
  24.8 1.1 choose.3
  25.9 1.3 collective-permute-start.7
  27.1 0.8 collective-permute-start.8
  28.0 1.4 %collective-permute-start.9 = (bf16[64,2048]{1,0:T(8,128)(2,1)S(1)}, bf16[64,2048]{1,0:T(8,128)(2,1)S(1)}, u32[]{:S(2)}, u32[]{:S(2)}) collective-permute-start(bf16[64,2048]{1,0:T(8,128)(2,1)S(1)} %get-tuple-element.98), channel_id=1, source_target_pairs={{0,6},{2,4},{4,2},{6,0},{8,14},{10,12},{12,10},{14,8},{16,22},{18,... | collective-permute-start | bytes 786440 | tf_op jit(solution)/shard_map/ppermute | solution.py:205
  29.4 5.8 %collective-permute-done.7 = bf16[64,2048]{1,0:T(8,128)(2,1)S(1)} collective-permute-done((bf16[64,2048]{1,0:T(8,128)(2,1)S(1)}, bf16[64,2048]{1,0:T(8,128)(2,1)S(1)}, u32[]{:S(2)}, u32[]{:S(2)}) %collective-permute-start.7) | collective-permute-done | bytes 262176 | tf_op jit(solution)/shard_map/ppermute | solution.py:205
  35.2 4.2 %collective-permute-done.8 = bf16[64,2048]{1,0:T(8,128)(2,1)S(1)} collective-permute-done((bf16[64,2048]{1,0:T(8,128)(2,1)S(1)}, bf16[64,2048]{1,0:T(8,128)(2,1)S(1)}, u32[]{:S(2)}, u32[]{:S(2)}) %collective-permute-start.8) | collective-permute-done | bytes 262176 | tf_op jit(solution)/shard_map/ppermute | solution.py:205
  39.3 1.8 %collective-permute-done.6.refs_0_ = bf16[272,1024]{1,0:T(8,128)(2,1)S(1)} collective-permute-done((bf16[272,1024]{1,0:T(8,128)(2,1)S(1)}, bf16[272,1024]{1,0:T(8,128)(2,1)S(1)}, u32[]{:S(2)}, u32[]{:S(2)}) %collective-permute-start.6) | collective-permute-done | bytes 557088 | tf_op jit(solution)/shard_map/ppermute | solution.py:250
  41.1 1.3 collective-permute-start.10
  42.4 1.1 choose.4
  43.5 1.5 %collective-permute-start.11 = (bf16[64,2048]{1,0:T(8,128)(2,1)S(1)}, bf16[64,2048]{1,0:T(8,128)(2,1)S(1)}, u32[]{:S(2)}, u32[]{:S(2)}) collective-permute-start(bf16[64,2048]{1,0:T(8,128)(2,1)S(1)} %get-tuple-element.116), channel_id=1, source_target_pairs={{0,2},{2,0},{4,6},{6,4},{8,10},{10,8},{12,14},{14,12},{16,18},{18,... | collective-permute-start | bytes 786440 | tf_op jit(solution)/shard_map/ppermute | solution.py:205
  45.1 1.2 collective-permute-start.12
  46.2 0.9 collective-permute-start.13
  47.1 1.0 pad_maximum_fusion
  48.2 6.9 %collective-permute-done.10.refs_0_ = bf16[272,1024]{1,0:T(8,128)(2,1)S(1)} collective-permute-done((bf16[272,1024]{1,0:T(8,128)(2,1)S(1)}, bf16[272,1024]{1,0:T(8,128)(2,1)S(1)}, u32[]{:S(2)}, u32[]{:S(2)}) %collective-permute-start.10) | collective-permute-done | bytes 557088 | tf_op jit(solution)/shard_map/ppermute | solution.py:254
  55.0 1.1 choose.5
  56.2 3.4 %collective-permute-done.12 = bf16[64,2048]{1,0:T(8,128)(2,1)S(1)} collective-permute-done((bf16[64,2048]{1,0:T(8,128)(2,1)S(1)}, bf16[64,2048]{1,0:T(8,128)(2,1)S(1)}, u32[]{:S(2)}, u32[]{:S(2)}) %collective-permute-start.12) | collective-permute-done | bytes 262176 | tf_op jit(solution)/shard_map/ppermute | solution.py:205
  59.7 3.3 %collective-permute-start.14 = (bf16[64,2048]{1,0:T(8,128)(2,1)S(1)}, bf16[64,2048]{1,0:T(8,128)(2,1)S(1)}, u32[]{:S(2)}, u32[]{:S(2)}) collective-permute-start(bf16[64,2048]{1,0:T(8,128)(2,1)S(1)} %get-tuple-element.124), channel_id=1, source_target_pairs={{0,2},{2,0},{4,6},{6,4},{8,10},{10,8},{12,14},{14,12},{16,18},{18,... | collective-permute-start | bytes 786440 | tf_op jit(solution)/shard_map/ppermute | solution.py:205
  63.3 3.6 %collective-permute-done.16 = bf16[64,2048]{1,0:T(8,128)(2,1)S(1)} collective-permute-done((bf16[64,2048]{1,0:T(8,128)(2,1)S(1)}, bf16[64,2048]{1,0:T(8,128)(2,1)S(1)}, u32[]{:S(2)}, u32[]{:S(2)}) %collective-permute-start.16) | collective-permute-done | bytes 262176 | tf_op jit(solution)/shard_map/ppermute | solution.py:205
  66.9 1.8 %collective-permute-done.15 = bf16[64,2048]{1,0:T(8,128)(2,1)S(1)} collective-permute-done((bf16[64,2048]{1,0:T(8,128)(2,1)S(1)}, bf16[64,2048]{1,0:T(8,128)(2,1)S(1)}, u32[]{:S(2)}, u32[]{:S(2)}) %collective-permute-start.15) | collective-permute-done | bytes 262176 | tf_op jit(solution)/shard_map/ppermute | solution.py:205
  69.6 2.0 %collective-permute-done.20.refs_7_.refs_15_ = bf16[4,4,16,2048]{3,2,1,0:T(8,128)(2,1)S(1)} collective-permute-done((bf16[4,4,16,2048]{3,2,1,0:T(8,128)(2,1)S(1)}, bf16[4,4,16,2048]{3,2,1,0:T(8,128)(2,1)S(1)}, u32[]{:S(2)}, u32[]{:S(2)}) %collective-permute-start.20) | collective-permute-done | bytes 1048608 | tf_op jit(solution)/shard_map/ppermute | solution.py:208
  71.5 14.7 %rows.1 = (bf16[4,704,256]{2,1,0:T(8,128)(2,1)S(1)}, bf16[4,704,256]{2,1,0:T(8,128)(2,1)S(1)}, bf16[4,4,16,1024]{3,2,1,0:T(8,128)(2,1)S(1)}, bf16[4,4,16,1024]{3...) custom-call(s32[4]{0:T(128)S(1)} %pad_add_fusion.where, ...), custom_call_target="tpu_custom_call" | custom-call | flops 8858370048 | bytes 35651584 | tf_op jit(solution)/shard_map/rows/pallas_call | solution.py:273
  87.3 0.9 collective-permute-done.25
  89.2 1.2 collective-permute-start.23
  91.0 1.9 %collective-permute-start.30 = (bf16[64,1024]{1,0:T(8,128)(2,1)S(1)}, bf16[64,1024]{1,0:T(8,128)(2,1)S(1)}, u32[]{:S(2)}, u32[]{:S(2)}) collective-permute-start(bf16[64,1024]{1,0:T(8,128)(2,1)S(1)} %bitcast.61), channel_id=1, source_target_pairs={{0,2},{2,0},{4,6},{6,4},{8,10},{10,8},{12,14},{14,12},{16,18},{18,... | collective-permute-start | bytes 393224 | tf_op jit(solution)/shard_map/ppermute | solution.py:205
  93.4 3.1 %collective-permute-done.23.refs_4_ = bf16[64,1024]{1,0:T(8,128)(2,1)S(1)} collective-permute-done((bf16[64,1024]{1,0:T(8,128)(2,1)S(1)}, bf16[64,1024]{1,0:T(8,128)(2,1)S(1)}, u32[]{:S(2)}, u32[]{:S(2)}) %collective-permute-start.23) | collective-permute-done | bytes 131104 | tf_op jit(solution)/shard_map/ppermute | solution.py:205
  97.2 1.0 collective-permute-start.34
  98.2 1.9 %collective-permute-start.26 = (bf16[128,1024]{1,0:T(8,128)(2,1)S(1)}, bf16[128,1024]{1,0:T(8,128)(2,1)S(1)}, u32[]{:S(2)}, u32[]{:S(2)}) collective-permute-start(bf16[128,1024]{1,0:T(8,128)(2,1)S(1)} %pad_maximum_fusion.6), channel_id=1, source_target_pairs={{0,6},{2,4},{4,2},{6,0},{8,14},{10,12},{12,10},{14,8},{16,22},{18,... | collective-permute-start | bytes 786440 | tf_op jit(solution)/shard_map/ppermute | solution.py:205
  100.3 2.6 %collective-permute-start.32 = (bf16[128,1024]{1,0:T(8,128)(2,1)S(1)}, bf16[128,1024]{1,0:T(8,128)(2,1)S(1)}, u32[]{:S(2)}, u32[]{:S(2)}) collective-permute-start(bf16[128,1024]{1,0:T(8,128)(2,1)S(1)} %combine.3.refs_18_), channel_id=1, source_target_pairs={{0,24},{2,26},{4,28},{6,30},{8,16},{10,18},{12,20},{14,22},{16,8},... | collective-permute-start | bytes 786440 | tf_op jit(solution)/shard_map/ppermute | solution.py:202
  102.9 10.8 %weight_grads.1 = (bf16[4,704,2048]{2,1,0:T(8,128)(2,1)}, bf16[4,704,2048]{2,1,0:T(8,128)(2,1)}, f32[8,128]{1,0:T(8,128)S(1)}) custom-call(s32[4]{0:T(128)S(1)} %pad_add_fusion.where, bf16[4,4,16,2048]{3,2,1,0:T(8,128)(2,1)S(1)} %bitcast.30, bf16[4,4,16,2048]{3,2,1,0:T(8,128)(2,1)S(1)} %bitcast.35, bf16[4,4,16,2048]{3,2,1,0:T(8,128)(2,1)S(1)} %bitcast.40, ...), custom_call_target="tpu_custom_call" | custom-call | flops 5905580032 | bytes 31457280 | tf_op jit(solution)/shard_map/weight_grads/pallas_call | solution.py:287
  113.7 0.7 collective-permute-start.27
  114.7 1.6 %collective-permute-start.36 = (bf16[128,1024]{1,0:T(8,128)(2,1)S(1)}, bf16[128,1024]{1,0:T(8,128)(2,1)S(1)}, u32[]{:S(2)}, u32[]{:S(2)}) collective-permute-start(bf16[128,1024]{1,0:T(8,128)(2,1)S(1)} %get-tuple-element.150), channel_id=1, source_target_pairs={{0,8},{2,10},{4,12},{6,14},{8,0},{10,2},{12,4},{14,6},{16,24},{18,... | collective-permute-start | bytes 786440 | tf_op jit(solution)/shard_map/ppermute | solution.py:202
  116.3 0.9 collective-permute-start.35
  117.2 1.4 %collective-permute-start.28 = (bf16[64,1024]{1,0:T(8,128)(2,1)S(1)}, bf16[64,1024]{1,0:T(8,128)(2,1)S(1)}, u32[]{:S(2)}, u32[]{:S(2)}) collective-permute-start(bf16[64,1024]{1,0:T(8,128)(2,1)S(1)} %bitcast.58), channel_id=1, source_target_pairs={{0,4},{2,6},{4,0},{6,2},{8,12},{10,14},{12,8},{14,10},{16,20},{18,... | collective-permute-start | bytes 393224 | tf_op jit(solution)/shard_map/ppermute | solution.py:205
  118.7 2.0 %collective-permute-start.29 = (bf16[64,1024]{1,0:T(8,128)(2,1)S(1)}, bf16[64,1024]{1,0:T(8,128)(2,1)S(1)}, u32[]{:S(2)}, u32[]{:S(2)}) collective-permute-start(bf16[64,1024]{1,0:T(8,128)(2,1)S(1)} %bitcast.57), channel_id=1, source_target_pairs={{0,6},{2,4},{4,2},{6,0},{8,14},{10,12},{12,10},{14,8},{16,22},{18,... | collective-permute-start | bytes 393224 | tf_op jit(solution)/shard_map/ppermute | solution.py:205
  120.7 1.7 %collective-permute-done.28.refs_3_ = bf16[64,1024]{1,0:T(8,128)(2,1)S(1)} collective-permute-done((bf16[64,1024]{1,0:T(8,128)(2,1)S(1)}, bf16[64,1024]{1,0:T(8,128)(2,1)S(1)}, u32[]{:S(2)}, u32[]{:S(2)}) %collective-permute-start.28) | collective-permute-done | bytes 131104 | tf_op jit(solution)/shard_map/ppermute | solution.py:205
  122.4 2.2 %collective-permute-done.29.refs_4_ = bf16[64,1024]{1,0:T(8,128)(2,1)S(1)} collective-permute-done((bf16[64,1024]{1,0:T(8,128)(2,1)S(1)}, bf16[64,1024]{1,0:T(8,128)(2,1)S(1)}, u32[]{:S(2)}, u32[]{:S(2)}) %collective-permute-start.29) | collective-permute-done | bytes 131104 | tf_op jit(solution)/shard_map/ppermute | solution.py:205
  124.8 1.1 collective-permute-done.36
  125.9 2.8 %collective-permute-done.35 = bf16[128,1024]{1,0:T(8,128)(2,1)S(1)} collective-permute-done((bf16[128,1024]{1,0:T(8,128)(2,1)S(1)}, bf16[128,1024]{1,0:T(8,128)(2,1)S(1)}, u32[]{:S(2)}, u32[]{:S(2)}) %collective-permute-start.35) | collective-permute-done | bytes 262176 | tf_op jit(solution)/shard_map/ppermute | solution.py:202
  128.8 0.9 convert_add_fusion
  (54 shorter events, 6.6 us)
Async XLA Ops:
  4.0 18.7 %collective-permute-start = (bf16[272,1024]{1,0:T(8,128)(2,1)}, bf16[272,1024]{1,0:T(8,128)(2,1)S(1)}, u32[]{:S(2)}, u32[]{:S(2)}) collective-permute-start(bf16[272,1024]{1,0:T(8,128)(2,1)} %get-tuple-element.79), channel_id=1, source_target_pairs={{0,8},{2,10},{4,12},{6,14},{8,0},{10,2},{12,4},{14,6},{16,24},{18,... | collective-permute-start | bytes 1671176 | tf_op jit(solution)/shard_map/ppermute | solution.py:202
  7.1 15.6 %collective-permute-start.1 = (bf16[272,1024]{1,0:T(8,128)(2,1)}, bf16[272,1024]{1,0:T(8,128)(2,1)S(1)}, u32[]{:S(2)}, u32[]{:S(2)}) collective-permute-start(bf16[272,1024]{1,0:T(8,128)(2,1)} %get-tuple-element.79), channel_id=1, source_target_pairs={{8,16},{10,18},{12,20},{14,22},{16,8},{18,10},{20,12},{22,14},{9,1... | collective-permute-start | bytes 1671176 | tf_op jit(solution)/shard_map/ppermute | solution.py:245
  7.8 9.5 %collective-permute-start.2 = (bf16[64,2048]{1,0:T(8,128)(2,1)}, bf16[64,2048]{1,0:T(8,128)(2,1)S(1)}, u32[]{:S(2)}, u32[]{:S(2)}) collective-permute-start(bf16[64,2048]{1,0:T(8,128)(2,1)} %get-tuple-element.80), channel_id=1, source_target_pairs={{0,2},{2,0},{4,6},{6,4},{8,10},{10,8},{12,14},{14,12},{16,18},{18,... | collective-permute-start | bytes 786440 | tf_op jit(solution)/shard_map/ppermute | solution.py:205
  9.3 13.3 %collective-permute-start.3 = (bf16[64,2048]{1,0:T(8,128)(2,1)}, bf16[64,2048]{1,0:T(8,128)(2,1)S(1)}, u32[]{:S(2)}, u32[]{:S(2)}) collective-permute-start(bf16[64,2048]{1,0:T(8,128)(2,1)} %get-tuple-element.81), channel_id=1, source_target_pairs={{0,4},{2,6},{4,0},{6,2},{8,12},{10,14},{12,8},{14,10},{16,20},{18,... | collective-permute-start | bytes 786440 | tf_op jit(solution)/shard_map/ppermute | solution.py:205
  10.8 11.8 %collective-permute-start.4 = (bf16[64,2048]{1,0:T(8,128)(2,1)}, bf16[64,2048]{1,0:T(8,128)(2,1)S(1)}, u32[]{:S(2)}, u32[]{:S(2)}) collective-permute-start(bf16[64,2048]{1,0:T(8,128)(2,1)} %get-tuple-element.82), channel_id=1, source_target_pairs={{0,6},{2,4},{4,2},{6,0},{8,14},{10,12},{12,10},{14,8},{16,22},{18,... | collective-permute-start | bytes 786440 | tf_op jit(solution)/shard_map/ppermute | solution.py:205
  22.7 16.7 %collective-permute-start.5 = (bf16[272,1024]{1,0:T(8,128)(2,1)S(1)}, bf16[272,1024]{1,0:T(8,128)(2,1)S(1)}, u32[]{:S(2)}, u32[]{:S(2)}) collective-permute-start(bf16[272,1024]{1,0:T(8,128)(2,1)S(1)} %collective-permute-done.refs_0_), channel_id=1, source_target_pairs={{8,16},{10,18},{12,20},{14,22},{16,8},{18,10},{20,12},{22,14},{9,1... | collective-permute-start | bytes 1671176 | tf_op jit(solution)/shard_map/ppermute | solution.py:249
  23.4 17.8 %collective-permute-start.6 = (bf16[272,1024]{1,0:T(8,128)(2,1)S(1)}, bf16[272,1024]{1,0:T(8,128)(2,1)S(1)}, u32[]{:S(2)}, u32[]{:S(2)}) collective-permute-start(bf16[272,1024]{1,0:T(8,128)(2,1)S(1)} %collective-permute-done.1.refs_1_), channel_id=1, source_target_pairs={{8,0},{10,2},{12,4},{14,6},{16,24},{18,26},{20,28},{22,30},{9,1},{... | collective-permute-start | bytes 1671176 | tf_op jit(solution)/shard_map/ppermute | solution.py:250
  25.9 9.3 %collective-permute-start.7 = (bf16[64,2048]{1,0:T(8,128)(2,1)S(1)}, bf16[64,2048]{1,0:T(8,128)(2,1)S(1)}, u32[]{:S(2)}, u32[]{:S(2)}) collective-permute-start(bf16[64,2048]{1,0:T(8,128)(2,1)S(1)} %get-tuple-element.96), channel_id=1, source_target_pairs={{0,2},{2,0},{4,6},{6,4},{8,10},{10,8},{12,14},{14,12},{16,18},{18,... | collective-permute-start | bytes 786440 | tf_op jit(solution)/shard_map/ppermute | solution.py:205
  27.1 12.2 %collective-permute-start.8 = (bf16[64,2048]{1,0:T(8,128)(2,1)S(1)}, bf16[64,2048]{1,0:T(8,128)(2,1)S(1)}, u32[]{:S(2)}, u32[]{:S(2)}) collective-permute-start(bf16[64,2048]{1,0:T(8,128)(2,1)S(1)} %get-tuple-element.97), channel_id=1, source_target_pairs={{0,4},{2,6},{4,0},{6,2},{8,12},{10,14},{12,8},{14,10},{16,20},{18,... | collective-permute-start | bytes 786440 | tf_op jit(solution)/shard_map/ppermute | solution.py:205
  28.0 11.4 %collective-permute-start.9 = (bf16[64,2048]{1,0:T(8,128)(2,1)S(1)}, bf16[64,2048]{1,0:T(8,128)(2,1)S(1)}, u32[]{:S(2)}, u32[]{:S(2)}) collective-permute-start(bf16[64,2048]{1,0:T(8,128)(2,1)S(1)} %get-tuple-element.98), channel_id=1, source_target_pairs={{0,6},{2,4},{4,2},{6,0},{8,14},{10,12},{12,10},{14,8},{16,22},{18,... | collective-permute-start | bytes 786440 | tf_op jit(solution)/shard_map/ppermute | solution.py:205
  41.1 13.9 %collective-permute-start.10 = (bf16[272,1024]{1,0:T(8,128)(2,1)S(1)}, bf16[272,1024]{1,0:T(8,128)(2,1)S(1)}, u32[]{:S(2)}, u32[]{:S(2)}) collective-permute-start(bf16[272,1024]{1,0:T(8,128)(2,1)S(1)} %collective-permute-done.5.refs_1_), channel_id=1, source_target_pairs={{8,0},{10,2},{12,4},{14,6},{16,24},{18,26},{20,28},{22,30},{9,1},{... | collective-permute-start | bytes 1671176 | tf_op jit(solution)/shard_map/ppermute | solution.py:254
  43.5 12.6 %collective-permute-start.11 = (bf16[64,2048]{1,0:T(8,128)(2,1)S(1)}, bf16[64,2048]{1,0:T(8,128)(2,1)S(1)}, u32[]{:S(2)}, u32[]{:S(2)}) collective-permute-start(bf16[64,2048]{1,0:T(8,128)(2,1)S(1)} %get-tuple-element.116), channel_id=1, source_target_pairs={{0,2},{2,0},{4,6},{6,4},{8,10},{10,8},{12,14},{14,12},{16,18},{18,... | collective-permute-start | bytes 786440 | tf_op jit(solution)/shard_map/ppermute | solution.py:205
  45.1 14.5 %collective-permute-start.12 = (bf16[64,2048]{1,0:T(8,128)(2,1)S(1)}, bf16[64,2048]{1,0:T(8,128)(2,1)S(1)}, u32[]{:S(2)}, u32[]{:S(2)}) collective-permute-start(bf16[64,2048]{1,0:T(8,128)(2,1)S(1)} %get-tuple-element.117), channel_id=1, source_target_pairs={{0,4},{2,6},{4,0},{6,2},{8,12},{10,14},{12,8},{14,10},{16,20},{18,... | collective-permute-start | bytes 786440 | tf_op jit(solution)/shard_map/ppermute | solution.py:205
  46.2 13.3 %collective-permute-start.13 = (bf16[64,2048]{1,0:T(8,128)(2,1)S(1)}, bf16[64,2048]{1,0:T(8,128)(2,1)S(1)}, u32[]{:S(2)}, u32[]{:S(2)}) collective-permute-start(bf16[64,2048]{1,0:T(8,128)(2,1)S(1)} %get-tuple-element.118), channel_id=1, source_target_pairs={{0,6},{2,4},{4,2},{6,0},{8,14},{10,12},{12,10},{14,8},{16,22},{18,... | collective-permute-start | bytes 786440 | tf_op jit(solution)/shard_map/ppermute | solution.py:205
  48.1 20.8 %collective-permute-start.17 = (bf16[4,4,16,2048]{3,2,1,0:T(8,128)(2,1)S(1)}, bf16[4,4,16,2048]{3,2,1,0:T(8,128)(2,1)S(1)}, u32[]{:S(2)}, u32[]{:S(2)}) collective-permute-start(bf16[4,4,16,2048]{3,2,1,0:T(8,128)(2,1)S(1)} %bitcast.27), channel_id=1, source_target_pairs={{0,1},{1,0},{2,3},{3,2},{4,5},{5,4},{6,7},{7,6},{8,9},{9,8},{10,11... | collective-permute-start | bytes 3145736 | tf_op jit(solution)/shard_map/ppermute | solution.py:208
  59.5 7.4 %collective-permute-start.16 = (bf16[64,2048]{1,0:T(8,128)(2,1)S(1)}, bf16[64,2048]{1,0:T(8,128)(2,1)S(1)}, u32[]{:S(2)}, u32[]{:S(2)}) collective-permute-start(bf16[64,2048]{1,0:T(8,128)(2,1)S(1)} %get-tuple-element.126), channel_id=1, source_target_pairs={{0,6},{2,4},{4,2},{6,0},{8,14},{10,12},{12,10},{14,8},{16,22},{18,... | collective-permute-start | bytes 786440 | tf_op jit(solution)/shard_map/ppermute | solution.py:205
  59.5 9.2 %collective-permute-start.15 = (bf16[64,2048]{1,0:T(8,128)(2,1)S(1)}, bf16[64,2048]{1,0:T(8,128)(2,1)S(1)}, u32[]{:S(2)}, u32[]{:S(2)}) collective-permute-start(bf16[64,2048]{1,0:T(8,128)(2,1)S(1)} %get-tuple-element.125), channel_id=1, source_target_pairs={{0,4},{2,6},{4,0},{6,2},{8,12},{10,14},{12,8},{14,10},{16,20},{18,... | collective-permute-start | bytes 786440 | tf_op jit(solution)/shard_map/ppermute | solution.py:205
  59.7 9.0 %collective-permute-start.14 = (bf16[64,2048]{1,0:T(8,128)(2,1)S(1)}, bf16[64,2048]{1,0:T(8,128)(2,1)S(1)}, u32[]{:S(2)}, u32[]{:S(2)}) collective-permute-start(bf16[64,2048]{1,0:T(8,128)(2,1)S(1)} %get-tuple-element.124), channel_id=1, source_target_pairs={{0,2},{2,0},{4,6},{6,4},{8,10},{10,8},{12,14},{14,12},{16,18},{18,... | collective-permute-start | bytes 786440 | tf_op jit(solution)/shard_map/ppermute | solution.py:205
  63.1 5.8 %collective-permute-start.18 = (bf16[4,4,16,2048]{3,2,1,0:T(8,128)(2,1)S(1)}, bf16[4,4,16,2048]{3,2,1,0:T(8,128)(2,1)S(1)}, u32[]{:S(2)}, u32[]{:S(2)}) collective-permute-start(bf16[4,4,16,2048]{3,2,1,0:T(8,128)(2,1)S(1)} %bitcast.32), channel_id=1, source_target_pairs={{0,1},{1,0},{2,3},{3,2},{4,5},{5,4},{6,7},{7,6},{8,9},{9,8},{10,11... | collective-permute-start | bytes 3145736 | tf_op jit(solution)/shard_map/ppermute | solution.py:208
  66.9 2.7 %collective-permute-start.19 = (bf16[4,4,16,2048]{3,2,1,0:T(8,128)(2,1)S(1)}, bf16[4,4,16,2048]{3,2,1,0:T(8,128)(2,1)S(1)}, u32[]{:S(2)}, u32[]{:S(2)}) collective-permute-start(bf16[4,4,16,2048]{3,2,1,0:T(8,128)(2,1)S(1)} %bitcast.37), channel_id=1, source_target_pairs={{0,1},{1,0},{2,3},{3,2},{4,5},{5,4},{6,7},{7,6},{8,9},{9,8},{10,11... | collective-permute-start | bytes 3145736 | tf_op jit(solution)/shard_map/ppermute | solution.py:208
  68.8 2.7 %collective-permute-start.20 = (bf16[4,4,16,2048]{3,2,1,0:T(8,128)(2,1)S(1)}, bf16[4,4,16,2048]{3,2,1,0:T(8,128)(2,1)S(1)}, u32[]{:S(2)}, u32[]{:S(2)}) collective-permute-start(bf16[4,4,16,2048]{3,2,1,0:T(8,128)(2,1)S(1)} %bitcast.42), channel_id=1, source_target_pairs={{0,1},{1,0},{2,3},{3,2},{4,5},{5,4},{6,7},{7,6},{8,9},{9,8},{10,11... | collective-permute-start | bytes 3145736 | tf_op jit(solution)/shard_map/ppermute | solution.py:208
  86.2 2.0 %collective-permute-start.25 = (bf16[4,4,16,1024]{3,2,1,0:T(8,128)(2,1)S(1)}, bf16[4,4,16,1024]{3,2,1,0:T(8,128)(2,1)S(1)}, u32[]{:S(2)}, u32[]{:S(2)}) collective-permute-start(bf16[4,4,16,1024]{3,2,1,0:T(8,128)(2,1)S(1)} %get-tuple-element.134), channel_id=1, source_target_pairs={{0,1},{1,0},{2,3},{3,2},{4,5},{5,4},{6,7},{7,6},{8,9},{9,8},{10,11... | collective-permute-start | bytes 1572872 | tf_op jit(solution)/shard_map/ppermute | solution.py:208
  86.4 2.5 %collective-permute-start.22 = (bf16[4,4,16,1024]{3,2,1,0:T(8,128)(2,1)S(1)}, bf16[4,4,16,1024]{3,2,1,0:T(8,128)(2,1)S(1)}, u32[]{:S(2)}, u32[]{:S(2)}) collective-permute-start(bf16[4,4,16,1024]{3,2,1,0:T(8,128)(2,1)S(1)} %get-tuple-element.130), channel_id=1, source_target_pairs={{0,1},{1,0},{2,3},{3,2},{4,5},{5,4},{6,7},{7,6},{8,9},{9,8},{10,11... | collective-permute-start | bytes 1572872 | tf_op jit(solution)/shard_map/ppermute | solution.py:208
  86.8 3.6 %collective-permute-start.24 = (bf16[4,4,16,1024]{3,2,1,0:T(8,128)(2,1)S(1)}, bf16[4,4,16,1024]{3,2,1,0:T(8,128)(2,1)S(1)}, u32[]{:S(2)}, u32[]{:S(2)}) collective-permute-start(bf16[4,4,16,1024]{3,2,1,0:T(8,128)(2,1)S(1)} %get-tuple-element.132), channel_id=1, source_target_pairs={{0,1},{1,0},{2,3},{3,2},{4,5},{5,4},{6,7},{7,6},{8,9},{9,8},{10,11... | collective-permute-start | bytes 1572872 | tf_op jit(solution)/shard_map/ppermute | solution.py:208
  86.9 3.8 %collective-permute-start.21 = (bf16[4,4,16,1024]{3,2,1,0:T(8,128)(2,1)S(1)}, bf16[4,4,16,1024]{3,2,1,0:T(8,128)(2,1)S(1)}, u32[]{:S(2)}, u32[]{:S(2)}) collective-permute-start(bf16[4,4,16,1024]{3,2,1,0:T(8,128)(2,1)S(1)} %get-tuple-element.128), channel_id=1, source_target_pairs={{0,1},{1,0},{2,3},{3,2},{4,5},{5,4},{6,7},{7,6},{8,9},{9,8},{10,11... | collective-permute-start | bytes 1572872 | tf_op jit(solution)/shard_map/ppermute | solution.py:208
  89.2 7.3 %collective-permute-start.23 = (bf16[64,1024]{1,0:T(8,128)(2,1)S(1)}, bf16[64,1024]{1,0:T(8,128)(2,1)S(1)}, u32[]{:S(2)}, u32[]{:S(2)}) collective-permute-start(bf16[64,1024]{1,0:T(8,128)(2,1)S(1)} %bitcast.62), channel_id=1, source_target_pairs={{0,6},{2,4},{4,2},{6,0},{8,14},{10,12},{12,10},{14,8},{16,22},{18,... | collective-permute-start | bytes 393224 | tf_op jit(solution)/shard_map/ppermute | solution.py:205
  91.0 9.0 %collective-permute-start.30 = (bf16[64,1024]{1,0:T(8,128)(2,1)S(1)}, bf16[64,1024]{1,0:T(8,128)(2,1)S(1)}, u32[]{:S(2)}, u32[]{:S(2)}) collective-permute-start(bf16[64,1024]{1,0:T(8,128)(2,1)S(1)} %bitcast.61), channel_id=1, source_target_pairs={{0,2},{2,0},{4,6},{6,4},{8,10},{10,8},{12,14},{14,12},{16,18},{18,... | collective-permute-start | bytes 393224 | tf_op jit(solution)/shard_map/ppermute | solution.py:205
  92.8 7.2 %collective-permute-start.31 = (bf16[64,1024]{1,0:T(8,128)(2,1)S(1)}, bf16[64,1024]{1,0:T(8,128)(2,1)S(1)}, u32[]{:S(2)}, u32[]{:S(2)}) collective-permute-start(bf16[64,1024]{1,0:T(8,128)(2,1)S(1)} %bitcast.60), channel_id=1, source_target_pairs={{0,4},{2,6},{4,0},{6,2},{8,12},{10,14},{12,8},{14,10},{16,20},{18,... | collective-permute-start | bytes 393224 | tf_op jit(solution)/shard_map/ppermute | solution.py:205
  96.5 17.8 %collective-permute-start.33 = (bf16[128,1024]{1,0:T(8,128)(2,1)S(1)}, bf16[128,1024]{1,0:T(8,128)(2,1)S(1)}, u32[]{:S(2)}, u32[]{:S(2)}) collective-permute-start(bf16[128,1024]{1,0:T(8,128)(2,1)S(1)} %get-tuple-element.146), channel_id=1, source_target_pairs={{0,2},{2,0},{4,6},{6,4},{8,10},{10,8},{12,14},{14,12},{16,18},{18,... | collective-permute-start | bytes 786440 | tf_op jit(solution)/shard_map/ppermute | solution.py:205
  97.2 17.2 %collective-permute-start.34 = (bf16[128,1024]{1,0:T(8,128)(2,1)S(1)}, bf16[128,1024]{1,0:T(8,128)(2,1)S(1)}, u32[]{:S(2)}, u32[]{:S(2)}) collective-permute-start(bf16[128,1024]{1,0:T(8,128)(2,1)S(1)} %get-tuple-element.147), channel_id=1, source_target_pairs={{0,4},{2,6},{4,0},{6,2},{8,12},{10,14},{12,8},{14,10},{16,20},{18,... | collective-permute-start | bytes 786440 | tf_op jit(solution)/shard_map/ppermute | solution.py:205
  98.2 15.5 %collective-permute-start.26 = (bf16[128,1024]{1,0:T(8,128)(2,1)S(1)}, bf16[128,1024]{1,0:T(8,128)(2,1)S(1)}, u32[]{:S(2)}, u32[]{:S(2)}) collective-permute-start(bf16[128,1024]{1,0:T(8,128)(2,1)S(1)} %pad_maximum_fusion.6), channel_id=1, source_target_pairs={{0,6},{2,4},{4,2},{6,0},{8,14},{10,12},{12,10},{14,8},{16,22},{18,... | collective-permute-start | bytes 786440 | tf_op jit(solution)/shard_map/ppermute | solution.py:205
  100.3 24.5 %collective-permute-start.32 = (bf16[128,1024]{1,0:T(8,128)(2,1)S(1)}, bf16[128,1024]{1,0:T(8,128)(2,1)S(1)}, u32[]{:S(2)}, u32[]{:S(2)}) collective-permute-start(bf16[128,1024]{1,0:T(8,128)(2,1)S(1)} %combine.3.refs_18_), channel_id=1, source_target_pairs={{0,24},{2,26},{4,28},{6,30},{8,16},{10,18},{12,20},{14,22},{16,8},... | collective-permute-start | bytes 786440 | tf_op jit(solution)/shard_map/ppermute | solution.py:202
  102.9 21.7 %copy-start = (bf16[256,128]{1,0:T(8,128)(2,1)S(1)}, bf16[256,128]{1,0:T(8,128)(2,1)}, u32[]{:S(2)}) copy-start(bf16[256,128]{1,0:T(8,128)(2,1)} %get-tuple-element.78.refs_0_) | copy-start | bytes 196612
  113.7 5.0 %collective-permute-start.27 = (bf16[64,1024]{1,0:T(8,128)(2,1)S(1)}, bf16[64,1024]{1,0:T(8,128)(2,1)S(1)}, u32[]{:S(2)}, u32[]{:S(2)}) collective-permute-start(bf16[64,1024]{1,0:T(8,128)(2,1)S(1)} %bitcast.59), channel_id=1, source_target_pairs={{0,2},{2,0},{4,6},{6,4},{8,10},{10,8},{12,14},{14,12},{16,18},{18,... | collective-permute-start | bytes 393224 | tf_op jit(solution)/shard_map/ppermute | solution.py:205
  114.7 11.2 %collective-permute-start.36 = (bf16[128,1024]{1,0:T(8,128)(2,1)S(1)}, bf16[128,1024]{1,0:T(8,128)(2,1)S(1)}, u32[]{:S(2)}, u32[]{:S(2)}) collective-permute-start(bf16[128,1024]{1,0:T(8,128)(2,1)S(1)} %get-tuple-element.150), channel_id=1, source_target_pairs={{0,8},{2,10},{4,12},{6,14},{8,0},{10,2},{12,4},{14,6},{16,24},{18,... | collective-permute-start | bytes 786440 | tf_op jit(solution)/shard_map/ppermute | solution.py:202
  116.3 12.4 %collective-permute-start.35 = (bf16[128,1024]{1,0:T(8,128)(2,1)S(1)}, bf16[128,1024]{1,0:T(8,128)(2,1)S(1)}, u32[]{:S(2)}, u32[]{:S(2)}) collective-permute-start(bf16[128,1024]{1,0:T(8,128)(2,1)S(1)} %get-tuple-element.149), channel_id=1, source_target_pairs={{0,16},{2,18},{4,20},{6,22},{8,24},{10,26},{12,28},{14,30},{16,0},... | collective-permute-start | bytes 786440 | tf_op jit(solution)/shard_map/ppermute | solution.py:202
  117.2 5.1 %collective-permute-start.28 = (bf16[64,1024]{1,0:T(8,128)(2,1)S(1)}, bf16[64,1024]{1,0:T(8,128)(2,1)S(1)}, u32[]{:S(2)}, u32[]{:S(2)}) collective-permute-start(bf16[64,1024]{1,0:T(8,128)(2,1)S(1)} %bitcast.58), channel_id=1, source_target_pairs={{0,4},{2,6},{4,0},{6,2},{8,12},{10,14},{12,8},{14,10},{16,20},{18,... | collective-permute-start | bytes 393224 | tf_op jit(solution)/shard_map/ppermute | solution.py:205
  118.7 5.9 %collective-permute-start.29 = (bf16[64,1024]{1,0:T(8,128)(2,1)S(1)}, bf16[64,1024]{1,0:T(8,128)(2,1)S(1)}, u32[]{:S(2)}, u32[]{:S(2)}) collective-permute-start(bf16[64,1024]{1,0:T(8,128)(2,1)S(1)} %bitcast.57), channel_id=1, source_target_pairs={{0,6},{2,4},{4,2},{6,0},{8,14},{10,12},{12,10},{14,8},{16,22},{18,... | collective-permute-start | bytes 393224 | tf_op jit(solution)/shard_map/ppermute | solution.py:205

commit v4 on v3

--- a/solution.py
+++ b/solution.py
@@ -14,7 +14,9 @@
 F32 = jnp.float32
 BF16 = jnp.bfloat16
 VMEM_LIMIT = 32 << 20
+SMALL_LIMIT = 8 << 20
 PAYLOAD_LIMIT = 62 << 20
+ROWS_LIMIT = 16 << 20
 
 
 def outer_extent(mesh):
@@ -63,12 +65,12 @@
     lift = dot(pick, bias_in[...], ((0,), (0,)))
     out[0:rows, :] = (rows_in[0].astype(F32) + lift).astype(BF16)
     out[rows : 2 * rows, :] = rows_in[1]
-    choose_body(inner, experts_here, where, out, *refs[: inner + 1])
-
-
-def choose_body(inner, experts_here, where, *refs):
+    choose_body(inner, experts_here, 1, where, out, *refs[: inner + 1])
+
+
+def choose_body(inner, experts_here, candidates, where, *refs):
     outs = refs[-(inner + 1) :]
-    payloads = refs[: -(inner + 1)]
+    payloads = refs[:candidates]
     table_out = outs[-1]
     rows = (payloads[0].shape[0] - META) // 2
     width = payloads[0].shape[1]
@@ -106,38 +108,44 @@
         outs[m][:, width : 2 * width] = scaled[m * part : (m + 1) * part]
 
 
-def gathered(refs):
-    return jnp.concatenate([ref[...].reshape(-1, ref.shape[-1]) for ref in refs], axis=0)
-
-
-def rows_body(rounds, pieces, where, *refs):
+def gathered(refs, *part):
+    values = [ref[part] if part else ref[...] for ref in refs]
+    return jnp.concatenate([value.reshape(-1, value.shape[-1]) for value in values], axis=0)
+
+
+def rows_body(rounds, pieces, skipped, where, *refs):
     n = rounds * pieces
-    lifted, scaled = refs[:n], refs[n : 2 * n]
-    up, down, hidden_out, pre_out = refs[2 * n : 2 * n + 4]
-    outs = refs[2 * n + 4 :]
+    xs = refs[:n]
+    up, down = refs[n : n + 2]
+    hidden_out, pre_out, *outs = refs[n + 2 + skipped :]
     width = outs[0].shape[-1]
     at = [pl.multiple_of(jnp.bitwise_xor(where[0], q) * width, width) for q in range(pieces)]
 
-    def project(weight, xs):
-        total = None
+    def one(e):
+        def project(weight, low):
+            total = None
+            for q in range(pieces):
+                x = gathered(xs[q * rounds : (q + 1) * rounds], slice(None), e, slice(None), slice(low, low + width))
+                term = dot(weight[e, :, pl.ds(at[q], width)], x, ((1,), (1,)))
+                total = term if total is None else total + term
+            return total
+
+        preact = project(up, 0)
+        backprop = project(down, width)
+        s = 1.0 / (1.0 + jnp.exp(-preact))
+        hidden_out[e] = (preact * s).astype(BF16)
+        pre = (backprop * s * (1.0 + preact * (1.0 - s))).astype(BF16)
+        pre_out[e] = pre
+        turned = pre.T
         for q in range(pieces):
-            term = dot(weight[0, :, pl.ds(at[q], width)], gathered(xs[q * rounds : (q + 1) * rounds]), ((1,), (1,)))
-            total = term if total is None else total + term
-        return total
-
-    preact = project(up, lifted)
-    backprop = project(down, scaled)
-    s = 1.0 / (1.0 + jnp.exp(-preact))
-    hidden_out[0] = (preact * s).astype(BF16)
-    pre = (backprop * s * (1.0 + preact * (1.0 - s))).astype(BF16)
-    pre_out[0] = pre
-    turned = pre.T
-    for q in range(pieces):
-        part = dot(turned, up[0, :, pl.ds(at[q], width)], ((1,), (0,))).astype(BF16)
-        each = part.shape[0] // rounds
-        for r in range(rounds):
-            ref = outs[q * rounds + r]
-            ref[...] = part[r * each : (r + 1) * each].reshape(ref.shape)
+            part = dot(turned, up[e, :, pl.ds(at[q], width)], ((1,), (0,))).astype(BF16)
+            each = part.shape[0] // rounds
+            for r in range(rounds):
+                ref = outs[q * rounds + r]
+                ref[:, e, :, :] = part[r * each : (r + 1) * each].reshape(ref.shape[0], ref.shape[2], width)
+
+    for e in range(up.shape[0]):
+        one(e)
 
 
 def grads_body(rounds, pieces, where, *refs):
@@ -150,6 +158,10 @@
             x = gathered(xs[q * rounds : (q + 1) * rounds])
             grad[0, :, pl.ds(at, width)] = dot(unit[0], x, ((1,), (0,))).astype(BF16)
     flag[...] = jnp.zeros(flag.shape, F32)
+
+
+def touch_body(weight, _, out):
+    out[...] = weight[0, 0:8, 0:128].astype(F32)
 
 
 def combine_body(blocks, groups, *refs):
@@ -207,18 +219,31 @@
     def core_swap(value, q):
         return lax.ppermute(value, "expert", [(i, i ^ q) for i in range(pieces)])
 
-    def choose(candidates):
+    small = pltpu.CompilerParams(vmem_limit_bytes=SMALL_LIMIT)
+    any_place = pl.BlockSpec(memory_space=pl.ANY)
+
+    def choose(candidates, earlier=()):
         outs = pl.pallas_call(
-            functools.partial(choose_body, inner, here),
-            in_specs=[smem] + [vmem] * len(candidates),
+            functools.partial(choose_body, inner, here, len(candidates)),
+            in_specs=[smem] + [vmem] * len(candidates) + [any_place] * len(earlier),
             out_specs=[vmem] * (inner + 1),
             out_shape=chosen_shape,
-            compiler_params=params,
+            compiler_params=small,
             cost_estimate=cost(4 * plane * count * width, 6 * plane * width),
             name="choose",
-        )(where, *candidates)
+        )(where, *candidates, *earlier)
         tables.append(outs[-1])
         return outs[:-1]
+
+    def touch(weight, earlier):
+        return pl.pallas_call(
+            touch_body,
+            in_specs=[vmem, any_place],
+            out_specs=vmem,
+            out_shape=shape((8, 128), F32),
+            compiler_params=small,
+            name="touch",
+        )(weight, earlier)
 
     tables, owned = [own[-1]], []
 
@@ -251,14 +276,19 @@
         second = chained(second, first)
         far, out_mid = held([far, out_mid], second)
         third = choose((out_mid, far))
+        up_flag = touch(up_weight, third[0])
         out_far = lax.ppermute(far, "dp", outward)
         third = chained(third, second)
-        fourth = choose((out_far, mid))
+        fourth = choose((out_far, mid), (up_flag,))
+        down_flag = touch(down_weight, fourth[0])
         fourth = chained(fourth, third)
+        fourth[-1], down_flag = lax.optimization_barrier((fourth[-1], down_flag))
+        flags_in = [down_flag]
         share(fourth)
     else:
         for m in range(outer):
             share(spread(choose((across(payload, m),)) if m else own[:-1]))
+        flags_in = []
 
     rows_in = [owned[r][q] for q in range(pieces) for r in range(outer)]
     n_in = len(rows_in)
@@ -271,18 +301,15 @@
     flops = 2 * here * line * hidden_width * features
     unit_shape = (here, hidden_width, line)
     back = pl.pallas_call(
-        functools.partial(rows_body, outer, pieces),
-        grid=(here,),
-        in_specs=[smem] + lifted_spec + scaled_spec + [weight_spec, weight_spec],
-        out_specs=[unit_spec, unit_spec] + lifted_spec,
+        functools.partial(rows_body, outer, pieces, len(flags_in)),
+        in_specs=[smem] + [vmem] * (n_in + 2) + [any_place] * len(flags_in),
+        out_specs=[vmem] * (n_in + 2),
         out_shape=[shape(unit_shape, BF16)] * 2 + [shape((inner, here, CAP, width), BF16)] * n_in,
-        compiler_params=params,
+        compiler_params=pltpu.CompilerParams(vmem_limit_bytes=ROWS_LIMIT),
         cost_estimate=cost(3 * flops, 2 * weight_bytes + 3 * row_bytes),
         name="rows",
-    )(where, *rows_in, *rows_in, up_weight, down_weight)
+    )(where, *rows_in, up_weight, down_weight, *flags_in)
     hidden, pre, partial = back[0], back[1], back[2:]
-    any_place = pl.BlockSpec(memory_space=pl.ANY)
-
     def weight_grads(earlier):
         return pl.pallas_call(
             functools.partial(grads_body, outer, pieces),

time: 130 us -> 127 us (0.977)
  local copies, waits for them, and re-layouts: 0.17 us -> 9.4 us
  waiting for transfers between devices: 53.6 us -> 45 us
  Pallas kernels: 32.9 us -> 29.3 us
    unnamed x2 -> x46, local copies, waits for them, and re-layouts: 0.01 us -> 9.24 us
    ppermute x1, waiting for transfers between devices: 6.86 us -> 2.28 us  [local(): out_far = lax.ppermute(far, 'dp', outward)]
    ppermute x21, waiting for transfers between devices: 37 us -> 32.7 us  [within(): return lax.ppermute(value, 'dp', [(i, i ^ m) for i in range(outer * inner)])]
    pallas_call x4 -> x6, Pallas kernels: 18 us -> 14.1 us  [the longest x1 10.8 us: local(): pl.pallas_call(functools.partial(rows_body, outer, pieces, len(flags_in))...]
  transfers between devices with their start and end apart: 37 -> 37, of which waited for: 18 -> 17; matrix products, arithmetic and copies ran while one was open for 2% -> 2% of each run, Pallas kernels for 11% -> 12%
where the time goes in v4:
time: 127 us
  waiting for transfers between devices  45 us (35%)
  starting transfers between devices  38.8 us (31%)
  Pallas kernels  29.3 us (23%)
  local copies, waits for them, and re-layouts  9.4 us (7%)
  other arithmetic  3.12 us (2%)
    ppermute x21, waiting for transfers between devices, within(): return lax.ppermute(value, 'dp', [(i, i ^ m) for i in range(outer * inner)])  32.7 us
    ppermute x21, starting transfers between devices, within(): return lax.ppermute(value, 'dp', [(i, i ^ m) for i in range(outer * inner)])  25.1 us
    pallas_call x1, Pallas kernels, weight_grads(): pl.pallas_call(functools.partial(grads_body, outer, pieces), grid=(here,)...  11 us
    pallas_call x1, Pallas kernels, local(): pl.pallas_call(functools.partial(rows_body, outer, pieces, len(flags_in))...  10.8 us
    unnamed x46, local copies, waits for them, and re-layouts  9.24 us
    ppermute x4, starting transfers between devices, across(): lax.ppermute(value, 'dp', [(i, i ^ m * inner) for i in range(outer * inne...  8.39 us
    ppermute x4, waiting for transfers between devices, across(): lax.ppermute(value, 'dp', [(i, i ^ m * inner) for i in range(outer * inne...  4.18 us
    ppermute x8, waiting for transfers between devices, core_swap(): return lax.ppermute(value, 'expert', [(i, i ^ q) for i in range(pieces)])  3.99 us
  transfers between devices with their start and end apart: 37, of which 17 were waited for; matrix products, arithmetic and copies ran while one was open for 2% of the time, Pallas kernels for 12%

profile of v4, /device:TPU:0, one launch (start us, length us, event | category | flops | bytes accessed | tf_op | source)
XLA Modules:
  0.0 126.8 jit_solution(17877293662256404478)
XLA Ops:
  0.6 3.3 %payload.1 = (bf16[272,1024]{1,0:T(8,128)(2,1)}, bf16[64,2048]{1,0:T(8,128)(2,1)}, bf16[64,2048]{1,0:T(8,128)(2,1)}, bf16[64,2048]{1,0:T(8,128)(2,1)}, bf16[64,2...) custom-call(s32[6,128]{1,0:T(8,128)} %bitcast.61, s32[6,128]{1,0:T(8,128)} %bitcast.62, s32[1,128]{1,0:T(1,128)} %bitcast.63, ...), custom_call_target="tpu_custom_call" | custom-call | tf_op jit(solution)/shard_map/payload/pallas_call | solution.py:199
  4.0 3.1 %collective-permute-start = (bf16[272,1024]{1,0:T(8,128)(2,1)}, bf16[272,1024]{1,0:T(8,128)(2,1)S(1)}, u32[]{:S(2)}, u32[]{:S(2)}) collective-permute-start(bf16[272,1024]{1,0:T(8,128)(2,1)} %get-tuple-element.81), channel_id=1, source_target_pairs={{0,8},{2,10},{4,12},{6,14},{8,0},{10,2},{12,4},{14,6},{16,24},{18,... | collective-permute-start | bytes 1671176 | tf_op jit(solution)/shard_map/ppermute | solution.py:214
  7.8 1.6 %collective-permute-start.2 = (bf16[64,2048]{1,0:T(8,128)(2,1)}, bf16[64,2048]{1,0:T(8,128)(2,1)S(1)}, u32[]{:S(2)}, u32[]{:S(2)}) collective-permute-start(bf16[64,2048]{1,0:T(8,128)(2,1)} %get-tuple-element.82), channel_id=1, source_target_pairs={{0,2},{2,0},{4,6},{6,4},{8,10},{10,8},{12,14},{14,12},{16,18},{18,... | collective-permute-start | bytes 786440 | tf_op jit(solution)/shard_map/ppermute | solution.py:217
  9.3 1.5 %collective-permute-start.3 = (bf16[64,2048]{1,0:T(8,128)(2,1)}, bf16[64,2048]{1,0:T(8,128)(2,1)S(1)}, u32[]{:S(2)}, u32[]{:S(2)}) collective-permute-start(bf16[64,2048]{1,0:T(8,128)(2,1)} %get-tuple-element.83), channel_id=1, source_target_pairs={{0,4},{2,6},{4,0},{6,2},{8,12},{10,14},{12,8},{14,10},{16,20},{18,... | collective-permute-start | bytes 786440 | tf_op jit(solution)/shard_map/ppermute | solution.py:217
  11.3 6.0 %collective-permute-done.2 = bf16[64,2048]{1,0:T(8,128)(2,1)S(1)} collective-permute-done((bf16[64,2048]{1,0:T(8,128)(2,1)}, bf16[64,2048]{1,0:T(8,128)(2,1)S(1)}, u32[]{:S(2)}, u32[]{:S(2)}) %collective-permute-start.2) | collective-permute-done | bytes 262176 | tf_op jit(solution)/shard_map/ppermute | solution.py:217
  17.3 5.4 %collective-permute-done.3 = bf16[64,2048]{1,0:T(8,128)(2,1)S(1)} collective-permute-done((bf16[64,2048]{1,0:T(8,128)(2,1)}, bf16[64,2048]{1,0:T(8,128)(2,1)S(1)}, u32[]{:S(2)}, u32[]{:S(2)}) %collective-permute-start.3) | collective-permute-done | bytes 262176 | tf_op jit(solution)/shard_map/ppermute | solution.py:217
  22.6 0.7 collective-permute-start.5
  23.4 1.3 %collective-permute-start.6 = (bf16[272,1024]{1,0:T(8,128)(2,1)S(1)}, bf16[272,1024]{1,0:T(8,128)(2,1)S(1)}, u32[]{:S(2)}, u32[]{:S(2)}) collective-permute-start(bf16[272,1024]{1,0:T(8,128)(2,1)S(1)} %collective-permute-done.1.refs_1_), channel_id=1, source_target_pairs={{8,0},{10,2},{12,4},{14,6},{16,24},{18,26},{20,28},{22,30},{9,1},{... | collective-permute-start | bytes 1671176 | tf_op jit(solution)/shard_map/ppermute | solution.py:275
  24.8 1.1 choose.3
  25.9 1.3 %collective-permute-start.7 = (bf16[64,2048]{1,0:T(8,128)(2,1)S(1)}, bf16[64,2048]{1,0:T(8,128)(2,1)S(1)}, u32[]{:S(2)}, u32[]{:S(2)}) collective-permute-start(bf16[64,2048]{1,0:T(8,128)(2,1)S(1)} %get-tuple-element.98), channel_id=1, source_target_pairs={{0,2},{2,0},{4,6},{6,4},{8,10},{10,8},{12,14},{14,12},{16,18},{18,... | collective-permute-start | bytes 786440 | tf_op jit(solution)/shard_map/ppermute | solution.py:217
  27.1 0.8 collective-permute-start.8
  28.0 1.4 %collective-permute-start.9 = (bf16[64,2048]{1,0:T(8,128)(2,1)S(1)}, bf16[64,2048]{1,0:T(8,128)(2,1)S(1)}, u32[]{:S(2)}, u32[]{:S(2)}) collective-permute-start(bf16[64,2048]{1,0:T(8,128)(2,1)S(1)} %get-tuple-element.100), channel_id=1, source_target_pairs={{0,6},{2,4},{4,2},{6,0},{8,14},{10,12},{12,10},{14,8},{16,22},{18,... | collective-permute-start | bytes 786440 | tf_op jit(solution)/shard_map/ppermute | solution.py:217
  29.4 5.8 %collective-permute-done.7 = bf16[64,2048]{1,0:T(8,128)(2,1)S(1)} collective-permute-done((bf16[64,2048]{1,0:T(8,128)(2,1)S(1)}, bf16[64,2048]{1,0:T(8,128)(2,1)S(1)}, u32[]{:S(2)}, u32[]{:S(2)}) %collective-permute-start.7) | collective-permute-done | bytes 262176 | tf_op jit(solution)/shard_map/ppermute | solution.py:217
  35.2 4.2 %collective-permute-done.8 = bf16[64,2048]{1,0:T(8,128)(2,1)S(1)} collective-permute-done((bf16[64,2048]{1,0:T(8,128)(2,1)S(1)}, bf16[64,2048]{1,0:T(8,128)(2,1)S(1)}, u32[]{:S(2)}, u32[]{:S(2)}) %collective-permute-start.8) | collective-permute-done | bytes 262176 | tf_op jit(solution)/shard_map/ppermute | solution.py:217
  39.3 1.8 %collective-permute-done.6.refs_0_ = bf16[272,1024]{1,0:T(8,128)(2,1)S(1)} collective-permute-done((bf16[272,1024]{1,0:T(8,128)(2,1)S(1)}, bf16[272,1024]{1,0:T(8,128)(2,1)S(1)}, u32[]{:S(2)}, u32[]{:S(2)}) %collective-permute-start.6) | collective-permute-done | bytes 557088 | tf_op jit(solution)/shard_map/ppermute | solution.py:275
  41.2 1.3 %collective-permute-start.10 = (bf16[272,1024]{1,0:T(8,128)(2,1)S(1)}, bf16[272,1024]{1,0:T(8,128)(2,1)S(1)}, u32[]{:S(2)}, u32[]{:S(2)}) collective-permute-start(bf16[272,1024]{1,0:T(8,128)(2,1)S(1)} %collective-permute-done.5.refs_1_), channel_id=1, source_target_pairs={{8,0},{10,2},{12,4},{14,6},{16,24},{18,26},{20,28},{22,30},{9,1},{... | collective-permute-start | bytes 1671176 | tf_op jit(solution)/shard_map/ppermute | solution.py:280
  42.4 1.1 choose.4
  43.5 1.5 %collective-permute-start.11 = (bf16[64,2048]{1,0:T(8,128)(2,1)S(1)}, bf16[64,2048]{1,0:T(8,128)(2,1)S(1)}, u32[]{:S(2)}, u32[]{:S(2)}) collective-permute-start(bf16[64,2048]{1,0:T(8,128)(2,1)S(1)} %get-tuple-element.118), channel_id=1, source_target_pairs={{0,2},{2,0},{4,6},{6,4},{8,10},{10,8},{12,14},{14,12},{16,18},{18,... | collective-permute-start | bytes 786440 | tf_op jit(solution)/shard_map/ppermute | solution.py:217
  45.0 1.2 collective-permute-start.12
  46.2 0.9 collective-permute-start.13
  47.1 1.0 pad_maximum_fusion
  48.2 4.6 %copy-done = bf16[4,704,2048]{2,1,0:T(8,128)(2,1)S(1)} copy-done((bf16[4,704,2048]{2,1,0:T(8,128)(2,1)S(1)}, bf16[4,704,2048]{2,1,0:T(8,128)(2,1)}, u32[]{:S(2)}) %copy-start) | copy-done | bytes 11534360
  52.8 2.3 %collective-permute-done.10.refs_0_ = bf16[272,1024]{1,0:T(8,128)(2,1)S(1)} collective-permute-done((bf16[272,1024]{1,0:T(8,128)(2,1)S(1)}, bf16[272,1024]{1,0:T(8,128)(2,1)S(1)}, u32[]{:S(2)}, u32[]{:S(2)}) %collective-permute-start.10) | collective-permute-done | bytes 557088 | tf_op jit(solution)/shard_map/ppermute | solution.py:280
  55.1 1.1 choose.5
  56.3 2.2 %collective-permute-start.16 = (bf16[64,2048]{1,0:T(8,128)(2,1)S(1)}, bf16[64,2048]{1,0:T(8,128)(2,1)S(1)}, u32[]{:S(2)}, u32[]{:S(2)}) collective-permute-start(bf16[64,2048]{1,0:T(8,128)(2,1)S(1)} %get-tuple-element.128), channel_id=1, source_target_pairs={{0,6},{2,4},{4,2},{6,0},{8,14},{10,12},{12,10},{14,8},{16,22},{18,... | collective-permute-start | bytes 786440 | tf_op jit(solution)/shard_map/ppermute | solution.py:217
  58.5 1.2 collective-permute-start.15
  60.0 4.6 %copy-done.1 = bf16[4,704,2048]{2,1,0:T(8,128)(2,1)S(1)} copy-done((bf16[4,704,2048]{2,1,0:T(8,128)(2,1)S(1)}, bf16[4,704,2048]{2,1,0:T(8,128)(2,1)}, u32[]{:S(2)}) %copy-start.1) | copy-done | bytes 11534360
  64.7 1.5 %collective-permute-done.16 = bf16[64,2048]{1,0:T(8,128)(2,1)S(1)} collective-permute-done((bf16[64,2048]{1,0:T(8,128)(2,1)S(1)}, bf16[64,2048]{1,0:T(8,128)(2,1)S(1)}, u32[]{:S(2)}, u32[]{:S(2)}) %collective-permute-start.16) | collective-permute-done | bytes 262176 | tf_op jit(solution)/shard_map/ppermute | solution.py:217
  66.2 2.7 %collective-permute-done.15 = bf16[64,2048]{1,0:T(8,128)(2,1)S(1)} collective-permute-done((bf16[64,2048]{1,0:T(8,128)(2,1)S(1)}, bf16[64,2048]{1,0:T(8,128)(2,1)S(1)}, u32[]{:S(2)}, u32[]{:S(2)}) %collective-permute-start.15) | collective-permute-done | bytes 262176 | tf_op jit(solution)/shard_map/ppermute | solution.py:217
  69.1 2.6 %collective-permute-done.20.refs_7_.refs_15_ = bf16[4,4,16,2048]{3,2,1,0:T(8,128)(2,1)S(1)} collective-permute-done((bf16[4,4,16,2048]{3,2,1,0:T(8,128)(2,1)S(1)}, bf16[4,4,16,2048]{3,2,1,0:T(8,128)(2,1)S(1)}, u32[]{:S(2)}, u32[]{:S(2)}) %collective-permute-start.20) | collective-permute-done | bytes 1048608 | tf_op jit(solution)/shard_map/ppermute | solution.py:220
  71.8 10.8 %rows.1 = (bf16[4,704,256]{2,1,0:T(8,128)(2,1)S(1)}, bf16[4,704,256]{2,1,0:T(8,128)(2,1)S(1)}, bf16[4,4,16,1024]{3,2,1,0:T(8,128)(2,1)S(1)}, bf16[4,4,16,1024]{3...) custom-call(s32[4]{0:T(128)S(1)} %pad_add_fusion.where, ...), custom_call_target="tpu_custom_call" | custom-call | flops 8858370048 | bytes 35651584 | tf_op jit(solution)/shard_map/rows/pallas_call | solution.py:303
  83.8 0.9 collective-permute-done.25
  85.7 2.2 %collective-permute-start.23 = (bf16[64,1024]{1,0:T(8,128)(2,1)S(1)}, bf16[64,1024]{1,0:T(8,128)(2,1)S(1)}, u32[]{:S(2)}, u32[]{:S(2)}) collective-permute-start(bf16[64,1024]{1,0:T(8,128)(2,1)S(1)} %bitcast.60), channel_id=1, source_target_pairs={{0,6},{2,4},{4,2},{6,0},{8,14},{10,12},{12,10},{14,8},{16,22},{18,... | collective-permute-start | bytes 393224 | tf_op jit(solution)/shard_map/ppermute | solution.py:217
  89.1 0.9 collective-permute-start.31
  90.1 2.6 %collective-permute-done.23.refs_4_ = bf16[64,1024]{1,0:T(8,128)(2,1)S(1)} collective-permute-done((bf16[64,1024]{1,0:T(8,128)(2,1)S(1)}, bf16[64,1024]{1,0:T(8,128)(2,1)S(1)}, u32[]{:S(2)}, u32[]{:S(2)}) %collective-permute-start.23) | collective-permute-done | bytes 131104 | tf_op jit(solution)/shard_map/ppermute | solution.py:217
  92.6 2.2 %collective-permute-start.33 = (bf16[128,1024]{1,0:T(8,128)(2,1)S(1)}, bf16[128,1024]{1,0:T(8,128)(2,1)S(1)}, u32[]{:S(2)}, u32[]{:S(2)}) collective-permute-start(bf16[128,1024]{1,0:T(8,128)(2,1)S(1)} %get-tuple-element.150), channel_id=1, source_target_pairs={{0,2},{2,0},{4,6},{6,4},{8,10},{10,8},{12,14},{14,12},{16,18},{18,... | collective-permute-start | bytes 786440 | tf_op jit(solution)/shard_map/ppermute | solution.py:217
  94.8 0.9 collective-permute-start.34
  96.6 2.6 %collective-permute-start.32 = (bf16[128,1024]{1,0:T(8,128)(2,1)S(1)}, bf16[128,1024]{1,0:T(8,128)(2,1)S(1)}, u32[]{:S(2)}, u32[]{:S(2)}) collective-permute-start(bf16[128,1024]{1,0:T(8,128)(2,1)S(1)} %combine.3.refs_18_), channel_id=1, source_target_pairs={{0,24},{2,26},{4,28},{6,30},{8,16},{10,18},{12,20},{14,22},{16,8},... | collective-permute-start | bytes 786440 | tf_op jit(solution)/shard_map/ppermute | solution.py:214
  99.2 11.0 %weight_grads.1 = (bf16[4,704,2048]{2,1,0:T(8,128)(2,1)}, bf16[4,704,2048]{2,1,0:T(8,128)(2,1)}, f32[8,128]{1,0:T(8,128)S(1)}) custom-call(s32[4]{0:T(128)S(1)} %pad_add_fusion.where, bf16[4,4,16,2048]{3,2,1,0:T(8,128)(2,1)S(1)} %bitcast.31, bf16[4,4,16,2048]{3,2,1,0:T(8,128)(2,1)S(1)} %bitcast.35, bf16[4,4,16,2048]{3,2,1,0:T(8,128)(2,1)S(1)} %bitcast.39, ...), custom_call_target="tpu_custom_call" | custom-call | flops 5905580032 | bytes 31457280 | tf_op jit(solution)/shard_map/weight_grads/pallas_call | solution.py:314
  110.2 1.2 collective-permute-start.27
  111.8 2.2 %collective-permute-start.36 = (bf16[128,1024]{1,0:T(8,128)(2,1)S(1)}, bf16[128,1024]{1,0:T(8,128)(2,1)S(1)}, u32[]{:S(2)}, u32[]{:S(2)}) collective-permute-start(bf16[128,1024]{1,0:T(8,128)(2,1)S(1)} %get-tuple-element.154), channel_id=1, source_target_pairs={{0,8},{2,10},{4,12},{6,14},{8,0},{10,2},{12,4},{14,6},{16,24},{18,... | collective-permute-start | bytes 786440 | tf_op jit(solution)/shard_map/ppermute | solution.py:214
  114.5 1.0 collective-permute-start.28
  115.5 1.3 %collective-permute-start.29 = (bf16[64,1024]{1,0:T(8,128)(2,1)S(1)}, bf16[64,1024]{1,0:T(8,128)(2,1)S(1)}, u32[]{:S(2)}, u32[]{:S(2)}) collective-permute-start(bf16[64,1024]{1,0:T(8,128)(2,1)S(1)} %bitcast.55), channel_id=1, source_target_pairs={{0,6},{2,4},{4,2},{6,0},{8,14},{10,12},{12,10},{14,8},{16,22},{18,... | collective-permute-start | bytes 393224 | tf_op jit(solution)/shard_map/ppermute | solution.py:217
  116.9 2.6 %collective-permute-done.28.refs_3_ = bf16[64,1024]{1,0:T(8,128)(2,1)S(1)} collective-permute-done((bf16[64,1024]{1,0:T(8,128)(2,1)S(1)}, bf16[64,1024]{1,0:T(8,128)(2,1)S(1)}, u32[]{:S(2)}, u32[]{:S(2)}) %collective-permute-start.28) | collective-permute-done | bytes 131104 | tf_op jit(solution)/shard_map/ppermute | solution.py:217
  119.5 1.9 %collective-permute-done.29.refs_4_ = bf16[64,1024]{1,0:T(8,128)(2,1)S(1)} collective-permute-done((bf16[64,1024]{1,0:T(8,128)(2,1)S(1)}, bf16[64,1024]{1,0:T(8,128)(2,1)S(1)}, u32[]{:S(2)}, u32[]{:S(2)}) %collective-permute-start.29) | collective-permute-done | bytes 131104 | tf_op jit(solution)/shard_map/ppermute | solution.py:217
  121.7 0.8 collective-permute-done.36
  122.5 3.4 %collective-permute-done.35 = bf16[128,1024]{1,0:T(8,128)(2,1)S(1)} collective-permute-done((bf16[128,1024]{1,0:T(8,128)(2,1)S(1)}, bf16[128,1024]{1,0:T(8,128)(2,1)S(1)}, u32[]{:S(2)}, u32[]{:S(2)}) %collective-permute-start.35) | collective-permute-done | bytes 262176 | tf_op jit(solution)/shard_map/ppermute | solution.py:214
  125.9 0.9 convert_add_fusion
  (101 shorter events, 7.3 us)
Async XLA Ops:
  4.0 18.7 %collective-permute-start = (bf16[272,1024]{1,0:T(8,128)(2,1)}, bf16[272,1024]{1,0:T(8,128)(2,1)S(1)}, u32[]{:S(2)}, u32[]{:S(2)}) collective-permute-start(bf16[272,1024]{1,0:T(8,128)(2,1)} %get-tuple-element.81), channel_id=1, source_target_pairs={{0,8},{2,10},{4,12},{6,14},{8,0},{10,2},{12,4},{14,6},{16,24},{18,... | collective-permute-start | bytes 1671176 | tf_op jit(solution)/shard_map/ppermute | solution.py:214
  7.1 15.6 %collective-permute-start.1 = (bf16[272,1024]{1,0:T(8,128)(2,1)}, bf16[272,1024]{1,0:T(8,128)(2,1)S(1)}, u32[]{:S(2)}, u32[]{:S(2)}) collective-permute-start(bf16[272,1024]{1,0:T(8,128)(2,1)} %get-tuple-element.81), channel_id=1, source_target_pairs={{8,16},{10,18},{12,20},{14,22},{16,8},{18,10},{20,12},{22,14},{9,1... | collective-permute-start | bytes 1671176 | tf_op jit(solution)/shard_map/ppermute | solution.py:270
  7.8 9.5 %collective-permute-start.2 = (bf16[64,2048]{1,0:T(8,128)(2,1)}, bf16[64,2048]{1,0:T(8,128)(2,1)S(1)}, u32[]{:S(2)}, u32[]{:S(2)}) collective-permute-start(bf16[64,2048]{1,0:T(8,128)(2,1)} %get-tuple-element.82), channel_id=1, source_target_pairs={{0,2},{2,0},{4,6},{6,4},{8,10},{10,8},{12,14},{14,12},{16,18},{18,... | collective-permute-start | bytes 786440 | tf_op jit(solution)/shard_map/ppermute | solution.py:217
  9.3 13.3 %collective-permute-start.3 = (bf16[64,2048]{1,0:T(8,128)(2,1)}, bf16[64,2048]{1,0:T(8,128)(2,1)S(1)}, u32[]{:S(2)}, u32[]{:S(2)}) collective-permute-start(bf16[64,2048]{1,0:T(8,128)(2,1)} %get-tuple-element.83), channel_id=1, source_target_pairs={{0,4},{2,6},{4,0},{6,2},{8,12},{10,14},{12,8},{14,10},{16,20},{18,... | collective-permute-start | bytes 786440 | tf_op jit(solution)/shard_map/ppermute | solution.py:217
  10.8 11.8 %collective-permute-start.4 = (bf16[64,2048]{1,0:T(8,128)(2,1)}, bf16[64,2048]{1,0:T(8,128)(2,1)S(1)}, u32[]{:S(2)}, u32[]{:S(2)}) collective-permute-start(bf16[64,2048]{1,0:T(8,128)(2,1)} %get-tuple-element.84), channel_id=1, source_target_pairs={{0,6},{2,4},{4,2},{6,0},{8,14},{10,12},{12,10},{14,8},{16,22},{18,... | collective-permute-start | bytes 786440 | tf_op jit(solution)/shard_map/ppermute | solution.py:217
  22.6 16.7 %collective-permute-start.5 = (bf16[272,1024]{1,0:T(8,128)(2,1)S(1)}, bf16[272,1024]{1,0:T(8,128)(2,1)S(1)}, u32[]{:S(2)}, u32[]{:S(2)}) collective-permute-start(bf16[272,1024]{1,0:T(8,128)(2,1)S(1)} %collective-permute-done.refs_0_), channel_id=1, source_target_pairs={{8,16},{10,18},{12,20},{14,22},{16,8},{18,10},{20,12},{22,14},{9,1... | collective-permute-start | bytes 1671176 | tf_op jit(solution)/shard_map/ppermute | solution.py:274
  23.4 17.8 %collective-permute-start.6 = (bf16[272,1024]{1,0:T(8,128)(2,1)S(1)}, bf16[272,1024]{1,0:T(8,128)(2,1)S(1)}, u32[]{:S(2)}, u32[]{:S(2)}) collective-permute-start(bf16[272,1024]{1,0:T(8,128)(2,1)S(1)} %collective-permute-done.1.refs_1_), channel_id=1, source_target_pairs={{8,0},{10,2},{12,4},{14,6},{16,24},{18,26},{20,28},{22,30},{9,1},{... | collective-permute-start | bytes 1671176 | tf_op jit(solution)/shard_map/ppermute | solution.py:275
  25.9 9.3 %collective-permute-start.7 = (bf16[64,2048]{1,0:T(8,128)(2,1)S(1)}, bf16[64,2048]{1,0:T(8,128)(2,1)S(1)}, u32[]{:S(2)}, u32[]{:S(2)}) collective-permute-start(bf16[64,2048]{1,0:T(8,128)(2,1)S(1)} %get-tuple-element.98), channel_id=1, source_target_pairs={{0,2},{2,0},{4,6},{6,4},{8,10},{10,8},{12,14},{14,12},{16,18},{18,... | collective-permute-start | bytes 786440 | tf_op jit(solution)/shard_map/ppermute | solution.py:217
  27.1 12.2 %collective-permute-start.8 = (bf16[64,2048]{1,0:T(8,128)(2,1)S(1)}, bf16[64,2048]{1,0:T(8,128)(2,1)S(1)}, u32[]{:S(2)}, u32[]{:S(2)}) collective-permute-start(bf16[64,2048]{1,0:T(8,128)(2,1)S(1)} %get-tuple-element.99), channel_id=1, source_target_pairs={{0,4},{2,6},{4,0},{6,2},{8,12},{10,14},{12,8},{14,10},{16,20},{18,... | collective-permute-start | bytes 786440 | tf_op jit(solution)/shard_map/ppermute | solution.py:217
  28.0 11.4 %collective-permute-start.9 = (bf16[64,2048]{1,0:T(8,128)(2,1)S(1)}, bf16[64,2048]{1,0:T(8,128)(2,1)S(1)}, u32[]{:S(2)}, u32[]{:S(2)}) collective-permute-start(bf16[64,2048]{1,0:T(8,128)(2,1)S(1)} %get-tuple-element.100), channel_id=1, source_target_pairs={{0,6},{2,4},{4,2},{6,0},{8,14},{10,12},{12,10},{14,8},{16,22},{18,... | collective-permute-start | bytes 786440 | tf_op jit(solution)/shard_map/ppermute | solution.py:217
  41.2 13.9 %collective-permute-start.10 = (bf16[272,1024]{1,0:T(8,128)(2,1)S(1)}, bf16[272,1024]{1,0:T(8,128)(2,1)S(1)}, u32[]{:S(2)}, u32[]{:S(2)}) collective-permute-start(bf16[272,1024]{1,0:T(8,128)(2,1)S(1)} %collective-permute-done.5.refs_1_), channel_id=1, source_target_pairs={{8,0},{10,2},{12,4},{14,6},{16,24},{18,26},{20,28},{22,30},{9,1},{... | collective-permute-start | bytes 1671176 | tf_op jit(solution)/shard_map/ppermute | solution.py:280
  43.5 12.6 %collective-permute-start.11 = (bf16[64,2048]{1,0:T(8,128)(2,1)S(1)}, bf16[64,2048]{1,0:T(8,128)(2,1)S(1)}, u32[]{:S(2)}, u32[]{:S(2)}) collective-permute-start(bf16[64,2048]{1,0:T(8,128)(2,1)S(1)} %get-tuple-element.118), channel_id=1, source_target_pairs={{0,2},{2,0},{4,6},{6,4},{8,10},{10,8},{12,14},{14,12},{16,18},{18,... | collective-permute-start | bytes 786440 | tf_op jit(solution)/shard_map/ppermute | solution.py:217
  45.0 11.3 %collective-permute-start.12 = (bf16[64,2048]{1,0:T(8,128)(2,1)S(1)}, bf16[64,2048]{1,0:T(8,128)(2,1)S(1)}, u32[]{:S(2)}, u32[]{:S(2)}) collective-permute-start(bf16[64,2048]{1,0:T(8,128)(2,1)S(1)} %get-tuple-element.119), channel_id=1, source_target_pairs={{0,4},{2,6},{4,0},{6,2},{8,12},{10,14},{12,8},{14,10},{16,20},{18,... | collective-permute-start | bytes 786440 | tf_op jit(solution)/shard_map/ppermute | solution.py:217
  46.2 10.1 %collective-permute-start.13 = (bf16[64,2048]{1,0:T(8,128)(2,1)S(1)}, bf16[64,2048]{1,0:T(8,128)(2,1)S(1)}, u32[]{:S(2)}, u32[]{:S(2)}) collective-permute-start(bf16[64,2048]{1,0:T(8,128)(2,1)S(1)} %get-tuple-element.120), channel_id=1, source_target_pairs={{0,6},{2,4},{4,2},{6,0},{8,14},{10,12},{12,10},{14,8},{16,22},{18,... | collective-permute-start | bytes 786440 | tf_op jit(solution)/shard_map/ppermute | solution.py:217
  48.1 23.6 %copy-start.3 = (bf16[256,2048]{1,0:T(8,128)(2,1)}, bf16[256,2048]{1,0:T(8,128)(2,1)S(1)}, u32[]{:S(2)}) copy-start(bf16[256,2048]{1,0:T(8,128)(2,1)S(1)} %pad_maximum_fusion) | copy-start | bytes 3145732
  48.1 21.0 %collective-permute-start.17 = (bf16[4,4,16,2048]{3,2,1,0:T(8,128)(2,1)S(1)}, bf16[4,4,16,2048]{3,2,1,0:T(8,128)(2,1)S(1)}, u32[]{:S(2)}, u32[]{:S(2)}) collective-permute-start(bf16[4,4,16,2048]{3,2,1,0:T(8,128)(2,1)S(1)} %bitcast.29), channel_id=1, source_target_pairs={{0,1},{1,0},{2,3},{3,2},{4,5},{5,4},{6,7},{7,6},{8,9},{9,8},{10,11... | collective-permute-start | bytes 3145736 | tf_op jit(solution)/shard_map/ppermute | solution.py:220
  52.8 19.0 %slice-start = ((s8[11534336]{0:T(1024)(128)(4,1)}), s8[4194304]{0:T(1024)(128)(4,1)S(1)}, s32[]{:S(2)}) async-start(s8[11534336]{0:T(1024)(128)(4,1)} %bitcast.27), calls=%async_computation | async-start | bytes 8388608
  52.8 19.0 %slice-start.1 = ((s8[11534336]{0:T(1024)(128)(4,1)}), s8[4194304]{0:T(1024)(128)(4,1)S(1)}, s32[]{:S(2)}) async-start(s8[11534336]{0:T(1024)(128)(4,1)} %bitcast.27), calls=%async_computation.1 | async-start | bytes 8388608
  56.3 9.9 %collective-permute-start.16 = (bf16[64,2048]{1,0:T(8,128)(2,1)S(1)}, bf16[64,2048]{1,0:T(8,128)(2,1)S(1)}, u32[]{:S(2)}, u32[]{:S(2)}) collective-permute-start(bf16[64,2048]{1,0:T(8,128)(2,1)S(1)} %get-tuple-element.128), channel_id=1, source_target_pairs={{0,6},{2,4},{4,2},{6,0},{8,14},{10,12},{12,10},{14,8},{16,22},{18,... | collective-permute-start | bytes 786440 | tf_op jit(solution)/shard_map/ppermute | solution.py:217
  58.5 10.4 %collective-permute-start.15 = (bf16[64,2048]{1,0:T(8,128)(2,1)S(1)}, bf16[64,2048]{1,0:T(8,128)(2,1)S(1)}, u32[]{:S(2)}, u32[]{:S(2)}) collective-permute-start(bf16[64,2048]{1,0:T(8,128)(2,1)S(1)} %get-tuple-element.127), channel_id=1, source_target_pairs={{0,4},{2,6},{4,0},{6,2},{8,12},{10,14},{12,8},{14,10},{16,20},{18,... | collective-permute-start | bytes 786440 | tf_op jit(solution)/shard_map/ppermute | solution.py:217
  59.7 9.2 %collective-permute-start.14 = (bf16[64,2048]{1,0:T(8,128)(2,1)S(1)}, bf16[64,2048]{1,0:T(8,128)(2,1)S(1)}, u32[]{:S(2)}, u32[]{:S(2)}) collective-permute-start(bf16[64,2048]{1,0:T(8,128)(2,1)S(1)} %get-tuple-element.126), channel_id=1, source_target_pairs={{0,2},{2,0},{4,6},{6,4},{8,10},{10,8},{12,14},{14,12},{16,18},{18,... | collective-permute-start | bytes 786440 | tf_op jit(solution)/shard_map/ppermute | solution.py:217
  59.9 11.8 %copy-start.5 = (bf16[256,2048]{1,0:T(8,128)(2,1)}, bf16[256,2048]{1,0:T(8,128)(2,1)S(1)}, u32[]{:S(2)}) copy-start(bf16[256,2048]{1,0:T(8,128)(2,1)S(1)} %pad_maximum_fusion.1) | copy-start | bytes 3145732
  59.9 9.2 %collective-permute-start.18 = (bf16[4,4,16,2048]{3,2,1,0:T(8,128)(2,1)S(1)}, bf16[4,4,16,2048]{3,2,1,0:T(8,128)(2,1)S(1)}, u32[]{:S(2)}, u32[]{:S(2)}) collective-permute-start(bf16[4,4,16,2048]{3,2,1,0:T(8,128)(2,1)S(1)} %bitcast.33), channel_id=1, source_target_pairs={{0,1},{1,0},{2,3},{3,2},{4,5},{5,4},{6,7},{7,6},{8,9},{9,8},{10,11... | collective-permute-start | bytes 3145736 | tf_op jit(solution)/shard_map/ppermute | solution.py:220
  64.7 18.0 %copy-start.7 = (bf16[256,2048]{1,0:T(8,128)(2,1)}, bf16[256,2048]{1,0:T(8,128)(2,1)S(1)}, u32[]{:S(2)}) copy-start(bf16[256,2048]{1,0:T(8,128)(2,1)S(1)} %pad_maximum_fusion.2) | copy-start | bytes 3145732
  66.2 2.9 %collective-permute-start.19 = (bf16[4,4,16,2048]{3,2,1,0:T(8,128)(2,1)S(1)}, bf16[4,4,16,2048]{3,2,1,0:T(8,128)(2,1)S(1)}, u32[]{:S(2)}, u32[]{:S(2)}) collective-permute-start(bf16[4,4,16,2048]{3,2,1,0:T(8,128)(2,1)S(1)} %bitcast.37), channel_id=1, source_target_pairs={{0,1},{1,0},{2,3},{3,2},{4,5},{5,4},{6,7},{7,6},{8,9},{9,8},{10,11... | collective-permute-start | bytes 3145736 | tf_op jit(solution)/shard_map/ppermute | solution.py:220
  69.0 13.6 %copy-start.9 = (bf16[256,2048]{1,0:T(8,128)(2,1)}, bf16[256,2048]{1,0:T(8,128)(2,1)S(1)}, u32[]{:S(2)}) copy-start(bf16[256,2048]{1,0:T(8,128)(2,1)S(1)} %pad_maximum_fusion.3) | copy-start | bytes 3145732
  69.0 2.7 %collective-permute-start.20 = (bf16[4,4,16,2048]{3,2,1,0:T(8,128)(2,1)S(1)}, bf16[4,4,16,2048]{3,2,1,0:T(8,128)(2,1)S(1)}, u32[]{:S(2)}, u32[]{:S(2)}) collective-permute-start(bf16[4,4,16,2048]{3,2,1,0:T(8,128)(2,1)S(1)} %bitcast.41), channel_id=1, source_target_pairs={{0,1},{1,0},{2,3},{3,2},{4,5},{5,4},{6,7},{7,6},{8,9},{9,8},{10,11... | collective-permute-start | bytes 3145736 | tf_op jit(solution)/shard_map/ppermute | solution.py:220
  69.1 13.6 %copy-start.12 = (bf16[4,4,16,2048]{3,2,1,0:T(8,128)(2,1)}, bf16[4,4,16,2048]{3,2,1,0:T(8,128)(2,1)S(1)}, u32[]{:S(2)}) copy-start(bf16[4,4,16,2048]{3,2,1,0:T(8,128)(2,1)S(1)} %collective-permute-done.17.refs_4_.refs_12_) | copy-start | bytes 3145732
  69.1 13.5 %copy-start.14 = (bf16[4,4,16,2048]{3,2,1,0:T(8,128)(2,1)}, bf16[4,4,16,2048]{3,2,1,0:T(8,128)(2,1)S(1)}, u32[]{:S(2)}) copy-start(bf16[4,4,16,2048]{3,2,1,0:T(8,128)(2,1)S(1)} %collective-permute-done.18.refs_5_.refs_13_) | copy-start | bytes 3145732
  69.1 13.5 %copy-start.16 = (bf16[4,4,16,2048]{3,2,1,0:T(8,128)(2,1)}, bf16[4,4,16,2048]{3,2,1,0:T(8,128)(2,1)S(1)}, u32[]{:S(2)}) copy-start(bf16[4,4,16,2048]{3,2,1,0:T(8,128)(2,1)S(1)} %collective-permute-done.19.refs_6_.refs_14_) | copy-start | bytes 3145732
  82.7 2.0 %collective-permute-start.25 = (bf16[4,4,16,1024]{3,2,1,0:T(8,128)(2,1)S(1)}, bf16[4,4,16,1024]{3,2,1,0:T(8,128)(2,1)S(1)}, u32[]{:S(2)}, u32[]{:S(2)}) collective-permute-start(bf16[4,4,16,1024]{3,2,1,0:T(8,128)(2,1)S(1)} %get-tuple-element.138), channel_id=1, source_target_pairs={{0,1},{1,0},{2,3},{3,2},{4,5},{5,4},{6,7},{7,6},{8,9},{9,8},{10,11... | collective-permute-start | bytes 1572872 | tf_op jit(solution)/shard_map/ppermute | solution.py:220
  82.9 2.5 %collective-permute-start.22 = (bf16[4,4,16,1024]{3,2,1,0:T(8,128)(2,1)S(1)}, bf16[4,4,16,1024]{3,2,1,0:T(8,128)(2,1)S(1)}, u32[]{:S(2)}, u32[]{:S(2)}) collective-permute-start(bf16[4,4,16,1024]{3,2,1,0:T(8,128)(2,1)S(1)} %get-tuple-element.134), channel_id=1, source_target_pairs={{0,1},{1,0},{2,3},{3,2},{4,5},{5,4},{6,7},{7,6},{8,9},{9,8},{10,11... | collective-permute-start | bytes 1572872 | tf_op jit(solution)/shard_map/ppermute | solution.py:220
  83.3 4.6 %collective-permute-start.24 = (bf16[4,4,16,1024]{3,2,1,0:T(8,128)(2,1)S(1)}, bf16[4,4,16,1024]{3,2,1,0:T(8,128)(2,1)S(1)}, u32[]{:S(2)}, u32[]{:S(2)}) collective-permute-start(bf16[4,4,16,1024]{3,2,1,0:T(8,128)(2,1)S(1)} %get-tuple-element.136), channel_id=1, source_target_pairs={{0,1},{1,0},{2,3},{3,2},{4,5},{5,4},{6,7},{7,6},{8,9},{9,8},{10,11... | collective-permute-start | bytes 1572872 | tf_op jit(solution)/shard_map/ppermute | solution.py:220
  83.4 4.8 %collective-permute-start.21 = (bf16[4,4,16,1024]{3,2,1,0:T(8,128)(2,1)S(1)}, bf16[4,4,16,1024]{3,2,1,0:T(8,128)(2,1)S(1)}, u32[]{:S(2)}, u32[]{:S(2)}) collective-permute-start(bf16[4,4,16,1024]{3,2,1,0:T(8,128)(2,1)S(1)} %get-tuple-element.132), channel_id=1, source_target_pairs={{0,1},{1,0},{2,3},{3,2},{4,5},{5,4},{6,7},{7,6},{8,9},{9,8},{10,11... | collective-permute-start | bytes 1572872 | tf_op jit(solution)/shard_map/ppermute | solution.py:220
  85.6 13.5 %copy-start.19 = (bf16[4,4,16,2048]{3,2,1,0:T(8,128)(2,1)S(1)}, bf16[4,4,16,2048]{3,2,1,0:T(8,128)(2,1)}, u32[]{:S(2)}) copy-start(bf16[4,4,16,2048]{3,2,1,0:T(8,128)(2,1)} %copy-done.18) | copy-start | bytes 3145732
  85.7 7.0 %collective-permute-start.23 = (bf16[64,1024]{1,0:T(8,128)(2,1)S(1)}, bf16[64,1024]{1,0:T(8,128)(2,1)S(1)}, u32[]{:S(2)}, u32[]{:S(2)}) collective-permute-start(bf16[64,1024]{1,0:T(8,128)(2,1)S(1)} %bitcast.60), channel_id=1, source_target_pairs={{0,6},{2,4},{4,2},{6,0},{8,14},{10,12},{12,10},{14,8},{16,22},{18,... | collective-permute-start | bytes 393224 | tf_op jit(solution)/shard_map/ppermute | solution.py:217
  88.5 7.8 %collective-permute-start.30 = (bf16[64,1024]{1,0:T(8,128)(2,1)S(1)}, bf16[64,1024]{1,0:T(8,128)(2,1)S(1)}, u32[]{:S(2)}, u32[]{:S(2)}) collective-permute-start(bf16[64,1024]{1,0:T(8,128)(2,1)S(1)} %bitcast.59), channel_id=1, source_target_pairs={{0,2},{2,0},{4,6},{6,4},{8,10},{10,8},{12,14},{14,12},{16,18},{18,... | collective-permute-start | bytes 393224 | tf_op jit(solution)/shard_map/ppermute | solution.py:217
  89.1 7.2 %collective-permute-start.31 = (bf16[64,1024]{1,0:T(8,128)(2,1)S(1)}, bf16[64,1024]{1,0:T(8,128)(2,1)S(1)}, u32[]{:S(2)}, u32[]{:S(2)}) collective-permute-start(bf16[64,1024]{1,0:T(8,128)(2,1)S(1)} %bitcast.58), channel_id=1, source_target_pairs={{0,4},{2,6},{4,0},{6,2},{8,12},{10,14},{12,8},{14,10},{16,20},{18,... | collective-permute-start | bytes 393224 | tf_op jit(solution)/shard_map/ppermute | solution.py:217
  92.6 18.8 %collective-permute-start.33 = (bf16[128,1024]{1,0:T(8,128)(2,1)S(1)}, bf16[128,1024]{1,0:T(8,128)(2,1)S(1)}, u32[]{:S(2)}, u32[]{:S(2)}) collective-permute-start(bf16[128,1024]{1,0:T(8,128)(2,1)S(1)} %get-tuple-element.150), channel_id=1, source_target_pairs={{0,2},{2,0},{4,6},{6,4},{8,10},{10,8},{12,14},{14,12},{16,18},{18,... | collective-permute-start | bytes 786440 | tf_op jit(solution)/shard_map/ppermute | solution.py:217
  94.8 16.6 %collective-permute-start.34 = (bf16[128,1024]{1,0:T(8,128)(2,1)S(1)}, bf16[128,1024]{1,0:T(8,128)(2,1)S(1)}, u32[]{:S(2)}, u32[]{:S(2)}) collective-permute-start(bf16[128,1024]{1,0:T(8,128)(2,1)S(1)} %get-tuple-element.151), channel_id=1, source_target_pairs={{0,4},{2,6},{4,0},{6,2},{8,12},{10,14},{12,8},{14,10},{16,20},{18,... | collective-permute-start | bytes 786440 | tf_op jit(solution)/shard_map/ppermute | solution.py:217
  95.7 14.5 %collective-permute-start.26 = (bf16[128,1024]{1,0:T(8,128)(2,1)S(1)}, bf16[128,1024]{1,0:T(8,128)(2,1)S(1)}, u32[]{:S(2)}, u32[]{:S(2)}) collective-permute-start(bf16[128,1024]{1,0:T(8,128)(2,1)S(1)} %pad_maximum_fusion.6), channel_id=1, source_target_pairs={{0,6},{2,4},{4,2},{6,0},{8,14},{10,12},{12,10},{14,8},{16,22},{18,... | collective-permute-start | bytes 786440 | tf_op jit(solution)/shard_map/ppermute | solution.py:217
  96.6 25.1 %collective-permute-start.32 = (bf16[128,1024]{1,0:T(8,128)(2,1)S(1)}, bf16[128,1024]{1,0:T(8,128)(2,1)S(1)}, u32[]{:S(2)}, u32[]{:S(2)}) collective-permute-start(bf16[128,1024]{1,0:T(8,128)(2,1)S(1)} %combine.3.refs_18_), channel_id=1, source_target_pairs={{0,24},{2,26},{4,28},{6,30},{8,16},{10,18},{12,20},{14,22},{16,8},... | collective-permute-start | bytes 786440 | tf_op jit(solution)/shard_map/ppermute | solution.py:214
  99.2 22.2 %copy-start.11 = (bf16[256,128]{1,0:T(8,128)(2,1)S(1)}, bf16[256,128]{1,0:T(8,128)(2,1)}, u32[]{:S(2)}) copy-start(bf16[256,128]{1,0:T(8,128)(2,1)} %get-tuple-element.80.refs_0_) | copy-start | bytes 196612
  110.2 5.3 %collective-permute-start.27 = (bf16[64,1024]{1,0:T(8,128)(2,1)S(1)}, bf16[64,1024]{1,0:T(8,128)(2,1)S(1)}, u32[]{:S(2)}, u32[]{:S(2)}) collective-permute-start(bf16[64,1024]{1,0:T(8,128)(2,1)S(1)} %bitcast.57), channel_id=1, source_target_pairs={{0,2},{2,0},{4,6},{6,4},{8,10},{10,8},{12,14},{14,12},{16,18},{18,... | collective-permute-start | bytes 393224 | tf_op jit(solution)/shard_map/ppermute | solution.py:217
  111.8 10.7 %collective-permute-start.36 = (bf16[128,1024]{1,0:T(8,128)(2,1)S(1)}, bf16[128,1024]{1,0:T(8,128)(2,1)S(1)}, u32[]{:S(2)}, u32[]{:S(2)}) collective-permute-start(bf16[128,1024]{1,0:T(8,128)(2,1)S(1)} %get-tuple-element.154), channel_id=1, source_target_pairs={{0,8},{2,10},{4,12},{6,14},{8,0},{10,2},{12,4},{14,6},{16,24},{18,... | collective-permute-start | bytes 786440 | tf_op jit(solution)/shard_map/ppermute | solution.py:214
  114.0 11.8 %collective-permute-start.35 = (bf16[128,1024]{1,0:T(8,128)(2,1)S(1)}, bf16[128,1024]{1,0:T(8,128)(2,1)S(1)}, u32[]{:S(2)}, u32[]{:S(2)}) collective-permute-start(bf16[128,1024]{1,0:T(8,128)(2,1)S(1)} %get-tuple-element.153), channel_id=1, source_target_pairs={{0,16},{2,18},{4,20},{6,22},{8,24},{10,26},{12,28},{14,30},{16,0},... | collective-permute-start | bytes 786440 | tf_op jit(solution)/shard_map/ppermute | solution.py:214
  114.5 5.0 %collective-permute-start.28 = (bf16[64,1024]{1,0:T(8,128)(2,1)S(1)}, bf16[64,1024]{1,0:T(8,128)(2,1)S(1)}, u32[]{:S(2)}, u32[]{:S(2)}) collective-permute-start(bf16[64,1024]{1,0:T(8,128)(2,1)S(1)} %bitcast.56), channel_id=1, source_target_pairs={{0,4},{2,6},{4,0},{6,2},{8,12},{10,14},{12,8},{14,10},{16,20},{18,... | collective-permute-start | bytes 393224 | tf_op jit(solution)/shard_map/ppermute | solution.py:217
  115.5 5.9 %collective-permute-start.29 = (bf16[64,1024]{1,0:T(8,128)(2,1)S(1)}, bf16[64,1024]{1,0:T(8,128)(2,1)S(1)}, u32[]{:S(2)}, u32[]{:S(2)}) collective-permute-start(bf16[64,1024]{1,0:T(8,128)(2,1)S(1)} %bitcast.55), channel_id=1, source_target_pairs={{0,6},{2,4},{4,2},{6,0},{8,14},{10,12},{12,10},{14,8},{16,22},{18,... | collective-permute-start | bytes 393224 | tf_op jit(solution)/shard_map/ppermute | solution.py:217
  (12 other events, 110.9 us)

commit v5 on v4

--- a/solution.py
+++ b/solution.py
@@ -15,6 +15,8 @@
 BF16 = jnp.bfloat16
 VMEM_LIMIT = 32 << 20
 SMALL_LIMIT = 8 << 20
+SLOTS = 4
+GRADS_LIMIT = 24 << 20
 PAYLOAD_LIMIT = 62 << 20
 ROWS_LIMIT = 16 << 20
 
@@ -150,14 +152,24 @@
 
 def grads_body(rounds, pieces, where, *refs):
     n = rounds * pieces
-    hidden, pre, _, grad_up, grad_down, flag = refs[2 * n :]
-    for unit, xs, grad in ((pre, refs[:n], grad_up), (hidden, refs[n : 2 * n], grad_down)):
-        for q in range(pieces):
-            width = xs[0].shape[-1]
-            at = pl.multiple_of(jnp.bitwise_xor(where[0], q) * width, width)
-            x = gathered(xs[q * rounds : (q + 1) * rounds])
-            grad[0, :, pl.ds(at, width)] = dot(unit[0], x, ((1,), (0,))).astype(BF16)
+    xs = refs[:n]
+    hidden, pre, _, grad_up, grad_down, flag, slots, sems = refs[n:]
+    width = xs[0].shape[-1] // 2
+    at = [pl.multiple_of(jnp.bitwise_xor(where[0], q) * width, width) for q in range(pieces)]
+    copies = []
+    for e in range(pre.shape[0]):
+        for unit, low, grad in ((pre, 0, grad_up), (hidden, width, grad_down)):
+            slot = len(copies) % SLOTS
+            if len(copies) >= SLOTS:
+                copies[len(copies) - SLOTS].wait()
+            for q in range(pieces):
+                x = gathered(xs[q * rounds : (q + 1) * rounds], slice(None), e, slice(None), slice(low, low + width))
+                slots[slot, :, pl.ds(at[q], width)] = dot(unit[e], x, ((1,), (0,))).astype(BF16)
+            copies.append(pltpu.make_async_copy(slots.at[slot], grad.at[e], sems.at[slot]))
+            copies[-1].start()
     flag[...] = jnp.zeros(flag.shape, F32)
+    for copy in copies[-SLOTS:]:
+        copy.wait()
 
 
 def touch_body(weight, _, out):
@@ -313,14 +325,14 @@
     def weight_grads(earlier):
         return pl.pallas_call(
             functools.partial(grads_body, outer, pieces),
-            grid=(here,),
-            in_specs=[smem] + lifted_spec + scaled_spec + [unit_spec, unit_spec, any_place],
-            out_specs=[weight_spec, weight_spec, pl.BlockSpec((8, 128), lambda e: (0, 0))],
+            in_specs=[smem] + [vmem] * (n_in + 2) + [any_place],
+            out_specs=[hbm, hbm, vmem],
             out_shape=[shape(up_weight.shape, BF16)] * 2 + [shape((8, 128), F32)],
-            compiler_params=params,
+            scratch_shapes=[pltpu.VMEM((SLOTS, hidden_width, features), BF16), pltpu.SemaphoreType.DMA((SLOTS,))],
+            compiler_params=pltpu.CompilerParams(vmem_limit_bytes=GRADS_LIMIT),
             cost_estimate=cost(2 * flops, 2 * weight_bytes + 2 * row_bytes),
             name="weight_grads",
-        )(where, *rows_in, *rows_in, hidden, pre, earlier)
+        )(where, *rows_in, hidden, pre, earlier)
 
     def combine(group, blocks, earlier):
         return pl.pallas_call(

time: 127 us -> 126 us (level)
  Pallas kernels: 29.3 us -> 27.8 us
    pallas_call x1, Pallas kernels: 11 us -> 9.52 us  [weight_grads(): pl.pallas_call(functools.partial(grads_body, outer, pieces), in_specs=[sm...]
    unnamed x46 -> x14, local copies, waits for them, and re-layouts: 9.24 us -> 8.56 us
  transfers between devices with their start and end apart: 37 -> 37, of which waited for: 17 -> 17; matrix products, arithmetic and copies ran while one was open for 2% -> 2% of each run, Pallas kernels for 12% -> 11%
where the time goes in v5:
time: 126 us; the launch traced here: 125 us
  waiting for transfers between devices  46.1 us (37%)
  starting transfers between devices  38.4 us (30%)
  Pallas kernels  27.8 us (22%)
  local copies, waits for them, and re-layouts  8.73 us (7%)
  other arithmetic  3.18 us (3%)
    ppermute x21, waiting for transfers between devices, within(): return lax.ppermute(value, 'dp', [(i, i ^ m) for i in range(outer * inner)])  33.5 us
    ppermute x21, starting transfers between devices, within(): return lax.ppermute(value, 'dp', [(i, i ^ m) for i in range(outer * inner)])  24.7 us
    pallas_call x1, Pallas kernels, local(): pl.pallas_call(functools.partial(rows_body, outer, pieces, len(flags_in))...  10.8 us
    pallas_call x1, Pallas kernels, weight_grads(): pl.pallas_call(functools.partial(grads_body, outer, pieces), in_specs=[sm...  9.52 us
    unnamed x14, local copies, waits for them, and re-layouts  8.56 us
    ppermute x4, starting transfers between devices, across(): lax.ppermute(value, 'dp', [(i, i ^ m * inner) for i in range(outer * inne...  8.41 us
    ppermute x4, waiting for transfers between devices, across(): lax.ppermute(value, 'dp', [(i, i ^ m * inner) for i in range(outer * inne...  4.2 us
    ppermute x8, waiting for transfers between devices, core_swap(): return lax.ppermute(value, 'expert', [(i, i ^ q) for i in range(pieces)])  4.02 us
  transfers between devices with their start and end apart: 37, of which 17 were waited for; matrix products, arithmetic and copies ran while one was open for 2% of the time, Pallas kernels for 11%

profile of v5, /device:TPU:0, one launch (start us, length us, event | category | flops | bytes accessed | tf_op | source)
XLA Modules:
  0.0 125.2 jit_solution(6132788958805747686)
XLA Ops:
  0.6 3.3 %payload.1 = (bf16[272,1024]{1,0:T(8,128)(2,1)}, bf16[64,2048]{1,0:T(8,128)(2,1)}, bf16[64,2048]{1,0:T(8,128)(2,1)}, bf16[64,2048]{1,0:T(8,128)(2,1)}, bf16[64,2...) custom-call(s32[6,128]{1,0:T(8,128)} %bitcast.57, s32[6,128]{1,0:T(8,128)} %bitcast.58, s32[1,128]{1,0:T(1,128)} %bitcast.59, ...), custom_call_target="tpu_custom_call" | custom-call | tf_op jit(solution)/shard_map/payload/pallas_call | solution.py:211
  4.0 3.1 %collective-permute-start = (bf16[272,1024]{1,0:T(8,128)(2,1)}, bf16[272,1024]{1,0:T(8,128)(2,1)S(1)}, u32[]{:S(2)}, u32[]{:S(2)}) collective-permute-start(bf16[272,1024]{1,0:T(8,128)(2,1)} %get-tuple-element.81), channel_id=1, source_target_pairs={{0,8},{2,10},{4,12},{6,14},{8,0},{10,2},{12,4},{14,6},{16,24},{18,... | collective-permute-start | bytes 1671176 | tf_op jit(solution)/shard_map/ppermute | solution.py:226
  7.8 1.6 %collective-permute-start.2 = (bf16[64,2048]{1,0:T(8,128)(2,1)}, bf16[64,2048]{1,0:T(8,128)(2,1)S(1)}, u32[]{:S(2)}, u32[]{:S(2)}) collective-permute-start(bf16[64,2048]{1,0:T(8,128)(2,1)} %get-tuple-element.82), channel_id=1, source_target_pairs={{0,2},{2,0},{4,6},{6,4},{8,10},{10,8},{12,14},{14,12},{16,18},{18,... | collective-permute-start | bytes 786440 | tf_op jit(solution)/shard_map/ppermute | solution.py:229
  9.3 1.5 %collective-permute-start.3 = (bf16[64,2048]{1,0:T(8,128)(2,1)}, bf16[64,2048]{1,0:T(8,128)(2,1)S(1)}, u32[]{:S(2)}, u32[]{:S(2)}) collective-permute-start(bf16[64,2048]{1,0:T(8,128)(2,1)} %get-tuple-element.83), channel_id=1, source_target_pairs={{0,4},{2,6},{4,0},{6,2},{8,12},{10,14},{12,8},{14,10},{16,20},{18,... | collective-permute-start | bytes 786440 | tf_op jit(solution)/shard_map/ppermute | solution.py:229
  11.3 6.0 %collective-permute-done.2 = bf16[64,2048]{1,0:T(8,128)(2,1)S(1)} collective-permute-done((bf16[64,2048]{1,0:T(8,128)(2,1)}, bf16[64,2048]{1,0:T(8,128)(2,1)S(1)}, u32[]{:S(2)}, u32[]{:S(2)}) %collective-permute-start.2) | collective-permute-done | bytes 262176 | tf_op jit(solution)/shard_map/ppermute | solution.py:229
  17.3 5.4 %collective-permute-done.3 = bf16[64,2048]{1,0:T(8,128)(2,1)S(1)} collective-permute-done((bf16[64,2048]{1,0:T(8,128)(2,1)}, bf16[64,2048]{1,0:T(8,128)(2,1)S(1)}, u32[]{:S(2)}, u32[]{:S(2)}) %collective-permute-start.3) | collective-permute-done | bytes 262176 | tf_op jit(solution)/shard_map/ppermute | solution.py:229
  23.3 1.3 %collective-permute-start.6 = (bf16[272,1024]{1,0:T(8,128)(2,1)S(1)}, bf16[272,1024]{1,0:T(8,128)(2,1)S(1)}, u32[]{:S(2)}, u32[]{:S(2)}) collective-permute-start(bf16[272,1024]{1,0:T(8,128)(2,1)S(1)} %collective-permute-done.1.refs_1_), channel_id=1, source_target_pairs={{8,0},{10,2},{12,4},{14,6},{16,24},{18,26},{20,28},{22,30},{9,1},{... | collective-permute-start | bytes 1671176 | tf_op jit(solution)/shard_map/ppermute | solution.py:287
  24.8 1.1 choose.3
  25.8 1.3 %collective-permute-start.7 = (bf16[64,2048]{1,0:T(8,128)(2,1)S(1)}, bf16[64,2048]{1,0:T(8,128)(2,1)S(1)}, u32[]{:S(2)}, u32[]{:S(2)}) collective-permute-start(bf16[64,2048]{1,0:T(8,128)(2,1)S(1)} %get-tuple-element.98), channel_id=1, source_target_pairs={{0,2},{2,0},{4,6},{6,4},{8,10},{10,8},{12,14},{14,12},{16,18},{18,... | collective-permute-start | bytes 786440 | tf_op jit(solution)/shard_map/ppermute | solution.py:229
  28.0 1.4 %collective-permute-start.9 = (bf16[64,2048]{1,0:T(8,128)(2,1)S(1)}, bf16[64,2048]{1,0:T(8,128)(2,1)S(1)}, u32[]{:S(2)}, u32[]{:S(2)}) collective-permute-start(bf16[64,2048]{1,0:T(8,128)(2,1)S(1)} %get-tuple-element.100), channel_id=1, source_target_pairs={{0,6},{2,4},{4,2},{6,0},{8,14},{10,12},{12,10},{14,8},{16,22},{18,... | collective-permute-start | bytes 786440 | tf_op jit(solution)/shard_map/ppermute | solution.py:229
  29.4 5.8 %collective-permute-done.7 = bf16[64,2048]{1,0:T(8,128)(2,1)S(1)} collective-permute-done((bf16[64,2048]{1,0:T(8,128)(2,1)S(1)}, bf16[64,2048]{1,0:T(8,128)(2,1)S(1)}, u32[]{:S(2)}, u32[]{:S(2)}) %collective-permute-start.7) | collective-permute-done | bytes 262176 | tf_op jit(solution)/shard_map/ppermute | solution.py:229
  35.2 4.2 %collective-permute-done.8 = bf16[64,2048]{1,0:T(8,128)(2,1)S(1)} collective-permute-done((bf16[64,2048]{1,0:T(8,128)(2,1)S(1)}, bf16[64,2048]{1,0:T(8,128)(2,1)S(1)}, u32[]{:S(2)}, u32[]{:S(2)}) %collective-permute-start.8) | collective-permute-done | bytes 262176 | tf_op jit(solution)/shard_map/ppermute | solution.py:229
  39.3 1.8 %collective-permute-done.6.refs_0_ = bf16[272,1024]{1,0:T(8,128)(2,1)S(1)} collective-permute-done((bf16[272,1024]{1,0:T(8,128)(2,1)S(1)}, bf16[272,1024]{1,0:T(8,128)(2,1)S(1)}, u32[]{:S(2)}, u32[]{:S(2)}) %collective-permute-start.6) | collective-permute-done | bytes 557088 | tf_op jit(solution)/shard_map/ppermute | solution.py:287
  41.1 1.3 %collective-permute-start.10 = (bf16[272,1024]{1,0:T(8,128)(2,1)S(1)}, bf16[272,1024]{1,0:T(8,128)(2,1)S(1)}, u32[]{:S(2)}, u32[]{:S(2)}) collective-permute-start(bf16[272,1024]{1,0:T(8,128)(2,1)S(1)} %collective-permute-done.5.refs_1_), channel_id=1, source_target_pairs={{8,0},{10,2},{12,4},{14,6},{16,24},{18,26},{20,28},{22,30},{9,1},{... | collective-permute-start | bytes 1671176 | tf_op jit(solution)/shard_map/ppermute | solution.py:292
  42.4 1.1 choose.4
  43.5 1.5 %collective-permute-start.11 = (bf16[64,2048]{1,0:T(8,128)(2,1)S(1)}, bf16[64,2048]{1,0:T(8,128)(2,1)S(1)}, u32[]{:S(2)}, u32[]{:S(2)}) collective-permute-start(bf16[64,2048]{1,0:T(8,128)(2,1)S(1)} %get-tuple-element.118), channel_id=1, source_target_pairs={{0,2},{2,0},{4,6},{6,4},{8,10},{10,8},{12,14},{14,12},{16,18},{18,... | collective-permute-start | bytes 786440 | tf_op jit(solution)/shard_map/ppermute | solution.py:229
  45.0 1.2 collective-permute-start.12
  46.2 0.9 collective-permute-start.13
  47.1 1.0 pad_maximum_fusion
  48.2 4.3 %copy-done = bf16[4,704,2048]{2,1,0:T(8,128)(2,1)S(1)} copy-done((bf16[4,704,2048]{2,1,0:T(8,128)(2,1)S(1)}, bf16[4,704,2048]{2,1,0:T(8,128)(2,1)}, u32[]{:S(2)}) %copy-start) | copy-done | bytes 11534360
  52.5 2.6 %collective-permute-done.10.refs_0_ = bf16[272,1024]{1,0:T(8,128)(2,1)S(1)} collective-permute-done((bf16[272,1024]{1,0:T(8,128)(2,1)S(1)}, bf16[272,1024]{1,0:T(8,128)(2,1)S(1)}, u32[]{:S(2)}, u32[]{:S(2)}) %collective-permute-start.10) | collective-permute-done | bytes 557088 | tf_op jit(solution)/shard_map/ppermute | solution.py:292
  55.1 1.1 choose.5
  56.3 2.2 %collective-permute-start.16 = (bf16[64,2048]{1,0:T(8,128)(2,1)S(1)}, bf16[64,2048]{1,0:T(8,128)(2,1)S(1)}, u32[]{:S(2)}, u32[]{:S(2)}) collective-permute-start(bf16[64,2048]{1,0:T(8,128)(2,1)S(1)} %get-tuple-element.128), channel_id=1, source_target_pairs={{0,6},{2,4},{4,2},{6,0},{8,14},{10,12},{12,10},{14,8},{16,22},{18,... | collective-permute-start | bytes 786440 | tf_op jit(solution)/shard_map/ppermute | solution.py:229
  58.5 1.2 collective-permute-start.15
  60.0 4.3 %copy-done.1 = bf16[4,704,2048]{2,1,0:T(8,128)(2,1)S(1)} copy-done((bf16[4,704,2048]{2,1,0:T(8,128)(2,1)S(1)}, bf16[4,704,2048]{2,1,0:T(8,128)(2,1)}, u32[]{:S(2)}) %copy-start.1) | copy-done | bytes 11534360
  64.4 1.8 %collective-permute-done.16 = bf16[64,2048]{1,0:T(8,128)(2,1)S(1)} collective-permute-done((bf16[64,2048]{1,0:T(8,128)(2,1)S(1)}, bf16[64,2048]{1,0:T(8,128)(2,1)S(1)}, u32[]{:S(2)}, u32[]{:S(2)}) %collective-permute-start.16) | collective-permute-done | bytes 262176 | tf_op jit(solution)/shard_map/ppermute | solution.py:229
  66.2 2.7 %collective-permute-done.15 = bf16[64,2048]{1,0:T(8,128)(2,1)S(1)} collective-permute-done((bf16[64,2048]{1,0:T(8,128)(2,1)S(1)}, bf16[64,2048]{1,0:T(8,128)(2,1)S(1)}, u32[]{:S(2)}, u32[]{:S(2)}) %collective-permute-start.15) | collective-permute-done | bytes 262176 | tf_op jit(solution)/shard_map/ppermute | solution.py:229
  69.1 2.6 %collective-permute-done.20.refs_7_ = bf16[4,4,16,2048]{3,2,1,0:T(8,128)(2,1)S(1)} collective-permute-done((bf16[4,4,16,2048]{3,2,1,0:T(8,128)(2,1)S(1)}, bf16[4,4,16,2048]{3,2,1,0:T(8,128)(2,1)S(1)}, u32[]{:S(2)}, u32[]{:S(2)}) %collective-permute-start.20) | collective-permute-done | bytes 1048608 | tf_op jit(solution)/shard_map/ppermute | solution.py:232
  71.8 10.8 %rows.1 = (bf16[4,704,256]{2,1,0:T(8,128)(2,1)S(1)}, bf16[4,704,256]{2,1,0:T(8,128)(2,1)S(1)}, bf16[4,4,16,1024]{3,2,1,0:T(8,128)(2,1)S(1)}, bf16[4,4,16,1024]{3...) custom-call(s32[4]{0:T(128)S(1)} %pad_add_fusion.where, ...), custom_call_target="tpu_custom_call" | custom-call | flops 8858370048 | bytes 35651584 | tf_op jit(solution)/shard_map/rows/pallas_call | solution.py:315
  83.7 0.9 collective-permute-done.25
  85.6 1.8 %collective-permute-start.23 = (bf16[64,1024]{1,0:T(8,128)(2,1)S(1)}, bf16[64,1024]{1,0:T(8,128)(2,1)S(1)}, u32[]{:S(2)}, u32[]{:S(2)}) collective-permute-start(bf16[64,1024]{1,0:T(8,128)(2,1)S(1)} %bitcast.56), channel_id=1, source_target_pairs={{0,6},{2,4},{4,2},{6,0},{8,14},{10,12},{12,10},{14,8},{16,22},{18,... | collective-permute-start | bytes 393224 | tf_op jit(solution)/shard_map/ppermute | solution.py:229
  87.9 0.9 collective-permute-start.30
  88.8 0.9 collective-permute-start.31
  89.8 3.1 %collective-permute-done.23.refs_4_ = bf16[64,1024]{1,0:T(8,128)(2,1)S(1)} collective-permute-done((bf16[64,1024]{1,0:T(8,128)(2,1)S(1)}, bf16[64,1024]{1,0:T(8,128)(2,1)S(1)}, u32[]{:S(2)}, u32[]{:S(2)}) %collective-permute-start.23) | collective-permute-done | bytes 131104 | tf_op jit(solution)/shard_map/ppermute | solution.py:229
  92.9 1.4 %collective-permute-start.33 = (bf16[128,1024]{1,0:T(8,128)(2,1)S(1)}, bf16[128,1024]{1,0:T(8,128)(2,1)S(1)}, u32[]{:S(2)}, u32[]{:S(2)}) collective-permute-start(bf16[128,1024]{1,0:T(8,128)(2,1)S(1)} %get-tuple-element.150), channel_id=1, source_target_pairs={{0,2},{2,0},{4,6},{6,4},{8,10},{10,8},{12,14},{14,12},{16,18},{18,... | collective-permute-start | bytes 786440 | tf_op jit(solution)/shard_map/ppermute | solution.py:229
  94.3 0.9 collective-permute-start.34
  95.2 1.2 collective-permute-start.26
  96.6 2.4 %collective-permute-start.32 = (bf16[128,1024]{1,0:T(8,128)(2,1)S(1)}, bf16[128,1024]{1,0:T(8,128)(2,1)S(1)}, u32[]{:S(2)}, u32[]{:S(2)}) collective-permute-start(bf16[128,1024]{1,0:T(8,128)(2,1)S(1)} %combine.3.refs_10_), channel_id=1, source_target_pairs={{0,24},{2,26},{4,28},{6,30},{8,16},{10,18},{12,20},{14,22},{16,8},... | collective-permute-start | bytes 786440 | tf_op jit(solution)/shard_map/ppermute | solution.py:226
  99.0 9.5 %weight_grads.1 = (bf16[4,704,2048]{2,1,0:T(8,128)(2,1)}, bf16[4,704,2048]{2,1,0:T(8,128)(2,1)}, f32[8,128]{1,0:T(8,128)S(1)}) custom-call(s32[4]{0:T(128)S(1)} %pad_add_fusion.where, bf16[4,4,16,2048]{3,2,1,0:T(8,128)(2,1)S(1)} %bitcast.31, bf16[4,4,16,2048]{3,2,1,0:T(8,128)(2,1)S(1)} %bitcast.34, bf16[4,4,16,2048]{3,2,1,0:T(8,128)(2,1)S(1)} %bitcast.37, ...), custom_call_target="tpu_custom_call" | custom-call | flops 5905580032 | bytes 31457280 | tf_op jit(solution)/shard_map/weight_grads/pallas_call | solution.py:326
  108.6 0.9 collective-permute-start.27
  109.8 2.7 %collective-permute-start.36 = (bf16[128,1024]{1,0:T(8,128)(2,1)S(1)}, bf16[128,1024]{1,0:T(8,128)(2,1)S(1)}, u32[]{:S(2)}, u32[]{:S(2)}) collective-permute-start(bf16[128,1024]{1,0:T(8,128)(2,1)S(1)} %get-tuple-element.154), channel_id=1, source_target_pairs={{0,8},{2,10},{4,12},{6,14},{8,0},{10,2},{12,4},{14,6},{16,24},{18,... | collective-permute-start | bytes 786440 | tf_op jit(solution)/shard_map/ppermute | solution.py:226
  112.7 1.3 %collective-permute-start.28 = (bf16[64,1024]{1,0:T(8,128)(2,1)S(1)}, bf16[64,1024]{1,0:T(8,128)(2,1)S(1)}, u32[]{:S(2)}, u32[]{:S(2)}) collective-permute-start(bf16[64,1024]{1,0:T(8,128)(2,1)S(1)} %bitcast.52), channel_id=1, source_target_pairs={{0,4},{2,6},{4,0},{6,2},{8,12},{10,14},{12,8},{14,10},{16,20},{18,... | collective-permute-start | bytes 393224 | tf_op jit(solution)/shard_map/ppermute | solution.py:229
  114.0 1.3 %collective-permute-start.29 = (bf16[64,1024]{1,0:T(8,128)(2,1)S(1)}, bf16[64,1024]{1,0:T(8,128)(2,1)S(1)}, u32[]{:S(2)}, u32[]{:S(2)}) collective-permute-start(bf16[64,1024]{1,0:T(8,128)(2,1)S(1)} %bitcast.51), channel_id=1, source_target_pairs={{0,6},{2,4},{4,2},{6,0},{8,14},{10,12},{12,10},{14,8},{16,22},{18,... | collective-permute-start | bytes 393224 | tf_op jit(solution)/shard_map/ppermute | solution.py:229
  115.3 2.3 %collective-permute-done.28.refs_3_ = bf16[64,1024]{1,0:T(8,128)(2,1)S(1)} collective-permute-done((bf16[64,1024]{1,0:T(8,128)(2,1)S(1)}, bf16[64,1024]{1,0:T(8,128)(2,1)S(1)}, u32[]{:S(2)}, u32[]{:S(2)}) %collective-permute-start.28) | collective-permute-done | bytes 131104 | tf_op jit(solution)/shard_map/ppermute | solution.py:229
  117.6 2.2 %collective-permute-done.29.refs_4_ = bf16[64,1024]{1,0:T(8,128)(2,1)S(1)} collective-permute-done((bf16[64,1024]{1,0:T(8,128)(2,1)S(1)}, bf16[64,1024]{1,0:T(8,128)(2,1)S(1)}, u32[]{:S(2)}, u32[]{:S(2)}) %collective-permute-start.29) | collective-permute-done | bytes 131104 | tf_op jit(solution)/shard_map/ppermute | solution.py:229
  120.1 0.9 collective-permute-done.36
  120.9 3.3 %collective-permute-done.35 = bf16[128,1024]{1,0:T(8,128)(2,1)S(1)} collective-permute-done((bf16[128,1024]{1,0:T(8,128)(2,1)S(1)}, bf16[128,1024]{1,0:T(8,128)(2,1)S(1)}, u32[]{:S(2)}, u32[]{:S(2)}) %collective-permute-start.35) | collective-permute-done | bytes 262176 | tf_op jit(solution)/shard_map/ppermute | solution.py:226
  124.3 0.9 convert_add_fusion
  (69 shorter events, 7.3 us)
Async XLA Ops:
  4.0 18.7 %collective-permute-start = (bf16[272,1024]{1,0:T(8,128)(2,1)}, bf16[272,1024]{1,0:T(8,128)(2,1)S(1)}, u32[]{:S(2)}, u32[]{:S(2)}) collective-permute-start(bf16[272,1024]{1,0:T(8,128)(2,1)} %get-tuple-element.81), channel_id=1, source_target_pairs={{0,8},{2,10},{4,12},{6,14},{8,0},{10,2},{12,4},{14,6},{16,24},{18,... | collective-permute-start | bytes 1671176 | tf_op jit(solution)/shard_map/ppermute | solution.py:226
  7.1 15.6 %collective-permute-start.1 = (bf16[272,1024]{1,0:T(8,128)(2,1)}, bf16[272,1024]{1,0:T(8,128)(2,1)S(1)}, u32[]{:S(2)}, u32[]{:S(2)}) collective-permute-start(bf16[272,1024]{1,0:T(8,128)(2,1)} %get-tuple-element.81), channel_id=1, source_target_pairs={{8,16},{10,18},{12,20},{14,22},{16,8},{18,10},{20,12},{22,14},{9,1... | collective-permute-start | bytes 1671176 | tf_op jit(solution)/shard_map/ppermute | solution.py:282
  7.8 9.5 %collective-permute-start.2 = (bf16[64,2048]{1,0:T(8,128)(2,1)}, bf16[64,2048]{1,0:T(8,128)(2,1)S(1)}, u32[]{:S(2)}, u32[]{:S(2)}) collective-permute-start(bf16[64,2048]{1,0:T(8,128)(2,1)} %get-tuple-element.82), channel_id=1, source_target_pairs={{0,2},{2,0},{4,6},{6,4},{8,10},{10,8},{12,14},{14,12},{16,18},{18,... | collective-permute-start | bytes 786440 | tf_op jit(solution)/shard_map/ppermute | solution.py:229
  9.3 13.3 %collective-permute-start.3 = (bf16[64,2048]{1,0:T(8,128)(2,1)}, bf16[64,2048]{1,0:T(8,128)(2,1)S(1)}, u32[]{:S(2)}, u32[]{:S(2)}) collective-permute-start(bf16[64,2048]{1,0:T(8,128)(2,1)} %get-tuple-element.83), channel_id=1, source_target_pairs={{0,4},{2,6},{4,0},{6,2},{8,12},{10,14},{12,8},{14,10},{16,20},{18,... | collective-permute-start | bytes 786440 | tf_op jit(solution)/shard_map/ppermute | solution.py:229
  10.8 11.8 %collective-permute-start.4 = (bf16[64,2048]{1,0:T(8,128)(2,1)}, bf16[64,2048]{1,0:T(8,128)(2,1)S(1)}, u32[]{:S(2)}, u32[]{:S(2)}) collective-permute-start(bf16[64,2048]{1,0:T(8,128)(2,1)} %get-tuple-element.84), channel_id=1, source_target_pairs={{0,6},{2,4},{4,2},{6,0},{8,14},{10,12},{12,10},{14,8},{16,22},{18,... | collective-permute-start | bytes 786440 | tf_op jit(solution)/shard_map/ppermute | solution.py:229
  22.6 16.7 %collective-permute-start.5 = (bf16[272,1024]{1,0:T(8,128)(2,1)S(1)}, bf16[272,1024]{1,0:T(8,128)(2,1)S(1)}, u32[]{:S(2)}, u32[]{:S(2)}) collective-permute-start(bf16[272,1024]{1,0:T(8,128)(2,1)S(1)} %collective-permute-done.refs_0_), channel_id=1, source_target_pairs={{8,16},{10,18},{12,20},{14,22},{16,8},{18,10},{20,12},{22,14},{9,1... | collective-permute-start | bytes 1671176 | tf_op jit(solution)/shard_map/ppermute | solution.py:286
  23.3 17.8 %collective-permute-start.6 = (bf16[272,1024]{1,0:T(8,128)(2,1)S(1)}, bf16[272,1024]{1,0:T(8,128)(2,1)S(1)}, u32[]{:S(2)}, u32[]{:S(2)}) collective-permute-start(bf16[272,1024]{1,0:T(8,128)(2,1)S(1)} %collective-permute-done.1.refs_1_), channel_id=1, source_target_pairs={{8,0},{10,2},{12,4},{14,6},{16,24},{18,26},{20,28},{22,30},{9,1},{... | collective-permute-start | bytes 1671176 | tf_op jit(solution)/shard_map/ppermute | solution.py:287
  25.8 9.3 %collective-permute-start.7 = (bf16[64,2048]{1,0:T(8,128)(2,1)S(1)}, bf16[64,2048]{1,0:T(8,128)(2,1)S(1)}, u32[]{:S(2)}, u32[]{:S(2)}) collective-permute-start(bf16[64,2048]{1,0:T(8,128)(2,1)S(1)} %get-tuple-element.98), channel_id=1, source_target_pairs={{0,2},{2,0},{4,6},{6,4},{8,10},{10,8},{12,14},{14,12},{16,18},{18,... | collective-permute-start | bytes 786440 | tf_op jit(solution)/shard_map/ppermute | solution.py:229
  27.1 12.2 %collective-permute-start.8 = (bf16[64,2048]{1,0:T(8,128)(2,1)S(1)}, bf16[64,2048]{1,0:T(8,128)(2,1)S(1)}, u32[]{:S(2)}, u32[]{:S(2)}) collective-permute-start(bf16[64,2048]{1,0:T(8,128)(2,1)S(1)} %get-tuple-element.99), channel_id=1, source_target_pairs={{0,4},{2,6},{4,0},{6,2},{8,12},{10,14},{12,8},{14,10},{16,20},{18,... | collective-permute-start | bytes 786440 | tf_op jit(solution)/shard_map/ppermute | solution.py:229
  28.0 11.4 %collective-permute-start.9 = (bf16[64,2048]{1,0:T(8,128)(2,1)S(1)}, bf16[64,2048]{1,0:T(8,128)(2,1)S(1)}, u32[]{:S(2)}, u32[]{:S(2)}) collective-permute-start(bf16[64,2048]{1,0:T(8,128)(2,1)S(1)} %get-tuple-element.100), channel_id=1, source_target_pairs={{0,6},{2,4},{4,2},{6,0},{8,14},{10,12},{12,10},{14,8},{16,22},{18,... | collective-permute-start | bytes 786440 | tf_op jit(solution)/shard_map/ppermute | solution.py:229
  41.1 13.9 %collective-permute-start.10 = (bf16[272,1024]{1,0:T(8,128)(2,1)S(1)}, bf16[272,1024]{1,0:T(8,128)(2,1)S(1)}, u32[]{:S(2)}, u32[]{:S(2)}) collective-permute-start(bf16[272,1024]{1,0:T(8,128)(2,1)S(1)} %collective-permute-done.5.refs_1_), channel_id=1, source_target_pairs={{8,0},{10,2},{12,4},{14,6},{16,24},{18,26},{20,28},{22,30},{9,1},{... | collective-permute-start | bytes 1671176 | tf_op jit(solution)/shard_map/ppermute | solution.py:292
  43.5 12.6 %collective-permute-start.11 = (bf16[64,2048]{1,0:T(8,128)(2,1)S(1)}, bf16[64,2048]{1,0:T(8,128)(2,1)S(1)}, u32[]{:S(2)}, u32[]{:S(2)}) collective-permute-start(bf16[64,2048]{1,0:T(8,128)(2,1)S(1)} %get-tuple-element.118), channel_id=1, source_target_pairs={{0,2},{2,0},{4,6},{6,4},{8,10},{10,8},{12,14},{14,12},{16,18},{18,... | collective-permute-start | bytes 786440 | tf_op jit(solution)/shard_map/ppermute | solution.py:229
  45.0 11.3 %collective-permute-start.12 = (bf16[64,2048]{1,0:T(8,128)(2,1)S(1)}, bf16[64,2048]{1,0:T(8,128)(2,1)S(1)}, u32[]{:S(2)}, u32[]{:S(2)}) collective-permute-start(bf16[64,2048]{1,0:T(8,128)(2,1)S(1)} %get-tuple-element.119), channel_id=1, source_target_pairs={{0,4},{2,6},{4,0},{6,2},{8,12},{10,14},{12,8},{14,10},{16,20},{18,... | collective-permute-start | bytes 786440 | tf_op jit(solution)/shard_map/ppermute | solution.py:229
  46.2 10.1 %collective-permute-start.13 = (bf16[64,2048]{1,0:T(8,128)(2,1)S(1)}, bf16[64,2048]{1,0:T(8,128)(2,1)S(1)}, u32[]{:S(2)}, u32[]{:S(2)}) collective-permute-start(bf16[64,2048]{1,0:T(8,128)(2,1)S(1)} %get-tuple-element.120), channel_id=1, source_target_pairs={{0,6},{2,4},{4,2},{6,0},{8,14},{10,12},{12,10},{14,8},{16,22},{18,... | collective-permute-start | bytes 786440 | tf_op jit(solution)/shard_map/ppermute | solution.py:229
  48.1 21.0 %collective-permute-start.17 = (bf16[4,4,16,2048]{3,2,1,0:T(8,128)(2,1)S(1)}, bf16[4,4,16,2048]{3,2,1,0:T(8,128)(2,1)S(1)}, u32[]{:S(2)}, u32[]{:S(2)}) collective-permute-start(bf16[4,4,16,2048]{3,2,1,0:T(8,128)(2,1)S(1)} %bitcast.29), channel_id=1, source_target_pairs={{0,1},{1,0},{2,3},{3,2},{4,5},{5,4},{6,7},{7,6},{8,9},{9,8},{10,11... | collective-permute-start | bytes 3145736 | tf_op jit(solution)/shard_map/ppermute | solution.py:232
  48.2 4.3 %copy-start = (bf16[4,704,2048]{2,1,0:T(8,128)(2,1)S(1)}, bf16[4,704,2048]{2,1,0:T(8,128)(2,1)}, u32[]{:S(2)}) copy-start(bf16[4,704,2048]{2,1,0:T(8,128)(2,1)} %refs_8_.1) | copy-start | bytes 34603012
  52.5 19.3 %slice-start = ((s8[11534336]{0:T(1024)(128)(4,1)}), s8[4194304]{0:T(1024)(128)(4,1)S(1)}, s32[]{:S(2)}) async-start(s8[11534336]{0:T(1024)(128)(4,1)} %bitcast.27), calls=%async_computation | async-start | bytes 8388608
  52.5 19.3 %slice-start.1 = ((s8[11534336]{0:T(1024)(128)(4,1)}), s8[4194304]{0:T(1024)(128)(4,1)S(1)}, s32[]{:S(2)}) async-start(s8[11534336]{0:T(1024)(128)(4,1)} %bitcast.27), calls=%async_computation.1 | async-start | bytes 8388608
  56.3 9.9 %collective-permute-start.16 = (bf16[64,2048]{1,0:T(8,128)(2,1)S(1)}, bf16[64,2048]{1,0:T(8,128)(2,1)S(1)}, u32[]{:S(2)}, u32[]{:S(2)}) collective-permute-start(bf16[64,2048]{1,0:T(8,128)(2,1)S(1)} %get-tuple-element.128), channel_id=1, source_target_pairs={{0,6},{2,4},{4,2},{6,0},{8,14},{10,12},{12,10},{14,8},{16,22},{18,... | collective-permute-start | bytes 786440 | tf_op jit(solution)/shard_map/ppermute | solution.py:229
  58.5 10.4 %collective-permute-start.15 = (bf16[64,2048]{1,0:T(8,128)(2,1)S(1)}, bf16[64,2048]{1,0:T(8,128)(2,1)S(1)}, u32[]{:S(2)}, u32[]{:S(2)}) collective-permute-start(bf16[64,2048]{1,0:T(8,128)(2,1)S(1)} %get-tuple-element.127), channel_id=1, source_target_pairs={{0,4},{2,6},{4,0},{6,2},{8,12},{10,14},{12,8},{14,10},{16,20},{18,... | collective-permute-start | bytes 786440 | tf_op jit(solution)/shard_map/ppermute | solution.py:229
  59.7 9.2 %collective-permute-start.14 = (bf16[64,2048]{1,0:T(8,128)(2,1)S(1)}, bf16[64,2048]{1,0:T(8,128)(2,1)S(1)}, u32[]{:S(2)}, u32[]{:S(2)}) collective-permute-start(bf16[64,2048]{1,0:T(8,128)(2,1)S(1)} %get-tuple-element.126), channel_id=1, source_target_pairs={{0,2},{2,0},{4,6},{6,4},{8,10},{10,8},{12,14},{14,12},{16,18},{18,... | collective-permute-start | bytes 786440 | tf_op jit(solution)/shard_map/ppermute | solution.py:229
  59.9 9.2 %collective-permute-start.18 = (bf16[4,4,16,2048]{3,2,1,0:T(8,128)(2,1)S(1)}, bf16[4,4,16,2048]{3,2,1,0:T(8,128)(2,1)S(1)}, u32[]{:S(2)}, u32[]{:S(2)}) collective-permute-start(bf16[4,4,16,2048]{3,2,1,0:T(8,128)(2,1)S(1)} %bitcast.32), channel_id=1, source_target_pairs={{0,1},{1,0},{2,3},{3,2},{4,5},{5,4},{6,7},{7,6},{8,9},{9,8},{10,11... | collective-permute-start | bytes 3145736 | tf_op jit(solution)/shard_map/ppermute | solution.py:232
  60.0 4.3 %copy-start.1 = (bf16[4,704,2048]{2,1,0:T(8,128)(2,1)S(1)}, bf16[4,704,2048]{2,1,0:T(8,128)(2,1)}, u32[]{:S(2)}) copy-start(bf16[4,704,2048]{2,1,0:T(8,128)(2,1)} %refs_9_.1) | copy-start | bytes 34603012
  64.3 7.5 %slice-start.2 = ((s8[11534336]{0:T(1024)(128)(4,1)}), s8[3145728]{0:T(1024)(128)(4,1)S(1)}, s32[]{:S(2)}) async-start(s8[11534336]{0:T(1024)(128)(4,1)} %bitcast.27), calls=%async_computation.2 | async-start | bytes 6291456
  64.3 7.5 %copy-start.2 = (bf16[4,704,2048]{2,1,0:T(8,128)(2,1)S(1)}, bf16[4,704,2048]{2,1,0:T(8,128)(2,1)}, u32[]{:S(2)}) copy-start(bf16[4,704,2048]{2,1,0:T(8,128)(2,1)} %refs_9_.1) | copy-start | bytes 34603012
  66.2 2.9 %collective-permute-start.19 = (bf16[4,4,16,2048]{3,2,1,0:T(8,128)(2,1)S(1)}, bf16[4,4,16,2048]{3,2,1,0:T(8,128)(2,1)S(1)}, u32[]{:S(2)}, u32[]{:S(2)}) collective-permute-start(bf16[4,4,16,2048]{3,2,1,0:T(8,128)(2,1)S(1)} %bitcast.35), channel_id=1, source_target_pairs={{0,1},{1,0},{2,3},{3,2},{4,5},{5,4},{6,7},{7,6},{8,9},{9,8},{10,11... | collective-permute-start | bytes 3145736 | tf_op jit(solution)/shard_map/ppermute | solution.py:232
  69.0 2.7 %collective-permute-start.20 = (bf16[4,4,16,2048]{3,2,1,0:T(8,128)(2,1)S(1)}, bf16[4,4,16,2048]{3,2,1,0:T(8,128)(2,1)S(1)}, u32[]{:S(2)}, u32[]{:S(2)}) collective-permute-start(bf16[4,4,16,2048]{3,2,1,0:T(8,128)(2,1)S(1)} %bitcast.38), channel_id=1, source_target_pairs={{0,1},{1,0},{2,3},{3,2},{4,5},{5,4},{6,7},{7,6},{8,9},{9,8},{10,11... | collective-permute-start | bytes 3145736 | tf_op jit(solution)/shard_map/ppermute | solution.py:232
  82.6 2.0 %collective-permute-start.25 = (bf16[4,4,16,1024]{3,2,1,0:T(8,128)(2,1)S(1)}, bf16[4,4,16,1024]{3,2,1,0:T(8,128)(2,1)S(1)}, u32[]{:S(2)}, u32[]{:S(2)}) collective-permute-start(bf16[4,4,16,1024]{3,2,1,0:T(8,128)(2,1)S(1)} %get-tuple-element.138), channel_id=1, source_target_pairs={{0,1},{1,0},{2,3},{3,2},{4,5},{5,4},{6,7},{7,6},{8,9},{9,8},{10,11... | collective-permute-start | bytes 1572872 | tf_op jit(solution)/shard_map/ppermute | solution.py:232
  82.8 2.5 %collective-permute-start.22 = (bf16[4,4,16,1024]{3,2,1,0:T(8,128)(2,1)S(1)}, bf16[4,4,16,1024]{3,2,1,0:T(8,128)(2,1)S(1)}, u32[]{:S(2)}, u32[]{:S(2)}) collective-permute-start(bf16[4,4,16,1024]{3,2,1,0:T(8,128)(2,1)S(1)} %get-tuple-element.134), channel_id=1, source_target_pairs={{0,1},{1,0},{2,3},{3,2},{4,5},{5,4},{6,7},{7,6},{8,9},{9,8},{10,11... | collective-permute-start | bytes 1572872 | tf_op jit(solution)/shard_map/ppermute | solution.py:232
  83.2 4.2 %collective-permute-start.24 = (bf16[4,4,16,1024]{3,2,1,0:T(8,128)(2,1)S(1)}, bf16[4,4,16,1024]{3,2,1,0:T(8,128)(2,1)S(1)}, u32[]{:S(2)}, u32[]{:S(2)}) collective-permute-start(bf16[4,4,16,1024]{3,2,1,0:T(8,128)(2,1)S(1)} %get-tuple-element.136), channel_id=1, source_target_pairs={{0,1},{1,0},{2,3},{3,2},{4,5},{5,4},{6,7},{7,6},{8,9},{9,8},{10,11... | collective-permute-start | bytes 1572872 | tf_op jit(solution)/shard_map/ppermute | solution.py:232
  83.3 4.3 %collective-permute-start.21 = (bf16[4,4,16,1024]{3,2,1,0:T(8,128)(2,1)S(1)}, bf16[4,4,16,1024]{3,2,1,0:T(8,128)(2,1)S(1)}, u32[]{:S(2)}, u32[]{:S(2)}) collective-permute-start(bf16[4,4,16,1024]{3,2,1,0:T(8,128)(2,1)S(1)} %get-tuple-element.132), channel_id=1, source_target_pairs={{0,1},{1,0},{2,3},{3,2},{4,5},{5,4},{6,7},{7,6},{8,9},{9,8},{10,11... | collective-permute-start | bytes 1572872 | tf_op jit(solution)/shard_map/ppermute | solution.py:232
  85.6 7.3 %collective-permute-start.23 = (bf16[64,1024]{1,0:T(8,128)(2,1)S(1)}, bf16[64,1024]{1,0:T(8,128)(2,1)S(1)}, u32[]{:S(2)}, u32[]{:S(2)}) collective-permute-start(bf16[64,1024]{1,0:T(8,128)(2,1)S(1)} %bitcast.56), channel_id=1, source_target_pairs={{0,6},{2,4},{4,2},{6,0},{8,14},{10,12},{12,10},{14,8},{16,22},{18,... | collective-permute-start | bytes 393224 | tf_op jit(solution)/shard_map/ppermute | solution.py:229
  87.9 8.5 %collective-permute-start.30 = (bf16[64,1024]{1,0:T(8,128)(2,1)S(1)}, bf16[64,1024]{1,0:T(8,128)(2,1)S(1)}, u32[]{:S(2)}, u32[]{:S(2)}) collective-permute-start(bf16[64,1024]{1,0:T(8,128)(2,1)S(1)} %bitcast.55), channel_id=1, source_target_pairs={{0,2},{2,0},{4,6},{6,4},{8,10},{10,8},{12,14},{14,12},{16,18},{18,... | collective-permute-start | bytes 393224 | tf_op jit(solution)/shard_map/ppermute | solution.py:229
  88.8 7.6 %collective-permute-start.31 = (bf16[64,1024]{1,0:T(8,128)(2,1)S(1)}, bf16[64,1024]{1,0:T(8,128)(2,1)S(1)}, u32[]{:S(2)}, u32[]{:S(2)}) collective-permute-start(bf16[64,1024]{1,0:T(8,128)(2,1)S(1)} %bitcast.54), channel_id=1, source_target_pairs={{0,4},{2,6},{4,0},{6,2},{8,12},{10,14},{12,8},{14,10},{16,20},{18,... | collective-permute-start | bytes 393224 | tf_op jit(solution)/shard_map/ppermute | solution.py:229
  92.9 16.6 %collective-permute-start.33 = (bf16[128,1024]{1,0:T(8,128)(2,1)S(1)}, bf16[128,1024]{1,0:T(8,128)(2,1)S(1)}, u32[]{:S(2)}, u32[]{:S(2)}) collective-permute-start(bf16[128,1024]{1,0:T(8,128)(2,1)S(1)} %get-tuple-element.150), channel_id=1, source_target_pairs={{0,2},{2,0},{4,6},{6,4},{8,10},{10,8},{12,14},{14,12},{16,18},{18,... | collective-permute-start | bytes 786440 | tf_op jit(solution)/shard_map/ppermute | solution.py:229
  94.3 15.2 %collective-permute-start.34 = (bf16[128,1024]{1,0:T(8,128)(2,1)S(1)}, bf16[128,1024]{1,0:T(8,128)(2,1)S(1)}, u32[]{:S(2)}, u32[]{:S(2)}) collective-permute-start(bf16[128,1024]{1,0:T(8,128)(2,1)S(1)} %get-tuple-element.151), channel_id=1, source_target_pairs={{0,4},{2,6},{4,0},{6,2},{8,12},{10,14},{12,8},{14,10},{16,20},{18,... | collective-permute-start | bytes 786440 | tf_op jit(solution)/shard_map/ppermute | solution.py:229
  95.2 13.4 %collective-permute-start.26 = (bf16[128,1024]{1,0:T(8,128)(2,1)S(1)}, bf16[128,1024]{1,0:T(8,128)(2,1)S(1)}, u32[]{:S(2)}, u32[]{:S(2)}) collective-permute-start(bf16[128,1024]{1,0:T(8,128)(2,1)S(1)} %pad_maximum_fusion.6), channel_id=1, source_target_pairs={{0,6},{2,4},{4,2},{6,0},{8,14},{10,12},{12,10},{14,8},{16,22},{18,... | collective-permute-start | bytes 786440 | tf_op jit(solution)/shard_map/ppermute | solution.py:229
  96.6 23.5 %collective-permute-start.32 = (bf16[128,1024]{1,0:T(8,128)(2,1)S(1)}, bf16[128,1024]{1,0:T(8,128)(2,1)S(1)}, u32[]{:S(2)}, u32[]{:S(2)}) collective-permute-start(bf16[128,1024]{1,0:T(8,128)(2,1)S(1)} %combine.3.refs_10_), channel_id=1, source_target_pairs={{0,24},{2,26},{4,28},{6,30},{8,16},{10,18},{12,20},{14,22},{16,8},... | collective-permute-start | bytes 786440 | tf_op jit(solution)/shard_map/ppermute | solution.py:226
  99.0 20.8 %copy-start.3 = (bf16[256,128]{1,0:T(8,128)(2,1)S(1)}, bf16[256,128]{1,0:T(8,128)(2,1)}, u32[]{:S(2)}) copy-start(bf16[256,128]{1,0:T(8,128)(2,1)} %get-tuple-element.80.refs_0_) | copy-start | bytes 196612
  108.6 5.4 %collective-permute-start.27 = (bf16[64,1024]{1,0:T(8,128)(2,1)S(1)}, bf16[64,1024]{1,0:T(8,128)(2,1)S(1)}, u32[]{:S(2)}, u32[]{:S(2)}) collective-permute-start(bf16[64,1024]{1,0:T(8,128)(2,1)S(1)} %bitcast.53), channel_id=1, source_target_pairs={{0,2},{2,0},{4,6},{6,4},{8,10},{10,8},{12,14},{14,12},{16,18},{18,... | collective-permute-start | bytes 393224 | tf_op jit(solution)/shard_map/ppermute | solution.py:229
  109.8 11.2 %collective-permute-start.36 = (bf16[128,1024]{1,0:T(8,128)(2,1)S(1)}, bf16[128,1024]{1,0:T(8,128)(2,1)S(1)}, u32[]{:S(2)}, u32[]{:S(2)}) collective-permute-start(bf16[128,1024]{1,0:T(8,128)(2,1)S(1)} %get-tuple-element.154), channel_id=1, source_target_pairs={{0,8},{2,10},{4,12},{6,14},{8,0},{10,2},{12,4},{14,6},{16,24},{18,... | collective-permute-start | bytes 786440 | tf_op jit(solution)/shard_map/ppermute | solution.py:226
  112.4 11.9 %collective-permute-start.35 = (bf16[128,1024]{1,0:T(8,128)(2,1)S(1)}, bf16[128,1024]{1,0:T(8,128)(2,1)S(1)}, u32[]{:S(2)}, u32[]{:S(2)}) collective-permute-start(bf16[128,1024]{1,0:T(8,128)(2,1)S(1)} %get-tuple-element.153), channel_id=1, source_target_pairs={{0,16},{2,18},{4,20},{6,22},{8,24},{10,26},{12,28},{14,30},{16,0},... | collective-permute-start | bytes 786440 | tf_op jit(solution)/shard_map/ppermute | solution.py:226
  112.7 5.0 %collective-permute-start.28 = (bf16[64,1024]{1,0:T(8,128)(2,1)S(1)}, bf16[64,1024]{1,0:T(8,128)(2,1)S(1)}, u32[]{:S(2)}, u32[]{:S(2)}) collective-permute-start(bf16[64,1024]{1,0:T(8,128)(2,1)S(1)} %bitcast.52), channel_id=1, source_target_pairs={{0,4},{2,6},{4,0},{6,2},{8,12},{10,14},{12,8},{14,10},{16,20},{18,... | collective-permute-start | bytes 393224 | tf_op jit(solution)/shard_map/ppermute | solution.py:229
  114.0 5.9 %collective-permute-start.29 = (bf16[64,1024]{1,0:T(8,128)(2,1)S(1)}, bf16[64,1024]{1,0:T(8,128)(2,1)S(1)}, u32[]{:S(2)}, u32[]{:S(2)}) collective-permute-start(bf16[64,1024]{1,0:T(8,128)(2,1)S(1)} %bitcast.51), channel_id=1, source_target_pairs={{0,6},{2,4},{4,2},{6,0},{8,14},{10,12},{12,10},{14,8},{16,22},{18,... | collective-permute-start | bytes 393224 | tf_op jit(solution)/shard_map/ppermute | solution.py:229

commit v6 on v5

--- a/solution.py
+++ b/solution.py
@@ -360,12 +360,12 @@
     sums, flag = [], []
     for i, group in enumerate(groups):
         blocks = [ready[i][0]] + [within(ready[i][m], m) for m in range(1, inner)]
-        if i + 1 < len(groups):
-            blocks[-1], ready[i + 1][1:] = lax.optimization_barrier((blocks[-1], ready[i + 1][1:]))
         if i == 1:
             grad_up, grad_down, flag = weight_grads(sent)
             flag = [flag]
         done = combine(group, blocks, flag)
+        if i + 1 < len(groups):
+            done, ready[i + 1][1:] = lax.optimization_barrier((done, ready[i + 1][1:]))
         for r, value in zip(group, done):
             if r:
                 sent = value

time: 126 us -> 139 us (1.10)
  waiting for transfers between devices: 46.1 us -> 57.4 us
  starting transfers between devices: 38.4 us -> 40.6 us
    ppermute x4, waiting for transfers between devices: 4.2 us -> 12.8 us  [across(): lax.ppermute(value, 'dp', [(i, i ^ m * inner) for i in range(outer * inne...]
    ppermute x21, waiting for transfers between devices: 33.5 us -> 37.6 us  [within(): return lax.ppermute(value, 'dp', [(i, i ^ m) for i in range(outer * inner)])]
    ppermute x4, starting transfers between devices: 8.41 us -> 10.3 us  [across(): lax.ppermute(value, 'dp', [(i, i ^ m * inner) for i in range(outer * inne...]
    ppermute x8, waiting for transfers between devices: 4.02 us -> 5.87 us  [core_swap(): return lax.ppermute(value, 'expert', [(i, i ^ q) for i in range(pieces)])]
    ppermute x1, waiting for transfers between devices: 1.82 us -> 0.01 us  [local(): out_mid = lax.ppermute(mid, 'dp', outward)]
    ppermute x1, waiting for transfers between devices: 2.59 us -> 1.14 us  [local(): out_far = lax.ppermute(far, 'dp', outward)]
  transfers between devices with their start and end apart: 37 -> 37, of which waited for: 17 -> 21; matrix products, arithmetic and copies ran while one was open for 2% -> 2% of each run, Pallas kernels for 11% -> 9%
where the time goes in v6:
time: 139 us
  waiting for transfers between devices  57.4 us (41%)
  starting transfers between devices  40.6 us (29%)
  Pallas kernels  27.8 us (20%)
  local copies, waits for them, and re-layouts  8.72 us (6%)
  other arithmetic  3.18 us (2%)
    ppermute x21, waiting for transfers between devices, within(): return lax.ppermute(value, 'dp', [(i, i ^ m) for i in range(outer * inner)])  37.6 us
    ppermute x21, starting transfers between devices, within(): return lax.ppermute(value, 'dp', [(i, i ^ m) for i in range(outer * inner)])  24.7 us
    ppermute x4, waiting for transfers between devices, across(): lax.ppermute(value, 'dp', [(i, i ^ m * inner) for i in range(outer * inne...  12.8 us
    pallas_call x1, Pallas kernels, local(): pl.pallas_call(functools.partial(rows_body, outer, pieces, len(flags_in))...  10.8 us
    ppermute x4, starting transfers between devices, across(): lax.ppermute(value, 'dp', [(i, i ^ m * inner) for i in range(outer * inne...  10.3 us
    pallas_call x1, Pallas kernels, weight_grads(): pl.pallas_call(functools.partial(grads_body, outer, pieces), in_specs=[sm...  9.52 us
    unnamed x14, local copies, waits for them, and re-layouts  8.56 us
    ppermute x8, waiting for transfers between devices, core_swap(): return lax.ppermute(value, 'expert', [(i, i ^ q) for i in range(pieces)])  5.87 us
  transfers between devices with their start and end apart: 37, of which 21 were waited for; matrix products, arithmetic and copies ran while one was open for 2% of the time, Pallas kernels for 9%

profile of v6, /device:TPU:0, one launch (start us, length us, event | category | flops | bytes accessed | tf_op | source)
XLA Modules:
  0.0 138.7 jit_solution(5400259456275099619)
XLA Ops:
  0.6 3.3 %payload.1 = (bf16[272,1024]{1,0:T(8,128)(2,1)}, bf16[64,2048]{1,0:T(8,128)(2,1)}, bf16[64,2048]{1,0:T(8,128)(2,1)}, bf16[64,2048]{1,0:T(8,128)(2,1)}, bf16[64,2...) custom-call(s32[6,128]{1,0:T(8,128)} %bitcast.57, s32[6,128]{1,0:T(8,128)} %bitcast.58, s32[1,128]{1,0:T(1,128)} %bitcast.59, ...), custom_call_target="tpu_custom_call" | custom-call | tf_op jit(solution)/shard_map/payload/pallas_call | solution.py:211
  4.0 0.7 collective-permute-start.1
  4.7 5.9 %collective-permute-start = (bf16[272,1024]{1,0:T(8,128)(2,1)}, bf16[272,1024]{1,0:T(8,128)(2,1)S(1)}, u32[]{:S(2)}, u32[]{:S(2)}) collective-permute-start(bf16[272,1024]{1,0:T(8,128)(2,1)} %get-tuple-element.82), channel_id=1, source_target_pairs={{0,8},{2,10},{4,12},{6,14},{8,0},{10,2},{12,4},{14,6},{16,24},{18,... | collective-permute-start | bytes 1671176 | tf_op jit(solution)/shard_map/ppermute | solution.py:226
  10.6 1.5 %collective-permute-start.2 = (bf16[64,2048]{1,0:T(8,128)(2,1)}, bf16[64,2048]{1,0:T(8,128)(2,1)S(1)}, u32[]{:S(2)}, u32[]{:S(2)}) collective-permute-start(bf16[64,2048]{1,0:T(8,128)(2,1)} %get-tuple-element.83), channel_id=1, source_target_pairs={{0,2},{2,0},{4,6},{6,4},{8,10},{10,8},{12,14},{14,12},{16,18},{18,... | collective-permute-start | bytes 786440 | tf_op jit(solution)/shard_map/ppermute | solution.py:229
  12.1 1.5 %collective-permute-start.3 = (bf16[64,2048]{1,0:T(8,128)(2,1)}, bf16[64,2048]{1,0:T(8,128)(2,1)S(1)}, u32[]{:S(2)}, u32[]{:S(2)}) collective-permute-start(bf16[64,2048]{1,0:T(8,128)(2,1)} %get-tuple-element.84), channel_id=1, source_target_pairs={{0,4},{2,6},{4,0},{6,2},{8,12},{10,14},{12,8},{14,10},{16,20},{18,... | collective-permute-start | bytes 786440 | tf_op jit(solution)/shard_map/ppermute | solution.py:229
  14.1 6.0 %collective-permute-done.2 = bf16[64,2048]{1,0:T(8,128)(2,1)S(1)} collective-permute-done((bf16[64,2048]{1,0:T(8,128)(2,1)}, bf16[64,2048]{1,0:T(8,128)(2,1)S(1)}, u32[]{:S(2)}, u32[]{:S(2)}) %collective-permute-start.2) | collective-permute-done | bytes 262176 | tf_op jit(solution)/shard_map/ppermute | solution.py:229
  20.0 5.1 %collective-permute-done.3 = bf16[64,2048]{1,0:T(8,128)(2,1)S(1)} collective-permute-done((bf16[64,2048]{1,0:T(8,128)(2,1)}, bf16[64,2048]{1,0:T(8,128)(2,1)S(1)}, u32[]{:S(2)}, u32[]{:S(2)}) %collective-permute-start.3) | collective-permute-done | bytes 262176 | tf_op jit(solution)/shard_map/ppermute | solution.py:229
  25.1 0.7 collective-permute-start.5
  25.8 1.3 collective-permute-start.6
  27.2 1.1 choose.3
  28.3 1.3 collective-permute-start.7
  29.6 0.8 collective-permute-start.8
  30.4 1.4 %collective-permute-start.9 = (bf16[64,2048]{1,0:T(8,128)(2,1)S(1)}, bf16[64,2048]{1,0:T(8,128)(2,1)S(1)}, u32[]{:S(2)}, u32[]{:S(2)}) collective-permute-start(bf16[64,2048]{1,0:T(8,128)(2,1)S(1)} %get-tuple-element.101), channel_id=1, source_target_pairs={{0,6},{2,4},{4,2},{6,0},{8,14},{10,12},{12,10},{14,8},{16,22},{18,... | collective-permute-start | bytes 786440 | tf_op jit(solution)/shard_map/ppermute | solution.py:229
  31.9 5.7 %collective-permute-done.7 = bf16[64,2048]{1,0:T(8,128)(2,1)S(1)} collective-permute-done((bf16[64,2048]{1,0:T(8,128)(2,1)S(1)}, bf16[64,2048]{1,0:T(8,128)(2,1)S(1)}, u32[]{:S(2)}, u32[]{:S(2)}) %collective-permute-start.7) | collective-permute-done | bytes 262176 | tf_op jit(solution)/shard_map/ppermute | solution.py:229
  37.5 4.0 %collective-permute-done.8 = bf16[64,2048]{1,0:T(8,128)(2,1)S(1)} collective-permute-done((bf16[64,2048]{1,0:T(8,128)(2,1)S(1)}, bf16[64,2048]{1,0:T(8,128)(2,1)S(1)}, u32[]{:S(2)}, u32[]{:S(2)}) %collective-permute-start.8) | collective-permute-done | bytes 262176 | tf_op jit(solution)/shard_map/ppermute | solution.py:229
  41.5 1.3 collective-permute-start.10
  42.8 1.1 choose.4
  44.5 1.6 %collective-permute-start.12 = (bf16[64,2048]{1,0:T(8,128)(2,1)S(1)}, bf16[64,2048]{1,0:T(8,128)(2,1)S(1)}, u32[]{:S(2)}, u32[]{:S(2)}) collective-permute-start(bf16[64,2048]{1,0:T(8,128)(2,1)S(1)} %get-tuple-element.120), channel_id=1, source_target_pairs={{0,4},{2,6},{4,0},{6,2},{8,12},{10,14},{12,8},{14,10},{16,20},{18,... | collective-permute-start | bytes 786440 | tf_op jit(solution)/shard_map/ppermute | solution.py:229
  46.1 1.3 collective-permute-start.13
  47.5 1.0 pad_maximum_fusion
  48.6 4.3 %copy-done = bf16[4,704,2048]{2,1,0:T(8,128)(2,1)S(1)} copy-done((bf16[4,704,2048]{2,1,0:T(8,128)(2,1)S(1)}, bf16[4,704,2048]{2,1,0:T(8,128)(2,1)}, u32[]{:S(2)}) %copy-start) | copy-done | bytes 11534360
  52.8 1.1 collective-permute-done.10.refs_0_
  54.0 1.1 choose.5
  55.2 1.6 %collective-permute-start.14 = (bf16[64,2048]{1,0:T(8,128)(2,1)S(1)}, bf16[64,2048]{1,0:T(8,128)(2,1)S(1)}, u32[]{:S(2)}, u32[]{:S(2)}) collective-permute-start(bf16[64,2048]{1,0:T(8,128)(2,1)S(1)} %get-tuple-element.127), channel_id=1, source_target_pairs={{0,2},{2,0},{4,6},{6,4},{8,10},{10,8},{12,14},{14,12},{16,18},{18,... | collective-permute-start | bytes 786440 | tf_op jit(solution)/shard_map/ppermute | solution.py:229
  56.8 1.4 %collective-permute-start.15 = (bf16[64,2048]{1,0:T(8,128)(2,1)S(1)}, bf16[64,2048]{1,0:T(8,128)(2,1)S(1)}, u32[]{:S(2)}, u32[]{:S(2)}) collective-permute-start(bf16[64,2048]{1,0:T(8,128)(2,1)S(1)} %get-tuple-element.128), channel_id=1, source_target_pairs={{0,4},{2,6},{4,0},{6,2},{8,12},{10,14},{12,8},{14,10},{16,20},{18,... | collective-permute-start | bytes 786440 | tf_op jit(solution)/shard_map/ppermute | solution.py:229
  58.9 4.3 %copy-done.1 = bf16[4,704,2048]{2,1,0:T(8,128)(2,1)S(1)} copy-done((bf16[4,704,2048]{2,1,0:T(8,128)(2,1)S(1)}, bf16[4,704,2048]{2,1,0:T(8,128)(2,1)}, u32[]{:S(2)}) %copy-start.1) | copy-done | bytes 11534360
  63.3 5.2 %collective-permute-done.16 = bf16[64,2048]{1,0:T(8,128)(2,1)S(1)} collective-permute-done((bf16[64,2048]{1,0:T(8,128)(2,1)S(1)}, bf16[64,2048]{1,0:T(8,128)(2,1)S(1)}, u32[]{:S(2)}, u32[]{:S(2)}) %collective-permute-start.16) | collective-permute-done | bytes 262176 | tf_op jit(solution)/shard_map/ppermute | solution.py:229
  69.2 2.0 %collective-permute-done.19.refs_6_ = bf16[4,4,16,2048]{3,2,1,0:T(8,128)(2,1)S(1)} collective-permute-done((bf16[4,4,16,2048]{3,2,1,0:T(8,128)(2,1)S(1)}, bf16[4,4,16,2048]{3,2,1,0:T(8,128)(2,1)S(1)}, u32[]{:S(2)}, u32[]{:S(2)}) %collective-permute-start.19) | collective-permute-done | bytes 1048608 | tf_op jit(solution)/shard_map/ppermute | solution.py:232
  71.1 1.5 %collective-permute-done.20.refs_7_ = bf16[4,4,16,2048]{3,2,1,0:T(8,128)(2,1)S(1)} collective-permute-done((bf16[4,4,16,2048]{3,2,1,0:T(8,128)(2,1)S(1)}, bf16[4,4,16,2048]{3,2,1,0:T(8,128)(2,1)S(1)}, u32[]{:S(2)}, u32[]{:S(2)}) %collective-permute-start.20) | collective-permute-done | bytes 1048608 | tf_op jit(solution)/shard_map/ppermute | solution.py:232
  72.7 10.8 %rows.1 = (bf16[4,704,256]{2,1,0:T(8,128)(2,1)S(1)}, bf16[4,704,256]{2,1,0:T(8,128)(2,1)S(1)}, bf16[4,4,16,1024]{3,2,1,0:T(8,128)(2,1)S(1)}, bf16[4,4,16,1024]{3...) custom-call(s32[4]{0:T(128)S(1)} %pad_add_fusion.where, ...), custom_call_target="tpu_custom_call" | custom-call | flops 8858370048 | bytes 35651584 | tf_op jit(solution)/shard_map/rows/pallas_call | solution.py:315
  84.6 0.9 collective-permute-done.21
  88.0 1.5 %collective-permute-start.26 = (bf16[64,1024]{1,0:T(8,128)(2,1)S(1)}, bf16[64,1024]{1,0:T(8,128)(2,1)S(1)}, u32[]{:S(2)}, u32[]{:S(2)}) collective-permute-start(bf16[64,1024]{1,0:T(8,128)(2,1)S(1)} %bitcast.56), channel_id=1, source_target_pairs={{0,4},{2,6},{4,0},{6,2},{8,12},{10,14},{12,8},{14,10},{16,20},{18,... | collective-permute-start | bytes 393224 | tf_op jit(solution)/shard_map/ppermute | solution.py:229
  89.5 1.6 %collective-permute-start.27 = (bf16[64,1024]{1,0:T(8,128)(2,1)S(1)}, bf16[64,1024]{1,0:T(8,128)(2,1)S(1)}, u32[]{:S(2)}, u32[]{:S(2)}) collective-permute-start(bf16[64,1024]{1,0:T(8,128)(2,1)S(1)} %bitcast.55), channel_id=1, source_target_pairs={{0,6},{2,4},{4,2},{6,0},{8,14},{10,12},{12,10},{14,8},{16,22},{18,... | collective-permute-start | bytes 393224 | tf_op jit(solution)/shard_map/ppermute | solution.py:229
  91.6 4.4 %collective-permute-done.26.refs_3_ = bf16[64,1024]{1,0:T(8,128)(2,1)S(1)} collective-permute-done((bf16[64,1024]{1,0:T(8,128)(2,1)S(1)}, bf16[64,1024]{1,0:T(8,128)(2,1)S(1)}, u32[]{:S(2)}, u32[]{:S(2)}) %collective-permute-start.26) | collective-permute-done | bytes 131104 | tf_op jit(solution)/shard_map/ppermute | solution.py:229
  96.0 0.8 collective-permute-done.27.refs_4_
  96.8 0.8 collective-permute-done.25.refs_2_
  97.9 1.6 %collective-permute-start.28 = (bf16[128,1024]{1,0:T(8,128)(2,1)S(1)}, bf16[128,1024]{1,0:T(8,128)(2,1)S(1)}, u32[]{:S(2)}, u32[]{:S(2)}) collective-permute-start(bf16[128,1024]{1,0:T(8,128)(2,1)S(1)} %get-tuple-element.143), channel_id=1, source_target_pairs={{0,2},{2,0},{4,6},{6,4},{8,10},{10,8},{12,14},{14,12},{16,18},{18,... | collective-permute-start | bytes 786440 | tf_op jit(solution)/shard_map/ppermute | solution.py:229
  100.0 1.4 %collective-permute-start.30 = (bf16[128,1024]{1,0:T(8,128)(2,1)S(1)}, bf16[128,1024]{1,0:T(8,128)(2,1)S(1)}, u32[]{:S(2)}, u32[]{:S(2)}) collective-permute-start(bf16[128,1024]{1,0:T(8,128)(2,1)S(1)} %pad_maximum_fusion.7), channel_id=1, source_target_pairs={{0,6},{2,4},{4,2},{6,0},{8,14},{10,12},{12,10},{14,8},{16,22},{18,... | collective-permute-start | bytes 786440 | tf_op jit(solution)/shard_map/ppermute | solution.py:229
  101.4 9.5 %weight_grads.1 = (bf16[4,704,2048]{2,1,0:T(8,128)(2,1)}, bf16[4,704,2048]{2,1,0:T(8,128)(2,1)}, f32[8,128]{1,0:T(8,128)S(1)}) custom-call(s32[4]{0:T(128)S(1)} %pad_add_fusion.where, bf16[4,4,16,2048]{3,2,1,0:T(8,128)(2,1)S(1)} %bitcast.31, bf16[4,4,16,2048]{3,2,1,0:T(8,128)(2,1)S(1)} %bitcast.34, bf16[4,4,16,2048]{3,2,1,0:T(8,128)(2,1)S(1)} %bitcast.37, ...), custom_call_target="tpu_custom_call" | custom-call | flops 5905580032 | bytes 31457280 | tf_op jit(solution)/shard_map/weight_grads/pallas_call | solution.py:326
  111.0 1.1 collective-permute-done.29.refs_4_
  113.0 1.5 %collective-permute-start.34 = (bf16[128,1024]{1,0:T(8,128)(2,1)S(1)}, bf16[128,1024]{1,0:T(8,128)(2,1)S(1)}, u32[]{:S(2)}, u32[]{:S(2)}) collective-permute-start(bf16[128,1024]{1,0:T(8,128)(2,1)S(1)} %combine.3.refs_10_), channel_id=1, source_target_pairs={{0,24},{2,26},{4,28},{6,30},{8,16},{10,18},{12,20},{14,22},{16,8},... | collective-permute-start | bytes 786440 | tf_op jit(solution)/shard_map/ppermute | solution.py:226
  114.5 2.7 %collective-permute-start.35 = (bf16[128,1024]{1,0:T(8,128)(2,1)S(1)}, bf16[128,1024]{1,0:T(8,128)(2,1)S(1)}, u32[]{:S(2)}, u32[]{:S(2)}) collective-permute-start(bf16[128,1024]{1,0:T(8,128)(2,1)S(1)} %get-tuple-element.155), channel_id=1, source_target_pairs={{0,16},{2,18},{4,20},{6,22},{8,24},{10,26},{12,28},{14,30},{16,0},... | collective-permute-start | bytes 786440 | tf_op jit(solution)/shard_map/ppermute | solution.py:226
  117.3 1.5 %collective-permute-start.32 = (bf16[64,1024]{1,0:T(8,128)(2,1)S(1)}, bf16[64,1024]{1,0:T(8,128)(2,1)S(1)}, u32[]{:S(2)}, u32[]{:S(2)}) collective-permute-start(bf16[64,1024]{1,0:T(8,128)(2,1)S(1)} %bitcast.52), channel_id=1, source_target_pairs={{0,4},{2,6},{4,0},{6,2},{8,12},{10,14},{12,8},{14,10},{16,20},{18,... | collective-permute-start | bytes 393224 | tf_op jit(solution)/shard_map/ppermute | solution.py:229
  118.8 1.6 %collective-permute-start.33 = (bf16[64,1024]{1,0:T(8,128)(2,1)S(1)}, bf16[64,1024]{1,0:T(8,128)(2,1)S(1)}, u32[]{:S(2)}, u32[]{:S(2)}) collective-permute-start(bf16[64,1024]{1,0:T(8,128)(2,1)S(1)} %bitcast.51), channel_id=1, source_target_pairs={{0,6},{2,4},{4,2},{6,0},{8,14},{10,12},{12,10},{14,8},{16,22},{18,... | collective-permute-start | bytes 393224 | tf_op jit(solution)/shard_map/ppermute | solution.py:229
  120.4 1.9 %collective-permute-done.32.refs_3_ = bf16[64,1024]{1,0:T(8,128)(2,1)S(1)} collective-permute-done((bf16[64,1024]{1,0:T(8,128)(2,1)S(1)}, bf16[64,1024]{1,0:T(8,128)(2,1)S(1)}, u32[]{:S(2)}, u32[]{:S(2)}) %collective-permute-start.32) | collective-permute-done | bytes 131104 | tf_op jit(solution)/shard_map/ppermute | solution.py:229
  122.3 2.4 %collective-permute-done.33.refs_4_ = bf16[64,1024]{1,0:T(8,128)(2,1)S(1)} collective-permute-done((bf16[64,1024]{1,0:T(8,128)(2,1)S(1)}, bf16[64,1024]{1,0:T(8,128)(2,1)S(1)}, u32[]{:S(2)}, u32[]{:S(2)}) %collective-permute-start.33) | collective-permute-done | bytes 131104 | tf_op jit(solution)/shard_map/ppermute | solution.py:229
  124.9 12.8 %collective-permute-done.35 = bf16[128,1024]{1,0:T(8,128)(2,1)S(1)} collective-permute-done((bf16[128,1024]{1,0:T(8,128)(2,1)S(1)}, bf16[128,1024]{1,0:T(8,128)(2,1)S(1)}, u32[]{:S(2)}, u32[]{:S(2)}) %collective-permute-start.35) | collective-permute-done | bytes 262176 | tf_op jit(solution)/shard_map/ppermute | solution.py:226
  137.7 0.9 convert_add_fusion
  (69 shorter events, 8.9 us)
Async XLA Ops:
  4.0 21.1 %collective-permute-start.1 = (bf16[272,1024]{1,0:T(8,128)(2,1)}, bf16[272,1024]{1,0:T(8,128)(2,1)S(1)}, u32[]{:S(2)}, u32[]{:S(2)}) collective-permute-start(bf16[272,1024]{1,0:T(8,128)(2,1)} %get-tuple-element.82), channel_id=1, source_target_pairs={{8,16},{10,18},{12,20},{14,22},{16,8},{18,10},{20,12},{22,14},{9,1... | collective-permute-start | bytes 1671176 | tf_op jit(solution)/shard_map/ppermute | solution.py:282
  4.7 20.4 %collective-permute-start = (bf16[272,1024]{1,0:T(8,128)(2,1)}, bf16[272,1024]{1,0:T(8,128)(2,1)S(1)}, u32[]{:S(2)}, u32[]{:S(2)}) collective-permute-start(bf16[272,1024]{1,0:T(8,128)(2,1)} %get-tuple-element.82), channel_id=1, source_target_pairs={{0,8},{2,10},{4,12},{6,14},{8,0},{10,2},{12,4},{14,6},{16,24},{18,... | collective-permute-start | bytes 1671176 | tf_op jit(solution)/shard_map/ppermute | solution.py:226
  10.6 9.5 %collective-permute-start.2 = (bf16[64,2048]{1,0:T(8,128)(2,1)}, bf16[64,2048]{1,0:T(8,128)(2,1)S(1)}, u32[]{:S(2)}, u32[]{:S(2)}) collective-permute-start(bf16[64,2048]{1,0:T(8,128)(2,1)} %get-tuple-element.83), channel_id=1, source_target_pairs={{0,2},{2,0},{4,6},{6,4},{8,10},{10,8},{12,14},{14,12},{16,18},{18,... | collective-permute-start | bytes 786440 | tf_op jit(solution)/shard_map/ppermute | solution.py:229
  12.1 13.0 %collective-permute-start.3 = (bf16[64,2048]{1,0:T(8,128)(2,1)}, bf16[64,2048]{1,0:T(8,128)(2,1)S(1)}, u32[]{:S(2)}, u32[]{:S(2)}) collective-permute-start(bf16[64,2048]{1,0:T(8,128)(2,1)} %get-tuple-element.84), channel_id=1, source_target_pairs={{0,4},{2,6},{4,0},{6,2},{8,12},{10,14},{12,8},{14,10},{16,20},{18,... | collective-permute-start | bytes 786440 | tf_op jit(solution)/shard_map/ppermute | solution.py:229
  13.6 11.5 %collective-permute-start.4 = (bf16[64,2048]{1,0:T(8,128)(2,1)}, bf16[64,2048]{1,0:T(8,128)(2,1)S(1)}, u32[]{:S(2)}, u32[]{:S(2)}) collective-permute-start(bf16[64,2048]{1,0:T(8,128)(2,1)} %get-tuple-element.85), channel_id=1, source_target_pairs={{0,6},{2,4},{4,2},{6,0},{8,14},{10,12},{12,10},{14,8},{16,22},{18,... | collective-permute-start | bytes 786440 | tf_op jit(solution)/shard_map/ppermute | solution.py:229
  25.1 16.4 %collective-permute-start.5 = (bf16[272,1024]{1,0:T(8,128)(2,1)S(1)}, bf16[272,1024]{1,0:T(8,128)(2,1)S(1)}, u32[]{:S(2)}, u32[]{:S(2)}) collective-permute-start(bf16[272,1024]{1,0:T(8,128)(2,1)S(1)} %collective-permute-done.refs_0_), channel_id=1, source_target_pairs={{8,16},{10,18},{12,20},{14,22},{16,8},{18,10},{20,12},{22,14},{9,1... | collective-permute-start | bytes 1671176 | tf_op jit(solution)/shard_map/ppermute | solution.py:286
  25.8 15.7 %collective-permute-start.6 = (bf16[272,1024]{1,0:T(8,128)(2,1)S(1)}, bf16[272,1024]{1,0:T(8,128)(2,1)S(1)}, u32[]{:S(2)}, u32[]{:S(2)}) collective-permute-start(bf16[272,1024]{1,0:T(8,128)(2,1)S(1)} %collective-permute-done.1.refs_1_), channel_id=1, source_target_pairs={{8,0},{10,2},{12,4},{14,6},{16,24},{18,26},{20,28},{22,30},{9,1},{... | collective-permute-start | bytes 1671176 | tf_op jit(solution)/shard_map/ppermute | solution.py:287
  28.3 9.2 %collective-permute-start.7 = (bf16[64,2048]{1,0:T(8,128)(2,1)S(1)}, bf16[64,2048]{1,0:T(8,128)(2,1)S(1)}, u32[]{:S(2)}, u32[]{:S(2)}) collective-permute-start(bf16[64,2048]{1,0:T(8,128)(2,1)S(1)} %get-tuple-element.99), channel_id=1, source_target_pairs={{0,2},{2,0},{4,6},{6,4},{8,10},{10,8},{12,14},{14,12},{16,18},{18,... | collective-permute-start | bytes 786440 | tf_op jit(solution)/shard_map/ppermute | solution.py:229
  29.6 11.9 %collective-permute-start.8 = (bf16[64,2048]{1,0:T(8,128)(2,1)S(1)}, bf16[64,2048]{1,0:T(8,128)(2,1)S(1)}, u32[]{:S(2)}, u32[]{:S(2)}) collective-permute-start(bf16[64,2048]{1,0:T(8,128)(2,1)S(1)} %get-tuple-element.100), channel_id=1, source_target_pairs={{0,4},{2,6},{4,0},{6,2},{8,12},{10,14},{12,8},{14,10},{16,20},{18,... | collective-permute-start | bytes 786440 | tf_op jit(solution)/shard_map/ppermute | solution.py:229
  30.4 11.1 %collective-permute-start.9 = (bf16[64,2048]{1,0:T(8,128)(2,1)S(1)}, bf16[64,2048]{1,0:T(8,128)(2,1)S(1)}, u32[]{:S(2)}, u32[]{:S(2)}) collective-permute-start(bf16[64,2048]{1,0:T(8,128)(2,1)S(1)} %get-tuple-element.101), channel_id=1, source_target_pairs={{0,6},{2,4},{4,2},{6,0},{8,14},{10,12},{12,10},{14,8},{16,22},{18,... | collective-permute-start | bytes 786440 | tf_op jit(solution)/shard_map/ppermute | solution.py:229
  41.5 12.5 %collective-permute-start.10 = (bf16[272,1024]{1,0:T(8,128)(2,1)S(1)}, bf16[272,1024]{1,0:T(8,128)(2,1)S(1)}, u32[]{:S(2)}, u32[]{:S(2)}) collective-permute-start(bf16[272,1024]{1,0:T(8,128)(2,1)S(1)} %collective-permute-done.5.refs_1_), channel_id=1, source_target_pairs={{8,0},{10,2},{12,4},{14,6},{16,24},{18,26},{20,28},{22,30},{9,1},{... | collective-permute-start | bytes 1671176 | tf_op jit(solution)/shard_map/ppermute | solution.py:292
  43.9 11.2 %collective-permute-start.11 = (bf16[64,2048]{1,0:T(8,128)(2,1)S(1)}, bf16[64,2048]{1,0:T(8,128)(2,1)S(1)}, u32[]{:S(2)}, u32[]{:S(2)}) collective-permute-start(bf16[64,2048]{1,0:T(8,128)(2,1)S(1)} %get-tuple-element.119), channel_id=1, source_target_pairs={{0,2},{2,0},{4,6},{6,4},{8,10},{10,8},{12,14},{14,12},{16,18},{18,... | collective-permute-start | bytes 786440 | tf_op jit(solution)/shard_map/ppermute | solution.py:229
  44.5 10.7 %collective-permute-start.12 = (bf16[64,2048]{1,0:T(8,128)(2,1)S(1)}, bf16[64,2048]{1,0:T(8,128)(2,1)S(1)}, u32[]{:S(2)}, u32[]{:S(2)}) collective-permute-start(bf16[64,2048]{1,0:T(8,128)(2,1)S(1)} %get-tuple-element.120), channel_id=1, source_target_pairs={{0,4},{2,6},{4,0},{6,2},{8,12},{10,14},{12,8},{14,10},{16,20},{18,... | collective-permute-start | bytes 786440 | tf_op jit(solution)/shard_map/ppermute | solution.py:229
  46.1 9.1 %collective-permute-start.13 = (bf16[64,2048]{1,0:T(8,128)(2,1)S(1)}, bf16[64,2048]{1,0:T(8,128)(2,1)S(1)}, u32[]{:S(2)}, u32[]{:S(2)}) collective-permute-start(bf16[64,2048]{1,0:T(8,128)(2,1)S(1)} %get-tuple-element.121), channel_id=1, source_target_pairs={{0,6},{2,4},{4,2},{6,0},{8,14},{10,12},{12,10},{14,8},{16,22},{18,... | collective-permute-start | bytes 786440 | tf_op jit(solution)/shard_map/ppermute | solution.py:229
  48.5 20.7 %collective-permute-start.17 = (bf16[4,4,16,2048]{3,2,1,0:T(8,128)(2,1)S(1)}, bf16[4,4,16,2048]{3,2,1,0:T(8,128)(2,1)S(1)}, u32[]{:S(2)}, u32[]{:S(2)}) collective-permute-start(bf16[4,4,16,2048]{3,2,1,0:T(8,128)(2,1)S(1)} %bitcast.29), channel_id=1, source_target_pairs={{0,1},{1,0},{2,3},{3,2},{4,5},{5,4},{6,7},{7,6},{8,9},{9,8},{10,11... | collective-permute-start | bytes 3145736 | tf_op jit(solution)/shard_map/ppermute | solution.py:232
  48.6 4.3 %copy-start = (bf16[4,704,2048]{2,1,0:T(8,128)(2,1)S(1)}, bf16[4,704,2048]{2,1,0:T(8,128)(2,1)}, u32[]{:S(2)}) copy-start(bf16[4,704,2048]{2,1,0:T(8,128)(2,1)} %refs_8_.1) | copy-start | bytes 34603012
  52.8 19.8 %slice-start = ((s8[11534336]{0:T(1024)(128)(4,1)}), s8[4194304]{0:T(1024)(128)(4,1)S(1)}, s32[]{:S(2)}) async-start(s8[11534336]{0:T(1024)(128)(4,1)} %bitcast.27), calls=%async_computation | async-start | bytes 8388608
  52.8 19.8 %slice-start.1 = ((s8[11534336]{0:T(1024)(128)(4,1)}), s8[4194304]{0:T(1024)(128)(4,1)S(1)}, s32[]{:S(2)}) async-start(s8[11534336]{0:T(1024)(128)(4,1)} %bitcast.27), calls=%async_computation.1 | async-start | bytes 8388608
  55.2 13.2 %collective-permute-start.14 = (bf16[64,2048]{1,0:T(8,128)(2,1)S(1)}, bf16[64,2048]{1,0:T(8,128)(2,1)S(1)}, u32[]{:S(2)}, u32[]{:S(2)}) collective-permute-start(bf16[64,2048]{1,0:T(8,128)(2,1)S(1)} %get-tuple-element.127), channel_id=1, source_target_pairs={{0,2},{2,0},{4,6},{6,4},{8,10},{10,8},{12,14},{14,12},{16,18},{18,... | collective-permute-start | bytes 786440 | tf_op jit(solution)/shard_map/ppermute | solution.py:229
  56.8 11.9 %collective-permute-start.15 = (bf16[64,2048]{1,0:T(8,128)(2,1)S(1)}, bf16[64,2048]{1,0:T(8,128)(2,1)S(1)}, u32[]{:S(2)}, u32[]{:S(2)}) collective-permute-start(bf16[64,2048]{1,0:T(8,128)(2,1)S(1)} %get-tuple-element.128), channel_id=1, source_target_pairs={{0,4},{2,6},{4,0},{6,2},{8,12},{10,14},{12,8},{14,10},{16,20},{18,... | collective-permute-start | bytes 786440 | tf_op jit(solution)/shard_map/ppermute | solution.py:229
  58.3 10.2 %collective-permute-start.16 = (bf16[64,2048]{1,0:T(8,128)(2,1)S(1)}, bf16[64,2048]{1,0:T(8,128)(2,1)S(1)}, u32[]{:S(2)}, u32[]{:S(2)}) collective-permute-start(bf16[64,2048]{1,0:T(8,128)(2,1)S(1)} %get-tuple-element.129), channel_id=1, source_target_pairs={{0,6},{2,4},{4,2},{6,0},{8,14},{10,12},{12,10},{14,8},{16,22},{18,... | collective-permute-start | bytes 786440 | tf_op jit(solution)/shard_map/ppermute | solution.py:229
  58.8 10.3 %collective-permute-start.18 = (bf16[4,4,16,2048]{3,2,1,0:T(8,128)(2,1)S(1)}, bf16[4,4,16,2048]{3,2,1,0:T(8,128)(2,1)S(1)}, u32[]{:S(2)}, u32[]{:S(2)}) collective-permute-start(bf16[4,4,16,2048]{3,2,1,0:T(8,128)(2,1)S(1)} %bitcast.32), channel_id=1, source_target_pairs={{0,1},{1,0},{2,3},{3,2},{4,5},{5,4},{6,7},{7,6},{8,9},{9,8},{10,11... | collective-permute-start | bytes 3145736 | tf_op jit(solution)/shard_map/ppermute | solution.py:232
  58.9 4.3 %copy-start.1 = (bf16[4,704,2048]{2,1,0:T(8,128)(2,1)S(1)}, bf16[4,704,2048]{2,1,0:T(8,128)(2,1)}, u32[]{:S(2)}) copy-start(bf16[4,704,2048]{2,1,0:T(8,128)(2,1)} %refs_9_.1) | copy-start | bytes 34603012
  63.2 9.4 %slice-start.2 = ((s8[11534336]{0:T(1024)(128)(4,1)}), s8[3145728]{0:T(1024)(128)(4,1)S(1)}, s32[]{:S(2)}) async-start(s8[11534336]{0:T(1024)(128)(4,1)} %bitcast.27), calls=%async_computation.2 | async-start | bytes 6291456
  63.2 9.4 %copy-start.2 = (bf16[4,704,2048]{2,1,0:T(8,128)(2,1)S(1)}, bf16[4,704,2048]{2,1,0:T(8,128)(2,1)}, u32[]{:S(2)}) copy-start(bf16[4,704,2048]{2,1,0:T(8,128)(2,1)} %refs_9_.1) | copy-start | bytes 34603012
  68.5 2.7 %collective-permute-start.19 = (bf16[4,4,16,2048]{3,2,1,0:T(8,128)(2,1)S(1)}, bf16[4,4,16,2048]{3,2,1,0:T(8,128)(2,1)S(1)}, u32[]{:S(2)}, u32[]{:S(2)}) collective-permute-start(bf16[4,4,16,2048]{3,2,1,0:T(8,128)(2,1)S(1)} %bitcast.35), channel_id=1, source_target_pairs={{0,1},{1,0},{2,3},{3,2},{4,5},{5,4},{6,7},{7,6},{8,9},{9,8},{10,11... | collective-permute-start | bytes 3145736 | tf_op jit(solution)/shard_map/ppermute | solution.py:232
  68.8 3.8 %collective-permute-start.20 = (bf16[4,4,16,2048]{3,2,1,0:T(8,128)(2,1)S(1)}, bf16[4,4,16,2048]{3,2,1,0:T(8,128)(2,1)S(1)}, u32[]{:S(2)}, u32[]{:S(2)}) collective-permute-start(bf16[4,4,16,2048]{3,2,1,0:T(8,128)(2,1)S(1)} %bitcast.38), channel_id=1, source_target_pairs={{0,1},{1,0},{2,3},{3,2},{4,5},{5,4},{6,7},{7,6},{8,9},{9,8},{10,11... | collective-permute-start | bytes 3145736 | tf_op jit(solution)/shard_map/ppermute | solution.py:232
  83.5 2.0 %collective-permute-start.21 = (bf16[4,4,16,1024]{3,2,1,0:T(8,128)(2,1)S(1)}, bf16[4,4,16,1024]{3,2,1,0:T(8,128)(2,1)S(1)}, u32[]{:S(2)}, u32[]{:S(2)}) collective-permute-start(bf16[4,4,16,1024]{3,2,1,0:T(8,128)(2,1)S(1)} %get-tuple-element.133), channel_id=1, source_target_pairs={{0,1},{1,0},{2,3},{3,2},{4,5},{5,4},{6,7},{7,6},{8,9},{9,8},{10,11... | collective-permute-start | bytes 1572872 | tf_op jit(solution)/shard_map/ppermute | solution.py:232
  83.7 2.5 %collective-permute-start.22 = (bf16[4,4,16,1024]{3,2,1,0:T(8,128)(2,1)S(1)}, bf16[4,4,16,1024]{3,2,1,0:T(8,128)(2,1)S(1)}, u32[]{:S(2)}, u32[]{:S(2)}) collective-permute-start(bf16[4,4,16,1024]{3,2,1,0:T(8,128)(2,1)S(1)} %get-tuple-element.137), channel_id=1, source_target_pairs={{0,1},{1,0},{2,3},{3,2},{4,5},{5,4},{6,7},{7,6},{8,9},{9,8},{10,11... | collective-permute-start | bytes 1572872 | tf_op jit(solution)/shard_map/ppermute | solution.py:232
  84.1 2.9 %collective-permute-start.23 = (bf16[4,4,16,1024]{3,2,1,0:T(8,128)(2,1)S(1)}, bf16[4,4,16,1024]{3,2,1,0:T(8,128)(2,1)S(1)}, u32[]{:S(2)}, u32[]{:S(2)}) collective-permute-start(bf16[4,4,16,1024]{3,2,1,0:T(8,128)(2,1)S(1)} %get-tuple-element.139), channel_id=1, source_target_pairs={{0,1},{1,0},{2,3},{3,2},{4,5},{5,4},{6,7},{7,6},{8,9},{9,8},{10,11... | collective-permute-start | bytes 1572872 | tf_op jit(solution)/shard_map/ppermute | solution.py:232
  84.2 3.5 %collective-permute-start.24 = (bf16[4,4,16,1024]{3,2,1,0:T(8,128)(2,1)S(1)}, bf16[4,4,16,1024]{3,2,1,0:T(8,128)(2,1)S(1)}, u32[]{:S(2)}, u32[]{:S(2)}) collective-permute-start(bf16[4,4,16,1024]{3,2,1,0:T(8,128)(2,1)S(1)} %get-tuple-element.142), channel_id=1, source_target_pairs={{0,1},{1,0},{2,3},{3,2},{4,5},{5,4},{6,7},{7,6},{8,9},{9,8},{10,11... | collective-permute-start | bytes 1572872 | tf_op jit(solution)/shard_map/ppermute | solution.py:232
  88.0 8.0 %collective-permute-start.26 = (bf16[64,1024]{1,0:T(8,128)(2,1)S(1)}, bf16[64,1024]{1,0:T(8,128)(2,1)S(1)}, u32[]{:S(2)}, u32[]{:S(2)}) collective-permute-start(bf16[64,1024]{1,0:T(8,128)(2,1)S(1)} %bitcast.56), channel_id=1, source_target_pairs={{0,4},{2,6},{4,0},{6,2},{8,12},{10,14},{12,8},{14,10},{16,20},{18,... | collective-permute-start | bytes 393224 | tf_op jit(solution)/shard_map/ppermute | solution.py:229
  89.5 7.3 %collective-permute-start.27 = (bf16[64,1024]{1,0:T(8,128)(2,1)S(1)}, bf16[64,1024]{1,0:T(8,128)(2,1)S(1)}, u32[]{:S(2)}, u32[]{:S(2)}) collective-permute-start(bf16[64,1024]{1,0:T(8,128)(2,1)S(1)} %bitcast.55), channel_id=1, source_target_pairs={{0,6},{2,4},{4,2},{6,0},{8,14},{10,12},{12,10},{14,8},{16,22},{18,... | collective-permute-start | bytes 393224 | tf_op jit(solution)/shard_map/ppermute | solution.py:229
  91.1 6.5 %collective-permute-start.25 = (bf16[64,1024]{1,0:T(8,128)(2,1)S(1)}, bf16[64,1024]{1,0:T(8,128)(2,1)S(1)}, u32[]{:S(2)}, u32[]{:S(2)}) collective-permute-start(bf16[64,1024]{1,0:T(8,128)(2,1)S(1)} %bitcast.54), channel_id=1, source_target_pairs={{0,2},{2,0},{4,6},{6,4},{8,10},{10,8},{12,14},{14,12},{16,18},{18,... | collective-permute-start | bytes 393224 | tf_op jit(solution)/shard_map/ppermute | solution.py:229
  97.9 13.1 %collective-permute-start.28 = (bf16[128,1024]{1,0:T(8,128)(2,1)S(1)}, bf16[128,1024]{1,0:T(8,128)(2,1)S(1)}, u32[]{:S(2)}, u32[]{:S(2)}) collective-permute-start(bf16[128,1024]{1,0:T(8,128)(2,1)S(1)} %get-tuple-element.143), channel_id=1, source_target_pairs={{0,2},{2,0},{4,6},{6,4},{8,10},{10,8},{12,14},{14,12},{16,18},{18,... | collective-permute-start | bytes 786440 | tf_op jit(solution)/shard_map/ppermute | solution.py:229
  99.5 12.6 %collective-permute-start.29 = (bf16[128,1024]{1,0:T(8,128)(2,1)S(1)}, bf16[128,1024]{1,0:T(8,128)(2,1)S(1)}, u32[]{:S(2)}, u32[]{:S(2)}) collective-permute-start(bf16[128,1024]{1,0:T(8,128)(2,1)S(1)} %get-tuple-element.144), channel_id=1, source_target_pairs={{0,4},{2,6},{4,0},{6,2},{8,12},{10,14},{12,8},{14,10},{16,20},{18,... | collective-permute-start | bytes 786440 | tf_op jit(solution)/shard_map/ppermute | solution.py:229
  100.0 12.1 %collective-permute-start.30 = (bf16[128,1024]{1,0:T(8,128)(2,1)S(1)}, bf16[128,1024]{1,0:T(8,128)(2,1)S(1)}, u32[]{:S(2)}, u32[]{:S(2)}) collective-permute-start(bf16[128,1024]{1,0:T(8,128)(2,1)S(1)} %pad_maximum_fusion.7), channel_id=1, source_target_pairs={{0,6},{2,4},{4,2},{6,0},{8,14},{10,12},{12,10},{14,8},{16,22},{18,... | collective-permute-start | bytes 786440 | tf_op jit(solution)/shard_map/ppermute | solution.py:229
  101.4 23.3 %copy-start.3 = (bf16[256,128]{1,0:T(8,128)(2,1)S(1)}, bf16[256,128]{1,0:T(8,128)(2,1)}, u32[]{:S(2)}) copy-start(bf16[256,128]{1,0:T(8,128)(2,1)} %get-tuple-element.81.refs_0_) | copy-start | bytes 196612
  112.4 6.4 %collective-permute-start.31 = (bf16[64,1024]{1,0:T(8,128)(2,1)S(1)}, bf16[64,1024]{1,0:T(8,128)(2,1)S(1)}, u32[]{:S(2)}, u32[]{:S(2)}) collective-permute-start(bf16[64,1024]{1,0:T(8,128)(2,1)S(1)} %bitcast.53), channel_id=1, source_target_pairs={{0,2},{2,0},{4,6},{6,4},{8,10},{10,8},{12,14},{14,12},{16,18},{18,... | collective-permute-start | bytes 393224 | tf_op jit(solution)/shard_map/ppermute | solution.py:229
  113.0 12.0 %collective-permute-start.34 = (bf16[128,1024]{1,0:T(8,128)(2,1)S(1)}, bf16[128,1024]{1,0:T(8,128)(2,1)S(1)}, u32[]{:S(2)}, u32[]{:S(2)}) collective-permute-start(bf16[128,1024]{1,0:T(8,128)(2,1)S(1)} %combine.3.refs_10_), channel_id=1, source_target_pairs={{0,24},{2,26},{4,28},{6,30},{8,16},{10,18},{12,20},{14,22},{16,8},... | collective-permute-start | bytes 786440 | tf_op jit(solution)/shard_map/ppermute | solution.py:226
  114.5 23.3 %collective-permute-start.35 = (bf16[128,1024]{1,0:T(8,128)(2,1)S(1)}, bf16[128,1024]{1,0:T(8,128)(2,1)S(1)}, u32[]{:S(2)}, u32[]{:S(2)}) collective-permute-start(bf16[128,1024]{1,0:T(8,128)(2,1)S(1)} %get-tuple-element.155), channel_id=1, source_target_pairs={{0,16},{2,18},{4,20},{6,22},{8,24},{10,26},{12,28},{14,30},{16,0},... | collective-permute-start | bytes 786440 | tf_op jit(solution)/shard_map/ppermute | solution.py:226
  117.2 20.5 %collective-permute-start.36 = (bf16[128,1024]{1,0:T(8,128)(2,1)S(1)}, bf16[128,1024]{1,0:T(8,128)(2,1)S(1)}, u32[]{:S(2)}, u32[]{:S(2)}) collective-permute-start(bf16[128,1024]{1,0:T(8,128)(2,1)S(1)} %get-tuple-element.156), channel_id=1, source_target_pairs={{0,8},{2,10},{4,12},{6,14},{8,0},{10,2},{12,4},{14,6},{16,24},{18,... | collective-permute-start | bytes 786440 | tf_op jit(solution)/shard_map/ppermute | solution.py:226
  117.3 5.0 %collective-permute-start.32 = (bf16[64,1024]{1,0:T(8,128)(2,1)S(1)}, bf16[64,1024]{1,0:T(8,128)(2,1)S(1)}, u32[]{:S(2)}, u32[]{:S(2)}) collective-permute-start(bf16[64,1024]{1,0:T(8,128)(2,1)S(1)} %bitcast.52), channel_id=1, source_target_pairs={{0,4},{2,6},{4,0},{6,2},{8,12},{10,14},{12,8},{14,10},{16,20},{18,... | collective-permute-start | bytes 393224 | tf_op jit(solution)/shard_map/ppermute | solution.py:229
  118.8 5.9 %collective-permute-start.33 = (bf16[64,1024]{1,0:T(8,128)(2,1)S(1)}, bf16[64,1024]{1,0:T(8,128)(2,1)S(1)}, u32[]{:S(2)}, u32[]{:S(2)}) collective-permute-start(bf16[64,1024]{1,0:T(8,128)(2,1)S(1)} %bitcast.51), channel_id=1, source_target_pairs={{0,6},{2,4},{4,2},{6,0},{8,14},{10,12},{12,10},{14,8},{16,22},{18,... | collective-permute-start | bytes 393224 | tf_op jit(solution)/shard_map/ppermute | solution.py:229
